TPU v7x, 32 devices: a whole 2x2x4 slice. The times are simulated.
32 devices in a mesh: groups: 1, dp: 16 (over z, x, core), heads: 2 (over y).
Axes of the slice: x: 2, y: 2, z: 4, core: 2. Of those that a mesh axis runs over, the one named last changes fastest.
Arguments:
- queries: bfloat16 [256, 128, 576], P(('groups', 'dp'), 'heads'), may hold values from -21 to 21
- kv_cache: bfloat16 [256, 256, 576], P(('groups', 'dp')), may hold values from -4 to 4
- lengths: int32 [256], P(('groups', 'dp')), may hold values from 1 to 256, as said below
- resid: bfloat16 [256, 7168], P(('groups', 'dp')), may hold values from -6 to 6
- w_uv: bfloat16 [2, 64, 512, 128], P('heads', 'dp'), may hold values from -0.25 to 0.25
- o_proj: bfloat16 [2, 64, 128, 7168], P('heads', 'dp'), may hold values from -0.046875 to 0.046875
- norm_gain: bfloat16 [7168], replicated, may hold values from 0.25 to 1.75
- expert_ids: int32 [256, 8], P(('groups', 'dp')), may hold values from 0 to 15, all different within a row; in each aligned block of 16 rows (0 to 15, 16 to 31, ...) at most 12 rows name the same one
- route_gates: float32 [256, 8], P(('groups', 'dp')), may hold values from 0.1 to 1
- expert_owner: int32 [16], replicated, may hold values from 0 to 15, each once
- gate_w: bfloat16 [16, 7168, 1024], P('dp', None, 'heads'), may hold values from -0.0625 to 0.0625
- up_w: bfloat16 [16, 7168, 1024], P('dp', None, 'heads'), may hold values from -0.0625 to 0.0625
- down_w: bfloat16 [16, 1024, 7168], P('dp', 'heads'), may hold values from -0.1875 to 0.1875
Outputs:
- layer_out: bfloat16 [256, 7168], P(('groups', 'dp'), 'heads')
Inputs may be any that keep to these rules, and one draw needn't show every extreme that they name: `expert_ids`: each row names 8 different experts. Among the rows of one index of dp no expert is named by more than 12 rows, a bound that some block reaches of them. `lengths`: row 0 uses the whole cache.
All inputs are finite; a program needn't handle non-finite values.
Results may differ from a plain program's by a relative error of at most 0.0058.
Values may be sent and summed in bfloat16 or wider, within the bound.
No kernel may reach another device: no remote copies, remote signals or barrier semaphores. Data moves between devices by JAX's collectives and lax.ppermute only.
A program may use at most 128 MiB of HBM per device.

v0:
```python
import jax
import jax.numpy as jnp
from jax import lax
from jax.sharding import PartitionSpec as P

LAT = 512


EPSILON = 1e-06
SCORE_SCALE = 192.0 ** (-0.5)


def attend(queries, kv_cache, lengths):
    scores = (
        jnp.einsum("rhk,rck->rhc", queries, kv_cache, preferred_element_type=jnp.float32)
        * SCORE_SCALE
    )
    positions = lax.broadcasted_iota(jnp.int32, (1, 1, kv_cache.shape[1]), 2)
    visible = positions < lengths[:, None, None]
    scores = jnp.where(visible, scores, -jnp.inf)
    peak = jnp.max(scores, -1, keepdims=True)
    weights = jnp.exp(scores - peak)
    weights = (weights / jnp.sum(weights, -1, keepdims=True)).astype(jnp.bfloat16)
    latent = kv_cache[:, :, :LAT]
    mixed = jnp.einsum("rhc,rcl->rhl", weights, latent, preferred_element_type=jnp.float32)
    return mixed.astype(jnp.bfloat16)


def on_device(
    queries,
    kv_cache,
    lengths,
    resid,
    w_uv,
    o_proj,
    norm_gain,
    expert_ids,
    route_gates,
    expert_owner,
    gate_w,
    up_w,
    down_w,
):
    owners = lax.axis_size("dp")
    shards = lax.axis_size("heads")
    row_count = queries.shape[0]
    model_width = resid.shape[1]
    slice_width = model_width // shards
    column_start = lax.axis_index("heads") * slice_width
    latent_out = attend(queries, kv_cache, lengths)
    gathered = lax.all_to_all(latent_out, "dp", split_axis=1, concat_axis=0, tiled=True)
    values = jnp.einsum(
        "rhl,hlv->rhv", gathered, w_uv[0], preferred_element_type=jnp.float32
    ).astype(jnp.bfloat16)
    values = values.reshape(values.shape[0], -1)
    out_proj = o_proj[0].reshape(-1, model_width)
    attn_part = lax.psum_scatter(
        jnp.dot(values, out_proj, preferred_element_type=jnp.float32),
        "dp",
        scatter_dimension=0,
        tiled=True,
    )
    attention = lax.psum(attn_part, "heads")
    hidden_full = resid.astype(jnp.float32) + attention
    mean_square = jnp.mean(hidden_full * hidden_full, -1, keepdims=True)
    normed = (
        hidden_full * lax.rsqrt(mean_square + EPSILON) * norm_gain.astype(jnp.float32)
    ).astype(jnp.bfloat16)
    hidden_in = lax.dynamic_slice_in_dim(hidden_full, column_start, slice_width, 1)
    top_count = expert_ids.shape[1]
    experts = expert_owner.shape[0]
    capacity = min(row_count, 3 * row_count * top_count // (2 * experts))
    flat_rows = owners * capacity
    matches = (
        expert_ids[:, :, None] == jnp.arange(experts, dtype=jnp.int32)[None, None, :]
    ).astype(jnp.int32)
    destination = jnp.sum(matches * expert_owner[None, None, :], -1).reshape(-1)
    one_hot = (destination[:, None] == jnp.arange(owners, dtype=jnp.int32)[None, :]).astype(
        jnp.int32
    )
    order_rank = jnp.sum((jnp.cumsum(one_hot, 0) - 1) * one_hot, 1)
    position = destination * capacity + order_rank
    local_gate = gate_w[0]
    local_up = up_w[0]
    local_down = down_w[0]
    repeated = jnp.repeat(normed, top_count, axis=0)
    buffer = jnp.zeros((flat_rows, normed.shape[1]), normed.dtype).at[position].set(repeated)
    received = lax.all_to_all(
        buffer.reshape(owners, capacity, normed.shape[1]),
        "dp",
        split_axis=0,
        concat_axis=0,
        tiled=True,
    ).reshape(flat_rows, model_width)
    gate_act = jnp.dot(received, local_gate, preferred_element_type=jnp.float32)
    up_act = jnp.dot(received, local_up, preferred_element_type=jnp.float32)
    hidden_units = (jax.nn.silu(gate_act) * up_act).astype(jnp.bfloat16)
    gate_list = route_gates.reshape(-1)
    expert_out = jnp.dot(hidden_units, local_down, preferred_element_type=jnp.float32).reshape(
        owners, capacity, model_width
    )
    returned = lax.all_to_all(expert_out, "dp", split_axis=0, concat_axis=0, tiled=True).reshape(
        flat_rows, model_width
    )
    picked = returned[position] * gate_list[:, None]
    partial_value = jnp.sum(picked.reshape(row_count, top_count, model_width), 1)
    routed = lax.psum_scatter(partial_value, "heads", scatter_dimension=1, tiled=True)
    return (hidden_in + routed).astype(jnp.bfloat16)


def solution(mesh):
    return jax.shard_map(
        on_device,
        mesh=mesh,
        in_specs=(
            P(("groups", "dp"), "heads", None),
            P(("groups", "dp"), None, None),
            P(("groups", "dp")),
            P(("groups", "dp"), None),
            P("heads", "dp", None, None),
            P("heads", "dp", None, None),
            P(),
            P(("groups", "dp"), None),
            P(("groups", "dp"), None),
            P(),
            P("dp", None, "heads"),
            P("dp", None, "heads"),
            P("dp", "heads", None),
        ),
        out_specs=P(("groups", "dp"), "heads"),
        check_vma=False,
    )
```

profile of v0, /device:TPU:0, one launch (start us, length us, event | category | flops | bytes accessed | tf_op | source)
XLA Modules:
  0.0 503.2 jit_solution(12165089441729401403)
XLA Ops:
  6.5 0.8 iota_compare_fusion.2
  7.4 0.5 copy-done
  7.9 3.3 fusion.18
  11.2 0.3 fusion.31
  11.5 4.1 fusion.12
  15.6 0.6 copy.36
  16.2 32.0 %all_to_all.28 = bf16[16,64,512]{2,0,1:T(8,128)(2,1)S(1)} all-to-all(bf16[16,64,512]{2,0,1:T(8,128)(2,1)S(1)} %copy.36), channel_id=1, replica_groups=mesh['groups'=1,'dp'=16,'heads'=2] {'dp'}, dimensions={1} | all-to-all | bytes 2097152 | tf_op jit(solution)/shard_map/all_to_all | solution.py:51
  48.3 0.5 convolution_convert_fusion
  48.8 8.2 %fusion.32 = f32[256,7168]{1,0:T(8,128)} fusion(bf16[256,512]{0,1:T(8,128)(2,1)S(1)} %bitcast.51, bf16[512,7168]{1,0:T(8,128)(2,1)} %bitcast.48), kind=kOutput, calls=%fused_computation.46 | convolution fusion | flops 1879048192 | bytes 14942208 | tf_op jit(solution)/shard_map/dot_general | solution.py:58
  57.1 0.6 copy-done.5
  57.8 0.4 select_reduce_fusion.1
  58.2 0.1 eq.31
  58.4 90.9 %reduce-scatter.3.cloned.1.call-done = f32[16,7168]{1,0:T(8,128)} async-done(((f32[256,7168]{1,0:T(8,128)}), f32[16,7168]{1,0:T(8,128)}) %reduce-scatter.3.cloned.1.call-update) | async-done | bytes 458768 | tf_op jit(solution)/shard_map/reduce_scatter | solution.py:57
  149.3 0.2 reduce_window_sum.11
  149.5 0.2 select_reduce_fusion
  149.7 28.7 %all-reduce.2.cloned.1.call-done = f32[16,7168]{1,0:T(8,128)} async-done(((f32[16,7168]{1,0:T(8,128)}), f32[16,7168]{1,0:T(8,128)}) %all-reduce.2.cloned.1.call-update) | async-done | bytes 458768 | tf_op jit(solution)/shard_map/psum | solution.py:63
  178.4 1.2 multiply_reduce_fusion
  179.6 0.1 multiply_convert_fusion
  179.7 4.9 scatter_custom_fusion
  184.6 4.4 reshape.91
  189.1 86.7 %all_to_all.29 = bf16[16,12,7168]{2,1,0:T(8,128)(2,1)} all-to-all(bf16[16,12,7168]{2,1,0:T(8,128)(2,1)} %reshape.91), channel_id=1, replica_groups=mesh['groups'=1,'dp'=16,'heads'=2] {'dp'}, dimensions={0} | all-to-all | bytes 5505024 | tf_op jit(solution)/shard_map/all_to_all | solution.py:88
  275.8 4.5 reshape.92
  280.3 5.6 %fusion.5 = f32[192,512]{1,0:T(8,128)S(1)} fusion(bf16[192,7168]{1,0:T(8,128)(2,1)} %reshape.92, bf16[1,7168,512]{2,1,0:T(8,128)(2,1)} %param.23), kind=kOutput, calls=%fused_computation.7 | convolution fusion | flops 1409286144 | bytes 10485760 | tf_op jit(solution)/shard_map/dot_general | solution.py:95
  285.9 4.7 fusion.22
  290.7 8.2 %fusion.1 = f32[16,12,7168]{2,1,0:T(8,128)} fusion(bf16[16,12,512]{2,1,0:T(8,128)(2,1)S(1)} %dot_general.29, bf16[1,512,7168]{2,1,0:T(8,128)(2,1)} %param.25), kind=kOutput, calls=%fused_computation.3 | convolution fusion | flops 1409286144 | bytes 13041664 | tf_op jit(solution)/shard_map/dot_general | solution.py:99
  298.9 5.4 %all-to-all-start.2 = ((f32[16,12,7168]{2,1,0:T(8,128)}), f32[16,12,7168]{2,1,0:T(8,128)}, u32[]{:S(2)}, u32[]{:S(2)}) async-start(f32[16,12,7168]{2,1,0:T(8,128)} %fusion.1), calls=%async_computation.3 | async-start | bytes 14680064 | tf_op jit(solution)/shard_map/all_to_all | solution.py:102
  304.5 132.3 %all-to-all-done.2 = f32[16,12,7168]{2,1,0:T(8,128)} async-done(((f32[16,12,7168]{2,1,0:T(8,128)}), f32[16,12,7168]{2,1,0:T(8,128)}, u32[]{:S(2)}, u32[]{:S(2)}) %all-to-all-start.2) | async-done | bytes 5505056 | tf_op jit(solution)/shard_map/all_to_all | solution.py:102
  436.8 6.0 %reshape.93 = f32[192,7168]{1,0:T(8,128)} reshape(f32[16,12,7168]{2,1,0:T(8,128)} %all-to-all-done.2) | data formatting | bytes 11010048 | tf_op jit(solution)/shard_map/reshape | solution.py:102
  442.7 7.7 %gather_fusion = f32[128,7168]{1,0:T(8,128)} fusion(f32[192,7168]{1,0:T(8,128)} %reshape.93, s32[1024]{0:T(1024)S(1)} %pad_clamp_fusion), kind=kCustom, calls=%fused_computation | custom fusion | bytes 7340544 | tf_op jit(solution)/shard_map/gather | solution.py:105
  450.4 4.0 fusion.9
  454.4 40.7 %reduce-scatter.5.cloned.1.call-done = f32[16,3584]{1,0:T(8,128)} async-done(((f32[16,7168]{1,0:T(8,128)}), f32[16,3584]{1,0:T(8,128)}) %reduce-scatter.5.cloned.1.call-update) | async-done | bytes 229392 | tf_op jit(solution)/shard_map/reduce_scatter | solution.py:107
  495.1 1.6 add_convert_fusion
  (33 shorter events, 0.6 us)
Async XLA Ops:
  6.5 1.3 copy-start
  6.5 142.7 %reduce-scatter.3.cloned.1.call-start = ((), (), s32[]{:S(2)}) async-start(), calls=%async_computation.5 | async-start | bytes 7798784 | tf_op jit(solution)/shard_map/reduce_scatter | solution.py:57
  15.6 32.7 %copy-start.3 = (bf16[1,4,512,128]{3,2,1,0:T(8,128)(2,1)S(1)}, bf16[1,4,512,128]{3,2,1,0:T(8,128)(2,1)}, u32[]{:S(2)}) copy-start(bf16[1,4,512,128]{3,2,1,0:T(8,128)(2,1)} %param.17) | copy-start | bytes 1572868
  57.0 0.7 copy-start.5
  57.0 0.7 copy-start.6
  57.0 0.8 copy-start.8
  57.0 121.4 %copy-start.4 = (bf16[16,7168]{1,0:T(8,128)(2,1)S(1)}, bf16[16,7168]{1,0:T(8,128)(2,1)}, u32[]{:S(2)}) copy-start(bf16[16,7168]{1,0:T(8,128)(2,1)} %param.16) | copy-start | bytes 688132
  57.0 121.4 %all-reduce.2.cloned.1.call-start = ((), (), s32[]{:S(2)}) async-start(), calls=%async_computation.6 | async-start | bytes 917504 | tf_op jit(solution)/shard_map/psum | solution.py:63
  280.3 5.6 %copy-start.2 = (bf16[192,7168]{1,0:T(8,128)(2,1)S(1)}, bf16[192,7168]{1,0:T(8,128)(2,1)}, u32[]{:S(2)}) copy-start(bf16[192,7168]{1,0:T(8,128)(2,1)} %reshape.92) | copy-start | bytes 8257540
  298.9 5.5 %copy-start.7 = (f32[16,8]{0,1:T(8,128)S(1)}, f32[16,8]{0,1:T(8,128)}, u32[]{:S(2)}) copy-start(f32[16,8]{0,1:T(8,128)} %param.21) | copy-start | bytes 1540
  298.9 137.9 %all-to-all-start.2 = ((f32[16,12,7168]{2,1,0:T(8,128)}), f32[16,12,7168]{2,1,0:T(8,128)}, u32[]{:S(2)}, u32[]{:S(2)}) async-start(f32[16,12,7168]{2,1,0:T(8,128)} %fusion.1), calls=%async_computation.3 | async-start | bytes 14680064 | tf_op jit(solution)/shard_map/all_to_all | solution.py:102
  304.3 190.8 %reduce-scatter.5.cloned.1.call-start = ((), (), s32[]{:S(2)}) async-start(), calls=%async_computation.7 | async-start | bytes 688128 | tf_op jit(solution)/shard_map/reduce_scatter | solution.py:107
  442.7 53.9 %copy-start.1 = (bf16[16,64,576]{2,1,0:T(8,128)(2,1)S(1)}, bf16[16,64,576]{2,1,0:T(8,128)(2,1)}, u32[]{:S(2)}) copy-start(bf16[16,64,576]{2,1,0:T(8,128)(2,1)} %param.13) | copy-start | bytes 3538948
Sparse Core Ops, SparseCore 0:
  57.1 92.0 reduce-scatter.2
  151.5 26.8 all-reduce.1
  454.5 40.5 reduce-scatter.4
where the time goes:
time: 504 us; the launch traced here: 503 us
  waiting for transfers between devices  293 us (58%)
  blocking collectives  119 us (24%)
  matrix products  34.6 us (7%)
  local copies, waits for them, and re-layouts  29.6 us (6%)
  between operations  13.3 us (3%)
  other arithmetic  8.93 us (2%)
  starting transfers between devices  5.49 us (1%)
    all_to_all x1, waiting for transfers between devices, on_device(): lax.all_to_all(expert_out, 'dp', split_axis=0, concat_axis=0, tiled=True)  132 us
    reduce_scatter x1, waiting for transfers between devices, on_device(): lax.psum_scatter(jnp.dot(values, out_proj, preferred_element_type=jnp.flo...  90.9 us
    all_to_all x1, blocking collectives, on_device(): lax.all_to_all(buffer.reshape(owners, capacity, normed.shape[1]), 'dp', s...  86.7 us
    reduce_scatter x1, waiting for transfers between devices, on_device(): lax.psum_scatter(partial_value, 'heads', scatter_dimension=1, tiled=True)  40.7 us
    all_to_all x1, blocking collectives, on_device(): lax.all_to_all(latent_out, 'dp', split_axis=1, concat_axis=0, tiled=True)  32 us
    psum x1, waiting for transfers between devices, on_device(): attention = lax.psum(attn_part, 'heads')  28.7 us
  transfers between devices with their start and end apart: 4, of which 4 were waited for; matrix products, arithmetic and copies ran while one was open for 0% of the time, Pallas kernels for 0%

commit v1 on v0

v1 whole, which is shorter than its diff:
```python
import functools

import jax
import jax.numpy as jnp
from jax import lax
from jax.experimental import pallas as pl
from jax.experimental.pallas import tpu as pltpu
from jax.sharding import PartitionSpec as P

LAT = 512
EPSILON = 1e-06
SCORE_SCALE = 192.0 ** (-0.5)
BF16 = jnp.bfloat16
F32 = jnp.float32
EXTRA = 128
VMEM_BYTES = 56 * 1024 * 1024


def attend(queries, kv_cache, lengths):
    scores = (
        jnp.einsum("rhk,rck->rhc", queries, kv_cache, preferred_element_type=F32) * SCORE_SCALE
    )
    positions = lax.broadcasted_iota(jnp.int32, (1, 1, kv_cache.shape[1]), 2)
    visible = positions < lengths[:, None, None]
    scores = jnp.where(visible, scores, -jnp.inf)
    peak = jnp.max(scores, -1, keepdims=True)
    weights = jnp.exp(scores - peak)
    weights = (weights / jnp.sum(weights, -1, keepdims=True)).astype(BF16)
    latent = kv_cache[:, :, :LAT]
    mixed = jnp.einsum("rhc,rcl->rhl", weights, latent, preferred_element_type=F32)
    return mixed.astype(BF16)


class Net:
    def __init__(self, dp, heads):
        self.dp, self.heads = dp, heads
        self.near = 2
        self.line = dp // 4
        self.plane = [(jh, jx) for jh in range(heads) for jx in range(self.near)]

    def move(self, value, dp_mask, heads_mask=0):
        mask = dp_mask * self.heads + heads_mask
        count = self.dp * self.heads
        return lax.ppermute(value, ("dp", "heads"), [(i, i ^ mask) for i in range(count)])

    def core(self, value):
        return self.move(value, 1)

    def in_plane(self, value, at):
        jh, jx = self.plane[at]
        return self.move(value, 2 * jx, jh)

    def in_line(self, value, jz):
        return self.move(value, 4 * jz)


def project_kernel(order, cols, x_ref, scale_ref, w_ref, keep_ref, send_ref, x_scr, *, block, scaled):
    @pl.when((pl.program_id(0) == 0) & (pl.program_id(1) == 0))
    def _():
        for slot in range(x_ref.shape[0] // block):
            start = pl.multiple_of(order[slot] * block, block)
            x_scr[slot * block : (slot + 1) * block, :] = x_ref[pl.ds(start, block), :]

    half = x_ref.shape[0] // 2
    out = jnp.dot(x_scr[...], w_ref[...], preferred_element_type=F32)
    if scaled:
        out = out * scale_ref[:, :1]
    keep_ref[0] = out[:half].astype(BF16)
    send_ref[0] = out[half:].astype(BF16)


def project(x, weights, order, cols, scale, tile, first, count, block):
    rows, depth = x.shape
    heads = cols.shape[0]
    per_slice = weights.shape[1] // (tile * heads)
    out = jax.ShapeDtypeStruct((heads, rows // 2, count * tile), BF16)
    scaled = scale is not None
    if scale is None:
        scale = jnp.zeros((8, EXTRA), F32)
    spec = pl.BlockSpec((1, rows // 2, tile), lambda h, t, o, c: (h, 0, t))
    return pl.pallas_call(
        functools.partial(project_kernel, block=block, scaled=scaled),
        grid_spec=pltpu.PrefetchScalarGridSpec(
            num_scalar_prefetch=2,
            grid=(heads, count),
            in_specs=[
                pl.BlockSpec((rows, depth), lambda h, t, o, c: (0, 0)),
                pl.BlockSpec(scale.shape, lambda h, t, o, c: (0, 0)),
                pl.BlockSpec((depth, tile), lambda h, t, o, c: (0, c[h] * per_slice + first + t)),
            ],
            out_specs=[spec, spec],
            scratch_shapes=[pltpu.VMEM((rows, depth), BF16)],
        ),
        out_shape=[out, out],
        compiler_params=pltpu.CompilerParams(vmem_limit_bytes=VMEM_BYTES),
        cost_estimate=pl.CostEstimate(
            flops=2 * rows * depth * count * tile * heads,
            bytes_accessed=2 * (depth + rows) * count * tile * heads,
            transcendentals=0,
        ),
    )(order, cols, x, scale, weights)


def pieces_of(value):
    high = lax.reduce_precision(value, 8, 7)
    rest = value - high
    middle = lax.reduce_precision(rest, 8, 7)
    return [high.astype(BF16), middle.astype(BF16), (rest - middle).astype(BF16)]


def row_parts(pieces, jh, net, by_line, rows_dev, lanes):
    parts = []
    for jc in range(2):
        for jx in range(net.near):
            at = jh * net.near + jx
            if by_line:
                for jz in range(net.line):
                    ref = pieces[jc][jz]
                    parts.append(ref[at * rows_dev : (at + 1) * rows_dev, lanes])
            else:
                parts.append(pieces[jc][at][:, lanes])
    return jnp.concatenate(parts, 0)


def gate_up_kernel(cols, me, *refs, net, by_line, rows_dev, tile, count, last, width):
    per_core = net.line if by_line else len(net.plane)
    pieces = [refs[:per_core], refs[per_core : 2 * per_core]]
    refs = refs[2 * per_core :]
    gate_ref, up_ref = refs[:2]
    refs = refs[2:]
    jh = pl.program_id(0)
    step = pl.program_id(1)
    if last:
        gate_in, up_in, squares_in, hidden_ref, coef_ref, gate_acc, up_acc = refs
    else:
        gate_acc, up_acc, squares_ref = refs

    @pl.when((jh == 0) & (step == 0))
    def _():
        if last:
            gate_acc[...] = gate_in[...]
            up_acc[...] = up_in[...]
        else:
            gate_acc[...] = jnp.zeros_like(gate_acc)
            up_acc[...] = jnp.zeros_like(up_acc)

    for which in range(net.heads):

        @pl.when(jh == which)
        def _():
            lanes = pl.ds(pl.multiple_of(step * tile, tile), tile)
            x = row_parts(pieces, which, net, by_line, rows_dev, lanes)
            gate_acc[...] += jnp.dot(x, gate_ref[...], preferred_element_type=F32)
            up_acc[...] += jnp.dot(x, up_ref[...], preferred_element_type=F32)

    @pl.when((jh == net.heads - 1) & (step == count - 1))
    def _():
        lanes = pl.ds(count * tile, EXTRA)
        extras = [
            row_parts(pieces, h, net, by_line, rows_dev, lanes).astype(F32)
            for h in range(net.heads)
        ]
        lane = lax.broadcasted_iota(jnp.int32, (1, EXTRA), 1)
        squares = sum(extras)
        squares = jnp.sum(jnp.where(lane < 3, squares, 0.0), -1, keepdims=True)
        if not last:
            squares_ref[...] = jnp.broadcast_to(squares, squares_ref.shape)
        else:
            total = squares + squares_in[:, :1]
            norm = lax.rsqrt(total / width + EPSILON)
            mine = (lane == 3 + me[0]) | (lane == 3 + net.dp + me[0]) | (lane == 3 + 2 * net.dp + me[0])
            coef = jnp.sum(jnp.where(mine, extras[0], 0.0), -1, keepdims=True)
            coef_ref[...] = jnp.broadcast_to(coef, coef_ref.shape)
            gate = gate_acc[...] * norm
            up = up_acc[...] * norm
            hidden_ref[...] = (gate / (1.0 + jnp.exp(-gate)) * up).astype(BF16)


def gate_up(net, pieces, by_line, gate_w, up_w, cols, me, tile, first, count, rows_dev, before=None):
    flat = [piece for group in pieces for piece in group]
    width, hidden = gate_w.shape
    rows = net.dp * rows_dev
    per_slice = width // (tile * net.heads)
    last = before is not None
    weight = pl.BlockSpec((tile, hidden), lambda h, t, c, m: (c[h] * per_slice + first + t, 0))
    whole = lambda shape: pl.BlockSpec(shape, lambda h, t, c, m: (0,) * len(shape))
    in_specs = [whole(piece.shape) for piece in flat] + [weight, weight]
    operands = [cols, me, *flat, gate_w, up_w]
    acc = jax.ShapeDtypeStruct((rows, hidden), F32)
    wide = jax.ShapeDtypeStruct((rows, EXTRA), F32)
    if last:
        in_specs += [whole(value.shape) for value in before]
        operands += list(before)
        outs = [jax.ShapeDtypeStruct((rows, hidden), BF16), wide]
        scratch = [pltpu.VMEM(acc.shape, F32), pltpu.VMEM(acc.shape, F32)]
    else:
        outs = [acc, acc, wide]
        scratch = []
    return pl.pallas_call(
        functools.partial(
            gate_up_kernel,
            net=net,
            by_line=by_line,
            rows_dev=rows_dev,
            tile=tile,
            count=count,
            last=last,
            width=width,
        ),
        grid_spec=pltpu.PrefetchScalarGridSpec(
            num_scalar_prefetch=2,
            grid=(net.heads, count),
            in_specs=in_specs,
            out_specs=[whole(out.shape) for out in outs],
            scratch_shapes=scratch,
        ),
        out_shape=outs,
        compiler_params=pltpu.CompilerParams(vmem_limit_bytes=VMEM_BYTES),
        cost_estimate=pl.CostEstimate(
            flops=4 * rows * count * tile * net.heads * hidden,
            bytes_accessed=4 * count * tile * net.heads * hidden,
            transcendentals=0,
        ),
    )(*operands)


def add_up(keep, received, pick):
    total = pick(keep).astype(F32)
    for value in received:
        total = total + value.astype(F32)
    return total


def reduce_plane_first(net, keep, send, rows_dev):
    other = net.core(send)
    width = keep.shape[-1]
    shape = (len(net.plane), net.line * rows_dev, width)
    keep, other = keep.reshape(shape), other.reshape(shape)
    summed = [keep[at].astype(F32) + other[at].astype(F32) for at in range(len(net.plane))]
    total = summed[0]
    arrived = [net.in_plane(summed[at].astype(BF16), at) for at in range(1, len(net.plane))]
    for value in arrived:
        total = total + value.astype(F32)
    total = total.reshape(net.line, rows_dev, width)
    arrived = [net.in_line(total[jz].astype(BF16), jz) for jz in range(1, net.line)]
    out = total[0]
    for value in arrived:
        out = out + value.astype(F32)
    return out


def reduce_line_first(net, keep, send, rows_dev):
    other = net.core(send)
    width = keep.shape[-1]
    shape = (len(net.plane), net.line, rows_dev, width)
    keep, other = keep.reshape(shape), other.reshape(shape)
    summed = [keep[:, jz].astype(F32) + other[:, jz].astype(F32) for jz in range(net.line)]
    total = summed[0]
    arrived = [net.in_line(summed[jz].astype(BF16), jz) for jz in range(1, net.line)]
    for value in arrived:
        total = total + value.astype(F32)
    arrived = [net.in_plane(total[at].astype(BF16), at) for at in range(1, len(net.plane))]
    out = total[0]
    for value in arrived:
        out = out + value.astype(F32)
    return out


def gather_line_first(net, value):
    held = jnp.concatenate([value] + [net.in_line(value, jz) for jz in range(1, net.line)], 0)
    own = [held] + [net.in_plane(held, at) for at in range(1, len(net.plane))]
    return [own, [net.core(piece) for piece in own]]


def gather_plane_first(net, value):
    held = jnp.concatenate([value] + [net.in_plane(value, at) for at in range(1, len(net.plane))], 0)
    own = [held] + [net.in_line(held, jz) for jz in range(1, net.line)]
    return [own, [net.core(piece) for piece in own]]


def on_device(
    queries,
    kv_cache,
    lengths,
    resid,
    w_uv,
    o_proj,
    norm_gain,
    expert_ids,
    route_gates,
    expert_owner,
    gate_w,
    up_w,
    down_w,
):
    dp = lax.axis_size("dp")
    heads = lax.axis_size("heads")
    net = Net(dp, heads)
    rows_dev, width = resid.shape
    slice_width = width // heads
    tile = slice_width // 7
    wide_count, narrow_count = 5, 2
    wide = wide_count * tile
    me = lax.axis_index("dp")
    my_head = lax.axis_index("heads")
    slots = jnp.array(
        [
            jc + 2 * jx + 4 * jz
            for jc in range(2)
            for jx in range(net.near)
            for jz in range(net.line)
        ],
        jnp.int32,
    )
    order = jnp.bitwise_xor(slots, me)
    natural = jnp.arange(dp, dtype=jnp.int32)
    cols = jnp.bitwise_xor(jnp.arange(heads, dtype=jnp.int32), my_head)

    latent_out = attend(queries, kv_cache, lengths)
    gathered = lax.all_to_all(latent_out, "dp", split_axis=1, concat_axis=0, tiled=True)
    values = jnp.einsum("rhl,hlv->rhv", gathered, w_uv[0], preferred_element_type=F32).astype(BF16)
    values = values.reshape(values.shape[0], -1)
    out_proj = o_proj[0].reshape(-1, width)

    holder = jnp.sum(
        (expert_ids[:, :, None] == jnp.arange(expert_owner.shape[0], dtype=jnp.int32)).astype(jnp.int32)
        * expert_owner,
        -1,
    )
    table = jnp.sum(jnp.where(holder[:, :, None] == natural, route_gates[:, :, None], 0.0), 1)
    table_parts = pieces_of(table)

    resid_slice = lax.dynamic_slice_in_dim(resid, my_head * slice_width, slice_width, 1).astype(F32)
    gain_slice = lax.dynamic_slice_in_dim(norm_gain, my_head * slice_width, slice_width, 0).astype(F32)

    def payload(attention, lo, hi):
        mid = resid_slice[:, lo:hi] + attention
        squares = jnp.sum(mid * mid, -1, keepdims=True)
        extra = pieces_of(squares) + table_parts
        pad = jnp.zeros((rows_dev, EXTRA - 3 - 3 * dp), BF16)
        row = (mid * gain_slice[lo:hi]).astype(BF16)
        return mid, jnp.concatenate([row, *extra, pad], 1)

    keep_a, send_a = project(values, out_proj, order, cols, None, tile, 0, wide_count, rows_dev)
    keep_b, send_b = project(
        values, out_proj, order, cols, None, tile, wide_count, narrow_count, rows_dev
    )
    mid_a, row_a = payload(reduce_plane_first(net, keep_a, send_a, rows_dev), 0, wide)
    mid_b, row_b = payload(reduce_line_first(net, keep_b, send_b, rows_dev), wide, slice_width)
    pieces_a = gather_line_first(net, row_a)
    pieces_b = gather_plane_first(net, row_b)

    mine = me.reshape(1).astype(jnp.int32)
    before = gate_up(
        net, pieces_b, True, gate_w[0], up_w[0], cols, mine, tile, wide_count, narrow_count, rows_dev
    )
    hidden, coef = gate_up(
        net, pieces_a, False, gate_w[0], up_w[0], cols, mine, tile, 0, wide_count, rows_dev, before
    )
    keep_a, send_a = project(hidden, down_w[0], natural, cols, coef, tile, 0, wide_count, rows_dev)
    keep_b, send_b = project(
        hidden, down_w[0], natural, cols, coef, tile, wide_count, narrow_count, rows_dev
    )
    out_a = mid_a + reduce_plane_first(net, keep_a, send_a, rows_dev)
    out_b = mid_b + reduce_line_first(net, keep_b, send_b, rows_dev)
    return jnp.concatenate([out_a, out_b], 1).astype(BF16)


def solution(mesh):
    return jax.shard_map(
        on_device,
        mesh=mesh,
        in_specs=(
            P(("groups", "dp"), "heads", None),
            P(("groups", "dp"), None, None),
            P(("groups", "dp")),
            P(("groups", "dp"), None),
            P("heads", "dp", None, None),
            P("heads", "dp", None, None),
            P(),
            P(("groups", "dp"), None),
            P(("groups", "dp"), None),
            P(),
            P("dp", None, "heads"),
            P("dp", None, "heads"),
            P("dp", "heads", None),
        ),
        out_specs=P(("groups", "dp"), "heads"),
        check_vma=False,
    )
```

time: 504 us -> 218 us (0.43)
  waiting for transfers between devices: 293 us -> 81.5 us
  blocking collectives: 119 us -> 0 us
  starting transfers between devices: 5.49 us -> 59 us
  Pallas kernels: 0 us -> 47.4 us
  matrix products: 34.6 us -> 7.85 us
  local copies, waits for them, and re-layouts: 29.6 us -> 8.39 us
  between operations: 13.3 us -> 0.56 us
    reduce_scatter x2 -> x0, waiting for transfers between devices: 132 us -> none  [the longest x1 90.9 us: on_device(): lax.psum_scatter(jnp.dot(values, out_proj, preferred_element_type=jnp.flo...]
    all_to_all x2 -> x0, blocking collectives: 119 us -> none  [the longest x1 86.7 us: on_device(): lax.all_to_all(buffer.reshape(owners, capacity, normed.shape[1]), 'dp', s...]
    all_to_all x1, waiting for transfers between devices: 132 us -> 21.9 us  [on_device(): lax.all_to_all(latent_out, 'dp', split_axis=1, concat_axis=0, tiled=True)]
    ppermute x0 -> x48, waiting for transfers between devices: none -> 59.6 us  [move(): lax.ppermute(value, ('dp', 'heads'), [(i, i ^ mask) for i in range(count)])]
    ppermute x0 -> x48, starting transfers between devices: none -> 51.5 us  [move(): lax.ppermute(value, ('dp', 'heads'), [(i, i ^ mask) for i in range(count)])]
    pallas_call x0 -> x6, Pallas kernels: none -> 47.4 us  [the longest x4 28.9 us: project(): pl.pallas_call(functools.partial(project_kernel, block=block, scaled=scal...]
    psum x1 -> x0, waiting for transfers between devices: 28.7 us -> none  [on_device(): attention = lax.psum(attn_part, 'heads')]
    dot_general x7 -> x3, matrix products: 34.6 us -> 7.85 us  [the longest x1 4.08 us: attend(): jnp.einsum('rhc,rcl->rhl', weights, latent, preferred_element_type=F32)]
  transfers between devices with their start and end apart: 4 -> 49, of which waited for: 4 -> 25; matrix products, arithmetic and copies ran while one was open for 0% -> 5% of each run, Pallas kernels for 0% -> 10%
where the time goes in v1:
time: 218 us; the launch traced here: 217 us
  waiting for transfers between devices  81.5 us (37%)
  starting transfers between devices  59 us (27%)
  Pallas kernels  47.4 us (22%)
  other arithmetic  11.9 us (5%)
  local copies, waits for them, and re-layouts  8.39 us (4%)
  matrix products  7.85 us (4%)
    ppermute x48, waiting for transfers between devices, move(): lax.ppermute(value, ('dp', 'heads'), [(i, i ^ mask) for i in range(count)])  59.6 us
    ppermute x48, starting transfers between devices, move(): lax.ppermute(value, ('dp', 'heads'), [(i, i ^ mask) for i in range(count)])  51.5 us
    pallas_call x4, Pallas kernels, project(): pl.pallas_call(functools.partial(project_kernel, block=block, scaled=scal...  28.9 us
    all_to_all x1, waiting for transfers between devices, on_device(): lax.all_to_all(latent_out, 'dp', split_axis=1, concat_axis=0, tiled=True)  21.9 us
    pallas_call x2, Pallas kernels, gate_up(): pl.pallas_call(functools.partial(gate_up_kernel, net=net, by_line=by_line...  18.5 us
    all_to_all x1, starting transfers between devices, on_device(): lax.all_to_all(latent_out, 'dp', split_axis=1, concat_axis=0, tiled=True)  7.5 us
  transfers between devices with their start and end apart: 49, of which 25 were waited for; matrix products, arithmetic and copies ran while one was open for 5% of the time, Pallas kernels for 10%

profile of v1, /device:TPU:0, one launch (start us, length us, event | category | flops | bytes accessed | tf_op | source)
XLA Modules:
  0.0 216.5 jit_solution(9326964763950292479)
XLA Ops:
  1.3 3.3 %fusion.8 = f32[16,64,256]{2,1,0:T(8,128)S(1)} fusion(bf16[16,64,576]{2,1,0:T(8,128)(2,1)S(1)} %copy-done, bf16[16,256,576]{1,2,0:T(8,128)(2,1)} %param.15, pred[16,256]{1,0:T(8,128)(4,1)S(1)} %iota_compare_fusion.2), kind=kOutput, calls=%fused_computation.7 | convolution fusion | flops 302514176 | bytes 6950912 | tf_op jit(solution)/shard_map/rhk,rck->rhc/dot_general | solution.py:21
  5.0 4.1 %fusion.3 = bf16[16,64,512]{2,1,0:T(8,128)(2,1)S(1)} fusion(bf16[16,256,576]{1,2,0:T(8,128)(2,1)} %param.15, f32[16,64]{1,0:T(8,128)S(1)} %fusion.63, f32[16,64,256]{2,1,0:T(8,128)S(1)} %fusion.8), kind=kOutput, calls=%fused_computation.3 | convolution fusion | flops 269747456 | bytes 7348224 | tf_op jit(solution)/shard_map/rhc,rcl->rhl/dot_general | solution.py:30
  10.6 7.5 %all-to-all-start = ((bf16[16,64,512]{2,0,1:T(8,128)(2,1)}), bf16[16,64,512]{2,0,1:T(8,128)(2,1)S(1)}, u32[]{:S(2)}, u32[]{:S(2)}) async-start(bf16[16,64,512]{2,0,1:T(8,128)(2,1)} %copy.114), calls=%async_computation | async-start | bytes 2097152 | tf_op jit(solution)/shard_map/all_to_all | solution.py:320
  19.2 21.9 %all-to-all-done = bf16[16,64,512]{2,0,1:T(8,128)(2,1)S(1)} async-done(((bf16[16,64,512]{2,0,1:T(8,128)(2,1)}), bf16[16,64,512]{2,0,1:T(8,128)(2,1)S(1)}, u32[]{:S(2)}, u32[]{:S(2)}) %all-to-all-start) | async-done | bytes 1048608 | tf_op jit(solution)/shard_map/all_to_all | solution.py:320
  43.1 5.0 %shard_map.137 = (bf16[2,128,1024]{2,1,0:T(8,128)(2,1)}, bf16[2,128,1024]{2,1,0:T(8,128)(2,1)}) custom-call(s32[16]{0:T(128)} %broadcast_xor_fusion.order, s32[2]{0:T(128)} %iota_xor_fusion.cols, bf16[256,512]{1,0:T(8,128)(2,1)} %copy.143.x_ref, f32[8,128]{1,0:T(8,128)} %broadcast_3_scale_ref.2.scale_ref, bf16[512,7168]{1,0:T(8,128)(2,1)} %bitcast.187), custom_call_target="tpu_custom_call" | custom-call | flops 536870912 | bytes 3145728 | tf_op jit(solution)/shard_map/pallas_call | solution.py:81
  49.4 9.4 %shard_map.136 = (bf16[2,128,2560]{2,1,0:T(8,128)(2,1)}, bf16[2,128,2560]{2,1,0:T(8,128)(2,1)}) custom-call(s32[16]{0:T(128)} %broadcast_xor_fusion.order, s32[2]{0:T(128)} %iota_xor_fusion.cols, bf16[256,512]{1,0:T(8,128)(2,1)} %copy.143.x_ref, f32[8,128]{1,0:T(8,128)} %broadcast_3_scale_ref.2.scale_ref, bf16[512,7168]{1,0:T(8,128)(2,1)} %bitcast.188), custom_call_target="tpu_custom_call" | custom-call | flops 1342177280 | bytes 7864320 | tf_op jit(solution)/shard_map/pallas_call | solution.py:81
  60.2 3.4 %collective-permute-start.20 = (bf16[4,16,1024]{2,1,0:T(8,128)(2,1)S(1)}, bf16[4,16,1024]{2,1,0:T(8,128)(2,1)S(1)}, u32[]{:S(2)}, u32[]{:S(2)}) collective-permute-start(bf16[4,16,1024]{2,1,0:T(8,128)(2,1)S(1)} %get-tuple-element.54), channel_id=1, source_target_pairs={{0,24},{1,25},{2,26},{3,27},{4,28},{5,29},{6,30},{7,31},{8,16},{9,... | collective-permute-start | bytes 393224 | tf_op jit(solution)/shard_map/ppermute | solution.py:44
  68.1 8.3 %collective-permute-done.19 = bf16[4,16,1024]{2,1,0:T(8,128)(2,1)S(1)} collective-permute-done((bf16[4,16,1024]{2,1,0:T(8,128)(2,1)S(1)}, bf16[4,16,1024]{2,1,0:T(8,128)(2,1)S(1)}, u32[]{:S(2)}, u32[]{:S(2)}) %collective-permute-start.19) | collective-permute-done | bytes 131104 | tf_op jit(solution)/shard_map/ppermute | solution.py:44
  77.4 3.2 %collective-permute-start.23 = (bf16[16,1024]{1,0:T(8,128)(2,1)S(1)}, bf16[16,1024]{1,0:T(8,128)(2,1)S(1)}, u32[]{:S(2)}, u32[]{:S(2)}) collective-permute-start(bf16[16,1024]{1,0:T(8,128)(2,1)S(1)} %get-tuple-element.65), channel_id=1, source_target_pairs={{0,5},{1,4},{2,7},{3,6},{4,1},{5,0},{6,3},{7,2},{8,13},{9,12},{10,... | collective-permute-start | bytes 98312 | tf_op jit(solution)/shard_map/ppermute | solution.py:44
  82.6 2.0 collective-permute-done.22
  91.2 7.0 %collective-permute-done.3 = bf16[64,2560]{1,0:T(8,128)(2,1)} collective-permute-done((bf16[64,2560]{1,0:T(8,128)(2,1)}, bf16[64,2560]{1,0:T(8,128)(2,1)}, u32[]{:S(2)}, u32[]{:S(2)}) %collective-permute-start.3) | collective-permute-done | bytes 327712 | tf_op jit(solution)/shard_map/ppermute | solution.py:44
  98.2 4.3 %collective-permute-done.2 = bf16[64,2560]{1,0:T(8,128)(2,1)} collective-permute-done((bf16[64,2560]{1,0:T(8,128)(2,1)}, bf16[64,2560]{1,0:T(8,128)(2,1)}, u32[]{:S(2)}, u32[]{:S(2)}) %collective-permute-start.2) | collective-permute-done | bytes 327712 | tf_op jit(solution)/shard_map/ppermute | solution.py:44
  105.9 2.9 %collective-permute-start.4 = (bf16[16,2560]{1,0:T(8,128)(2,1)S(1)}, bf16[16,2560]{1,0:T(8,128)(2,1)S(1)}, u32[]{:S(2)}, u32[]{:S(2)}) collective-permute-start(bf16[16,2560]{1,0:T(8,128)(2,1)S(1)} %get-tuple-element.58), channel_id=1, source_target_pairs={{0,8},{1,9},{2,10},{3,11},{4,12},{5,13},{6,14},{7,15},{8,0},{9,1},... | collective-permute-start | bytes 245768 | tf_op jit(solution)/shard_map/ppermute | solution.py:44
  116.0 2.6 %collective-permute-start.7 = (bf16[16,2688]{1,0:T(8,128)(2,1)S(1)}, bf16[16,2688]{1,0:T(8,128)(2,1)S(1)}, u32[]{:S(2)}, u32[]{:S(2)}) collective-permute-start(bf16[16,2688]{1,0:T(8,128)(2,1)S(1)} %concatenate.16), channel_id=1, source_target_pairs={{0,8},{1,9},{2,10},{3,11},{4,12},{5,13},{6,14},{7,15},{8,0},{9,1},... | collective-permute-start | bytes 258056 | tf_op jit(solution)/shard_map/ppermute | solution.py:44
  118.7 2.3 %collective-permute-start.28 = (bf16[64,1152]{1,0:T(8,128)(2,1)S(1)}, bf16[64,1152]{1,0:T(8,128)(2,1)S(1)}, u32[]{:S(2)}, u32[]{:S(2)}) collective-permute-start(bf16[64,1152]{1,0:T(8,128)(2,1)S(1)} %pad_maximum_fusion.1.refs_0_), channel_id=1, source_target_pairs={{0,16},{1,17},{2,18},{3,19},{4,20},{5,21},{6,22},{7,23},{8,24},{9,... | collective-permute-start | bytes 442376 | tf_op jit(solution)/shard_map/ppermute | solution.py:44
  121.5 2.8 %collective-permute-done.8 = bf16[16,2688]{1,0:T(8,128)(2,1)S(1)} collective-permute-done((bf16[16,2688]{1,0:T(8,128)(2,1)S(1)}, bf16[16,2688]{1,0:T(8,128)(2,1)S(1)}, u32[]{:S(2)}, u32[]{:S(2)}) %collective-permute-start.8) | collective-permute-done | bytes 86048 | tf_op jit(solution)/shard_map/ppermute | solution.py:44
  124.3 2.6 %collective-permute-done.7 = bf16[16,2688]{1,0:T(8,128)(2,1)S(1)} collective-permute-done((bf16[16,2688]{1,0:T(8,128)(2,1)S(1)}, bf16[16,2688]{1,0:T(8,128)(2,1)S(1)}, u32[]{:S(2)}, u32[]{:S(2)}) %collective-permute-start.7) | collective-permute-done | bytes 86048 | tf_op jit(solution)/shard_map/ppermute | solution.py:44
  132.3 5.7 %collective-permute-done.29.refs_3_ = bf16[64,1152]{1,0:T(8,128)(2,1)S(1)} collective-permute-done((bf16[64,1152]{1,0:T(8,128)(2,1)S(1)}, bf16[64,1152]{1,0:T(8,128)(2,1)S(1)}, u32[]{:S(2)}, u32[]{:S(2)}) %collective-permute-start.29) | collective-permute-done | bytes 147488 | tf_op jit(solution)/shard_map/ppermute | solution.py:44
  139.9 2.2 %collective-permute-done.11.refs_2_ = bf16[64,2688]{1,0:T(8,128)(2,1)S(1)} collective-permute-done((bf16[64,2688]{1,0:T(8,128)(2,1)S(1)}, bf16[64,2688]{1,0:T(8,128)(2,1)S(1)}, u32[]{:S(2)}, u32[]{:S(2)}) %collective-permute-start.11) | collective-permute-done | bytes 344096 | tf_op jit(solution)/shard_map/ppermute | solution.py:44
  145.2 6.2 %shard_map.138 = (f32[256,512]{1,0:T(8,128)}, f32[256,512]{1,0:T(8,128)}, f32[256,128]{1,0:T(8,128)}) custom-call(s32[2]{0:T(128)} %iota_xor_fusion.cols, s32[1]{0:T(128)} %bitcast.13.me, bf16[64,1152]{1,0:T(8,128)(2,1)} %copy-done.7, bf16[64,1152]{1,0:T(8,128)(2,1)} %copy-done.17, bf16[64,1152]{1,0:T(8,128)(2,1)} %copy-done.18, ...), custom_call_target="tpu_custom_call" | custom-call | flops 1073741824 | bytes 4194304 | tf_op jit(solution)/shard_map/pallas_call | solution.py:199
  152.5 12.3 %shard_map.139 = (bf16[256,512]{1,0:T(8,128)(2,1)}, f32[256,128]{1,0:T(8,128)}) custom-call(s32[2]{0:T(128)} %iota_xor_fusion.cols, s32[1]{0:T(128)} %bitcast.13.me, bf16[64,2688]{1,0:T(8,128)(2,1)} %copy-done.2, bf16[64,2688]{1,0:T(8,128)(2,1)} %copy-done.10, bf16[64,2688]{1,0:T(8,128)(2,1)} %copy-done.11, bf16[64,2688]{1,0:T(8,128)(2,1)} %copy-done.12, ...), custom_call_target="tpu_custom_call" | custom-call | flops 2684354560 | bytes 10485760 | tf_op jit(solution)/shard_map/pallas_call | solution.py:199
  165.4 9.3 %shard_map.140 = (bf16[2,128,2560]{2,1,0:T(8,128)(2,1)}, bf16[2,128,2560]{2,1,0:T(8,128)(2,1)}) custom-call(s32[16]{0:T(128)} %iota.22.order, s32[2]{0:T(128)} %iota_xor_fusion.cols, bf16[256,512]{1,0:T(8,128)(2,1)} %get-tuple-element.25.x_ref, f32[256,128]{1,0:T(8,128)} %get-tuple-element.26.scale_ref, bf16[512,7168]{1,0:T(8,128)(2,1)} %bitcast.193), custom_call_target="tpu_custom_call" | custom-call | flops 1342177280 | bytes 7864320 | tf_op jit(solution)/shard_map/pallas_call | solution.py:81
  175.4 5.1 %shard_map.141 = (bf16[2,128,1024]{2,1,0:T(8,128)(2,1)}, bf16[2,128,1024]{2,1,0:T(8,128)(2,1)}) custom-call(s32[16]{0:T(128)} %iota.23.order, s32[2]{0:T(128)} %iota_xor_fusion.cols, bf16[256,512]{1,0:T(8,128)(2,1)} %get-tuple-element.25.x_ref, f32[256,128]{1,0:T(8,128)} %get-tuple-element.26.scale_ref, bf16[512,7168]{1,0:T(8,128)(2,1)} %bitcast.194), custom_call_target="tpu_custom_call" | custom-call | flops 536870912 | bytes 3145728 | tf_op jit(solution)/shard_map/pallas_call | solution.py:81
  183.7 2.4 %collective-permute-start.44 = (bf16[4,16,1024]{2,1,0:T(8,128)(2,1)S(1)}, bf16[4,16,1024]{2,1,0:T(8,128)(2,1)S(1)}, u32[]{:S(2)}, u32[]{:S(2)}) collective-permute-start(bf16[4,16,1024]{2,1,0:T(8,128)(2,1)S(1)} %get-tuple-element.51), channel_id=1, source_target_pairs={{0,24},{1,25},{2,26},{3,27},{4,28},{5,29},{6,30},{7,31},{8,16},{9,... | collective-permute-start | bytes 393224 | tf_op jit(solution)/shard_map/ppermute | solution.py:44
  186.2 2.0 collective-permute-start.42
  189.2 2.0 collective-permute-start.36
  193.3 3.8 %collective-permute-done.43 = bf16[4,16,1024]{2,1,0:T(8,128)(2,1)S(1)} collective-permute-done((bf16[4,16,1024]{2,1,0:T(8,128)(2,1)S(1)}, bf16[4,16,1024]{2,1,0:T(8,128)(2,1)S(1)}, u32[]{:S(2)}, u32[]{:S(2)}) %collective-permute-start.43) | collective-permute-done | bytes 131104 | tf_op jit(solution)/shard_map/ppermute | solution.py:44
  201.7 4.3 %collective-permute-done.36 = bf16[64,2560]{1,0:T(8,128)(2,1)S(1)} collective-permute-done((bf16[64,2560]{1,0:T(8,128)(2,1)S(1)}, bf16[64,2560]{1,0:T(8,128)(2,1)S(1)}, u32[]{:S(2)}, u32[]{:S(2)}) %collective-permute-start.36) | collective-permute-done | bytes 327712 | tf_op jit(solution)/shard_map/ppermute | solution.py:44
  206.3 2.2 collective-permute-start.40
  208.5 2.3 %collective-permute-start.38 = (bf16[16,2560]{1,0:T(8,128)(2,1)S(1)}, bf16[16,2560]{1,0:T(8,128)(2,1)S(1)}, u32[]{:S(2)}, u32[]{:S(2)}) collective-permute-start(bf16[16,2560]{1,0:T(8,128)(2,1)S(1)} %get-tuple-element.55), channel_id=1, source_target_pairs={{0,8},{1,9},{2,10},{3,11},{4,12},{5,13},{6,14},{7,15},{8,0},{9,1},... | collective-permute-start | bytes 245768 | tf_op jit(solution)/shard_map/ppermute | solution.py:44
  210.8 2.8 %collective-permute-done.40 = bf16[16,2560]{1,0:T(8,128)(2,1)S(1)} collective-permute-done((bf16[16,2560]{1,0:T(8,128)(2,1)S(1)}, bf16[16,2560]{1,0:T(8,128)(2,1)S(1)}, u32[]{:S(2)}, u32[]{:S(2)}) %collective-permute-start.40) | collective-permute-done | bytes 81952 | tf_op jit(solution)/shard_map/ppermute | solution.py:44
  213.6 2.2 %collective-permute-done.39 = bf16[16,2560]{1,0:T(8,128)(2,1)S(1)} collective-permute-done((bf16[16,2560]{1,0:T(8,128)(2,1)S(1)}, bf16[16,2560]{1,0:T(8,128)(2,1)S(1)}, u32[]{:S(2)}, u32[]{:S(2)}) %collective-permute-start.39) | collective-permute-done | bytes 81952 | tf_op jit(solution)/shard_map/ppermute | solution.py:44
  (199 shorter events, 58.4 us)
Async XLA Ops:
  10.6 30.4 %all-to-all-start = ((bf16[16,64,512]{2,0,1:T(8,128)(2,1)}), bf16[16,64,512]{2,0,1:T(8,128)(2,1)S(1)}, u32[]{:S(2)}, u32[]{:S(2)}) async-start(bf16[16,64,512]{2,0,1:T(8,128)(2,1)} %copy.114), calls=%async_computation | async-start | bytes 2097152 | tf_op jit(solution)/shard_map/all_to_all | solution.py:320
  48.2 10.8 %collective-permute-start.17 = (bf16[2,128,1024]{2,1,0:T(8,128)(2,1)}, bf16[2,128,1024]{2,1,0:T(8,128)(2,1)}, u32[]{:S(2)}, u32[]{:S(2)}) collective-permute-start(bf16[2,128,1024]{2,1,0:T(8,128)(2,1)} %get-tuple-element.21), channel_id=1, source_target_pairs={{0,2},{1,3},{2,0},{3,1},{4,6},{5,7},{6,4},{7,5},{8,10},{9,11},{10,... | collective-permute-start | bytes 1572872 | tf_op jit(solution)/shard_map/ppermute | solution.py:44
  58.8 26.4 %collective-permute-start = (bf16[2,128,2560]{2,1,0:T(8,128)(2,1)}, bf16[2,128,2560]{2,1,0:T(8,128)(2,1)S(1)}, u32[]{:S(2)}, u32[]{:S(2)}) collective-permute-start(bf16[2,128,2560]{2,1,0:T(8,128)(2,1)} %get-tuple-element.19), channel_id=1, source_target_pairs={{0,2},{1,3},{2,0},{3,1},{4,6},{5,7},{6,4},{7,5},{8,10},{9,11},{10,... | collective-permute-start | bytes 3932168 | tf_op jit(solution)/shard_map/ppermute | solution.py:44
  60.2 7.9 %collective-permute-start.20 = (bf16[4,16,1024]{2,1,0:T(8,128)(2,1)S(1)}, bf16[4,16,1024]{2,1,0:T(8,128)(2,1)S(1)}, u32[]{:S(2)}, u32[]{:S(2)}) collective-permute-start(bf16[4,16,1024]{2,1,0:T(8,128)(2,1)S(1)} %get-tuple-element.54), channel_id=1, source_target_pairs={{0,24},{1,25},{2,26},{3,27},{4,28},{5,29},{6,30},{7,31},{8,16},{9,... | collective-permute-start | bytes 393224 | tf_op jit(solution)/shard_map/ppermute | solution.py:44
  63.6 12.8 %collective-permute-start.19 = (bf16[4,16,1024]{2,1,0:T(8,128)(2,1)S(1)}, bf16[4,16,1024]{2,1,0:T(8,128)(2,1)S(1)}, u32[]{:S(2)}, u32[]{:S(2)}) collective-permute-start(bf16[4,16,1024]{2,1,0:T(8,128)(2,1)S(1)} %get-tuple-element.53), channel_id=1, source_target_pairs={{0,16},{1,17},{2,18},{3,19},{4,20},{5,21},{6,22},{7,23},{8,24},{9,... | collective-permute-start | bytes 393224 | tf_op jit(solution)/shard_map/ppermute | solution.py:44
  65.3 11.1 %collective-permute-start.18 = (bf16[4,16,1024]{2,1,0:T(8,128)(2,1)S(1)}, bf16[4,16,1024]{2,1,0:T(8,128)(2,1)S(1)}, u32[]{:S(2)}, u32[]{:S(2)}) collective-permute-start(bf16[4,16,1024]{2,1,0:T(8,128)(2,1)S(1)} %get-tuple-element.52), channel_id=1, source_target_pairs={{0,8},{1,9},{2,10},{3,11},{4,12},{5,13},{6,14},{7,15},{8,0},{9,1},... | collective-permute-start | bytes 393224 | tf_op jit(solution)/shard_map/ppermute | solution.py:44
  86.3 11.9 %collective-permute-start.3 = (bf16[64,2560]{1,0:T(8,128)(2,1)}, bf16[64,2560]{1,0:T(8,128)(2,1)}, u32[]{:S(2)}, u32[]{:S(2)}) collective-permute-start(bf16[64,2560]{1,0:T(8,128)(2,1)} %get-tuple-element.47), channel_id=1, source_target_pairs={{0,5},{1,4},{2,7},{3,6},{4,1},{5,0},{6,3},{7,2},{8,13},{9,12},{10,... | collective-permute-start | bytes 983048 | tf_op jit(solution)/shard_map/ppermute | solution.py:44
  87.3 15.2 %collective-permute-start.2 = (bf16[64,2560]{1,0:T(8,128)(2,1)}, bf16[64,2560]{1,0:T(8,128)(2,1)}, u32[]{:S(2)}, u32[]{:S(2)}) collective-permute-start(bf16[64,2560]{1,0:T(8,128)(2,1)} %get-tuple-element.48), channel_id=1, source_target_pairs={{0,1},{1,0},{2,3},{3,2},{4,5},{5,4},{6,7},{7,6},{8,9},{9,8},{10,11... | collective-permute-start | bytes 983048 | tf_op jit(solution)/shard_map/ppermute | solution.py:44
  87.9 15.0 %collective-permute-start.1 = (bf16[64,2560]{1,0:T(8,128)(2,1)S(1)}, bf16[64,2560]{1,0:T(8,128)(2,1)}, u32[]{:S(2)}, u32[]{:S(2)}) collective-permute-start(bf16[64,2560]{1,0:T(8,128)(2,1)S(1)} %get-tuple-element.46), channel_id=1, source_target_pairs={{0,4},{1,5},{2,6},{3,7},{4,0},{5,1},{6,2},{7,3},{8,12},{9,13},{10,... | collective-permute-start | bytes 983048 | tf_op jit(solution)/shard_map/ppermute | solution.py:44
  105.9 7.8 %collective-permute-start.5 = (bf16[16,2560]{1,0:T(8,128)(2,1)S(1)}, bf16[16,2560]{1,0:T(8,128)(2,1)S(1)}, u32[]{:S(2)}, u32[]{:S(2)}) collective-permute-start(bf16[16,2560]{1,0:T(8,128)(2,1)S(1)} %get-tuple-element.60), channel_id=1, source_target_pairs={{0,16},{1,17},{2,18},{3,19},{4,20},{5,21},{6,22},{7,23},{8,24},{9,... | collective-permute-start | bytes 245768 | tf_op jit(solution)/shard_map/ppermute | solution.py:44
  110.2 8.4 %collective-permute-start.25 = (bf16[16,1152]{1,0:T(8,128)(2,1)S(1)}, bf16[16,1152]{1,0:T(8,128)(2,1)S(1)}, u32[]{:S(2)}, u32[]{:S(2)}) collective-permute-start(bf16[16,1152]{1,0:T(8,128)(2,1)S(1)} %concatenate.18), channel_id=1, source_target_pairs={{0,1},{1,0},{2,3},{3,2},{4,5},{5,4},{6,7},{7,6},{8,9},{9,8},{10,11... | collective-permute-start | bytes 110600 | tf_op jit(solution)/shard_map/ppermute | solution.py:44
  116.0 8.3 %collective-permute-start.8 = (bf16[16,2688]{1,0:T(8,128)(2,1)S(1)}, bf16[16,2688]{1,0:T(8,128)(2,1)S(1)}, u32[]{:S(2)}, u32[]{:S(2)}) collective-permute-start(bf16[16,2688]{1,0:T(8,128)(2,1)S(1)} %concatenate.16), channel_id=1, source_target_pairs={{0,16},{1,17},{2,18},{3,19},{4,20},{5,21},{6,22},{7,23},{8,24},{9,... | collective-permute-start | bytes 258056 | tf_op jit(solution)/shard_map/ppermute | solution.py:44
  116.0 11.0 %collective-permute-start.7 = (bf16[16,2688]{1,0:T(8,128)(2,1)S(1)}, bf16[16,2688]{1,0:T(8,128)(2,1)S(1)}, u32[]{:S(2)}, u32[]{:S(2)}) collective-permute-start(bf16[16,2688]{1,0:T(8,128)(2,1)S(1)} %concatenate.16), channel_id=1, source_target_pairs={{0,8},{1,9},{2,10},{3,11},{4,12},{5,13},{6,14},{7,15},{8,0},{9,1},... | collective-permute-start | bytes 258056 | tf_op jit(solution)/shard_map/ppermute | solution.py:44
  118.7 11.9 %collective-permute-start.27 = (bf16[64,1152]{1,0:T(8,128)(2,1)S(1)}, bf16[64,1152]{1,0:T(8,128)(2,1)S(1)}, u32[]{:S(2)}, u32[]{:S(2)}) collective-permute-start(bf16[64,1152]{1,0:T(8,128)(2,1)S(1)} %pad_maximum_fusion.1.refs_0_), channel_id=1, source_target_pairs={{0,8},{1,9},{2,10},{3,11},{4,12},{5,13},{6,14},{7,15},{8,0},{9,1},... | collective-permute-start | bytes 442376 | tf_op jit(solution)/shard_map/ppermute | solution.py:44
  118.7 13.6 %collective-permute-start.28 = (bf16[64,1152]{1,0:T(8,128)(2,1)S(1)}, bf16[64,1152]{1,0:T(8,128)(2,1)S(1)}, u32[]{:S(2)}, u32[]{:S(2)}) collective-permute-start(bf16[64,1152]{1,0:T(8,128)(2,1)S(1)} %pad_maximum_fusion.1.refs_0_), channel_id=1, source_target_pairs={{0,16},{1,17},{2,18},{3,19},{4,20},{5,21},{6,22},{7,23},{8,24},{9,... | collective-permute-start | bytes 442376 | tf_op jit(solution)/shard_map/ppermute | solution.py:44
  127.0 12.5 %collective-permute-start.10 = (bf16[64,2688]{1,0:T(8,128)(2,1)S(1)}, bf16[64,2688]{1,0:T(8,128)(2,1)S(1)}, u32[]{:S(2)}, u32[]{:S(2)}) collective-permute-start(bf16[64,2688]{1,0:T(8,128)(2,1)S(1)} %pad_maximum_fusion.refs_0_), channel_id=1, source_target_pairs={{0,4},{1,5},{2,6},{3,7},{4,0},{5,1},{6,2},{7,3},{8,12},{9,13},{10,... | collective-permute-start | bytes 1032200 | tf_op jit(solution)/shard_map/ppermute | solution.py:44
  127.3 14.8 %collective-permute-start.11 = (bf16[64,2688]{1,0:T(8,128)(2,1)S(1)}, bf16[64,2688]{1,0:T(8,128)(2,1)S(1)}, u32[]{:S(2)}, u32[]{:S(2)}) collective-permute-start(bf16[64,2688]{1,0:T(8,128)(2,1)S(1)} %pad_maximum_fusion.refs_0_), channel_id=1, source_target_pairs={{0,1},{1,0},{2,3},{3,2},{4,5},{5,4},{6,7},{7,6},{8,9},{9,8},{10,11... | collective-permute-start | bytes 1032200 | tf_op jit(solution)/shard_map/ppermute | solution.py:44
  129.1 13.1 %collective-permute-start.12 = (bf16[64,2688]{1,0:T(8,128)(2,1)S(1)}, bf16[64,2688]{1,0:T(8,128)(2,1)S(1)}, u32[]{:S(2)}, u32[]{:S(2)}) collective-permute-start(bf16[64,2688]{1,0:T(8,128)(2,1)S(1)} %pad_maximum_fusion.refs_0_), channel_id=1, source_target_pairs={{0,5},{1,4},{2,7},{3,6},{4,1},{5,0},{6,3},{7,2},{8,13},{9,12},{10,... | collective-permute-start | bytes 1032200 | tf_op jit(solution)/shard_map/ppermute | solution.py:44
  139.4 12.0 %collective-permute-start.13 = (bf16[64,2688]{1,0:T(8,128)(2,1)S(1)}, bf16[64,2688]{1,0:T(8,128)(2,1)S(1)}, u32[]{:S(2)}, u32[]{:S(2)}) collective-permute-start(bf16[64,2688]{1,0:T(8,128)(2,1)S(1)} %pad_maximum_fusion.refs_0_), channel_id=1, source_target_pairs={{0,2},{1,3},{2,0},{3,1},{4,6},{5,7},{6,4},{7,5},{8,10},{9,11},{10,... | collective-permute-start | bytes 1032200 | tf_op jit(solution)/shard_map/ppermute | solution.py:44
  139.5 11.9 %collective-permute-start.14 = (bf16[64,2688]{1,0:T(8,128)(2,1)S(1)}, bf16[64,2688]{1,0:T(8,128)(2,1)S(1)}, u32[]{:S(2)}, u32[]{:S(2)}) collective-permute-start(bf16[64,2688]{1,0:T(8,128)(2,1)S(1)} %collective-permute-done.10.refs_1_), channel_id=1, source_target_pairs={{0,2},{1,3},{2,0},{3,1},{4,6},{5,7},{6,4},{7,5},{8,10},{9,11},{10,... | collective-permute-start | bytes 1032200 | tf_op jit(solution)/shard_map/ppermute | solution.py:44
  142.1 9.3 %collective-permute-start.15 = (bf16[64,2688]{1,0:T(8,128)(2,1)S(1)}, bf16[64,2688]{1,0:T(8,128)(2,1)S(1)}, u32[]{:S(2)}, u32[]{:S(2)}) collective-permute-start(bf16[64,2688]{1,0:T(8,128)(2,1)S(1)} %collective-permute-done.11.refs_2_), channel_id=1, source_target_pairs={{0,2},{1,3},{2,0},{3,1},{4,6},{5,7},{6,4},{7,5},{8,10},{9,11},{10,... | collective-permute-start | bytes 1032200 | tf_op jit(solution)/shard_map/ppermute | solution.py:44
  142.1 9.3 %collective-permute-start.16 = (bf16[64,2688]{1,0:T(8,128)(2,1)S(1)}, bf16[64,2688]{1,0:T(8,128)(2,1)S(1)}, u32[]{:S(2)}, u32[]{:S(2)}) collective-permute-start(bf16[64,2688]{1,0:T(8,128)(2,1)S(1)} %collective-permute-done.12.refs_3_), channel_id=1, source_target_pairs={{0,2},{1,3},{2,0},{3,1},{4,6},{5,7},{6,4},{7,5},{8,10},{9,11},{10,... | collective-permute-start | bytes 1032200 | tf_op jit(solution)/shard_map/ppermute | solution.py:44
  174.7 13.5 %collective-permute-start.34 = (bf16[2,128,2560]{2,1,0:T(8,128)(2,1)}, bf16[2,128,2560]{2,1,0:T(8,128)(2,1)S(1)}, u32[]{:S(2)}, u32[]{:S(2)}) collective-permute-start(bf16[2,128,2560]{2,1,0:T(8,128)(2,1)} %get-tuple-element.28), channel_id=1, source_target_pairs={{0,2},{1,3},{2,0},{3,1},{4,6},{5,7},{6,4},{7,5},{8,10},{9,11},{10,... | collective-permute-start | bytes 3932168 | tf_op jit(solution)/shard_map/ppermute | solution.py:44
  183.7 8.3 %collective-permute-start.44 = (bf16[4,16,1024]{2,1,0:T(8,128)(2,1)S(1)}, bf16[4,16,1024]{2,1,0:T(8,128)(2,1)S(1)}, u32[]{:S(2)}, u32[]{:S(2)}) collective-permute-start(bf16[4,16,1024]{2,1,0:T(8,128)(2,1)S(1)} %get-tuple-element.51), channel_id=1, source_target_pairs={{0,24},{1,25},{2,26},{3,27},{4,28},{5,29},{6,30},{7,31},{8,16},{9,... | collective-permute-start | bytes 393224 | tf_op jit(solution)/shard_map/ppermute | solution.py:44
  186.2 10.9 %collective-permute-start.43 = (bf16[4,16,1024]{2,1,0:T(8,128)(2,1)S(1)}, bf16[4,16,1024]{2,1,0:T(8,128)(2,1)S(1)}, u32[]{:S(2)}, u32[]{:S(2)}) collective-permute-start(bf16[4,16,1024]{2,1,0:T(8,128)(2,1)S(1)} %get-tuple-element.50), channel_id=1, source_target_pairs={{0,16},{1,17},{2,18},{3,19},{4,20},{5,21},{6,22},{7,23},{8,24},{9,... | collective-permute-start | bytes 393224 | tf_op jit(solution)/shard_map/ppermute | solution.py:44
  186.2 10.9 %collective-permute-start.42 = (bf16[4,16,1024]{2,1,0:T(8,128)(2,1)S(1)}, bf16[4,16,1024]{2,1,0:T(8,128)(2,1)S(1)}, u32[]{:S(2)}, u32[]{:S(2)}) collective-permute-start(bf16[4,16,1024]{2,1,0:T(8,128)(2,1)S(1)} %get-tuple-element.49), channel_id=1, source_target_pairs={{0,8},{1,9},{2,10},{3,11},{4,12},{5,13},{6,14},{7,15},{8,0},{9,1},... | collective-permute-start | bytes 393224 | tf_op jit(solution)/shard_map/ppermute | solution.py:44
  188.5 12.4 %collective-permute-start.37 = (bf16[64,2560]{1,0:T(8,128)(2,1)S(1)}, bf16[64,2560]{1,0:T(8,128)(2,1)S(1)}, u32[]{:S(2)}, u32[]{:S(2)}) collective-permute-start(bf16[64,2560]{1,0:T(8,128)(2,1)S(1)} %get-tuple-element.44), channel_id=1, source_target_pairs={{0,5},{1,4},{2,7},{3,6},{4,1},{5,0},{6,3},{7,2},{8,13},{9,12},{10,... | collective-permute-start | bytes 983048 | tf_op jit(solution)/shard_map/ppermute | solution.py:44
  189.2 16.8 %collective-permute-start.36 = (bf16[64,2560]{1,0:T(8,128)(2,1)S(1)}, bf16[64,2560]{1,0:T(8,128)(2,1)S(1)}, u32[]{:S(2)}, u32[]{:S(2)}) collective-permute-start(bf16[64,2560]{1,0:T(8,128)(2,1)S(1)} %get-tuple-element.45), channel_id=1, source_target_pairs={{0,1},{1,0},{2,3},{3,2},{4,5},{5,4},{6,7},{7,6},{8,9},{9,8},{10,11... | collective-permute-start | bytes 983048 | tf_op jit(solution)/shard_map/ppermute | solution.py:44
  192.1 14.0 %collective-permute-start.35 = (bf16[64,2560]{1,0:T(8,128)(2,1)S(1)}, bf16[64,2560]{1,0:T(8,128)(2,1)S(1)}, u32[]{:S(2)}, u32[]{:S(2)}) collective-permute-start(bf16[64,2560]{1,0:T(8,128)(2,1)S(1)} %get-tuple-element.43), channel_id=1, source_target_pairs={{0,4},{1,5},{2,6},{3,7},{4,0},{5,1},{6,2},{7,3},{8,12},{9,13},{10,... | collective-permute-start | bytes 983048 | tf_op jit(solution)/shard_map/ppermute | solution.py:44
  198.1 10.4 %collective-permute-start.47 = (bf16[16,1024]{1,0:T(8,128)(2,1)S(1)}, bf16[16,1024]{1,0:T(8,128)(2,1)S(1)}, u32[]{:S(2)}, u32[]{:S(2)}) collective-permute-start(bf16[16,1024]{1,0:T(8,128)(2,1)S(1)} %get-tuple-element.62), channel_id=1, source_target_pairs={{0,5},{1,4},{2,7},{3,6},{4,1},{5,0},{6,3},{7,2},{8,13},{9,12},{10,... | collective-permute-start | bytes 98312 | tf_op jit(solution)/shard_map/ppermute | solution.py:44
  198.9 11.9 %collective-permute-start.46 = (bf16[16,1024]{1,0:T(8,128)(2,1)S(1)}, bf16[16,1024]{1,0:T(8,128)(2,1)S(1)}, u32[]{:S(2)}, u32[]{:S(2)}) collective-permute-start(bf16[16,1024]{1,0:T(8,128)(2,1)S(1)} %get-tuple-element.63), channel_id=1, source_target_pairs={{0,1},{1,0},{2,3},{3,2},{4,5},{5,4},{6,7},{7,6},{8,9},{9,8},{10,11... | collective-permute-start | bytes 98312 | tf_op jit(solution)/shard_map/ppermute | solution.py:44
  200.9 9.9 %collective-permute-start.45 = (bf16[16,1024]{1,0:T(8,128)(2,1)S(1)}, bf16[16,1024]{1,0:T(8,128)(2,1)S(1)}, u32[]{:S(2)}, u32[]{:S(2)}) collective-permute-start(bf16[16,1024]{1,0:T(8,128)(2,1)S(1)} %get-tuple-element.61), channel_id=1, source_target_pairs={{0,4},{1,5},{2,6},{3,7},{4,0},{5,1},{6,2},{7,3},{8,12},{9,13},{10,... | collective-permute-start | bytes 98312 | tf_op jit(solution)/shard_map/ppermute | solution.py:44
  (54 other events, 481.0 us)

commit v2 on v0

v2 whole, which is shorter than its diff:
```python
import functools

import jax
import jax.numpy as jnp
from jax import lax
from jax.experimental import pallas as pl
from jax.experimental.pallas import tpu as pltpu
from jax.sharding import PartitionSpec as P

LAT = 512
EPSILON = 1e-06
SCORE_SCALE = 192.0 ** (-0.5)
BF16 = jnp.bfloat16
F32 = jnp.float32
EXTRA = 128
PROJECT_BYTES = 12 * 1024 * 1024
EXPERT_BYTES = 16 * 1024 * 1024
PAYLOAD_BYTES = 4 * 1024 * 1024


def attend_kernel(lengths, q_ref, cache_ref, out_ref, *, rows, latent):
    positions = lax.broadcasted_iota(jnp.int32, (1, cache_ref.shape[2]), 1)
    scores = [
        jnp.dot(q_ref[row], cache_ref[row], preferred_element_type=F32) * SCORE_SCALE
        for row in range(rows)
    ]
    weights = []
    for row in range(rows):
        live = positions < lengths[pl.program_id(0) * rows + row]
        score = jnp.where(live, scores[row], -jnp.inf)
        weight = jnp.exp(score - jnp.max(score, -1, keepdims=True))
        weights.append((weight / jnp.sum(weight, -1, keepdims=True)).astype(BF16))
    for row in range(rows):
        mixed = lax.dot_general(
            weights[row],
            cache_ref[row, :latent],
            (((1,), (1,)), ((), ())),
            preferred_element_type=F32,
        )
        out_ref[row] = mixed.astype(BF16)


def attend(queries, kv_cache, lengths):
    count, heads, depth = queries.shape
    context = kv_cache.shape[1]
    cache = jnp.swapaxes(kv_cache, 1, 2)
    rows = 4
    return pl.pallas_call(
        functools.partial(attend_kernel, rows=rows, latent=LAT),
        grid=(count // rows,),
        in_specs=[
            pl.BlockSpec(memory_space=pltpu.SMEM),
            pl.BlockSpec((rows, heads, depth), lambda i: (i, 0, 0)),
            pl.BlockSpec((rows, depth, context), lambda i: (i, 0, 0)),
        ],
        out_specs=pl.BlockSpec((rows, heads, LAT), lambda i: (i, 0, 0)),
        out_shape=jax.ShapeDtypeStruct((count, heads, LAT), BF16),
        compiler_params=pltpu.CompilerParams(vmem_limit_bytes=57 * 1024 * 1024),
    )(lengths, queries, cache)


class Net:
    def __init__(self, dp, heads):
        self.dp, self.heads = dp, heads
        self.near = 2
        self.line = dp // 4
        self.plane = [(jh, jx) for jh in range(heads) for jx in range(self.near)]

    def move(self, value, dp_mask, heads_mask=0):
        mask = dp_mask * self.heads + heads_mask
        count = self.dp * self.heads
        return lax.ppermute(value, ("dp", "heads"), [(i, i ^ mask) for i in range(count)])

    def core(self, value):
        return self.move(value, 1)

    def in_plane(self, value, at):
        jh, jx = self.plane[at]
        return self.move(value, 2 * jx, jh)

    def in_line(self, value, jz):
        return self.move(value, 4 * jz)


def values_kernel(order, latent_ref, map_ref, out_ref, x_scr):
    sources, heads, rows, _ = latent_ref.shape
    wide = map_ref.shape[-1]
    for head in range(heads):
        for slot in range(sources):
            x_scr[slot * rows : (slot + 1) * rows, :] = latent_ref[order[slot], head]
        out = jnp.dot(x_scr[...], map_ref[head], preferred_element_type=F32)
        out_ref[:, head * wide : (head + 1) * wide] = out.astype(BF16)


def values_of(latents, maps, order):
    sources, heads, rows, latent = latents.shape
    vmem = pl.BlockSpec(memory_space=pltpu.VMEM)
    return pl.pallas_call(
        values_kernel,
        in_specs=[pl.BlockSpec(memory_space=pltpu.SMEM), vmem, vmem],
        out_specs=vmem,
        out_shape=jax.ShapeDtypeStruct((sources * rows, heads * maps.shape[-1]), BF16),
        scratch_shapes=[pltpu.VMEM((sources * rows, latent), BF16)],
        compiler_params=pltpu.CompilerParams(vmem_limit_bytes=16 * 1024 * 1024),
    )(order, latents, maps)


def put(out, keep_ref, send_ref, head, lanes):
    half = out.shape[0] // 2
    keep_ref[head, :, lanes] = out[:half].astype(BF16)
    send_ref[head, :, lanes] = out[half:].astype(BF16)


def column_lanes(cols, h, tile, first, t, slice_width):
    return pl.ds(pl.multiple_of(cols[h] * slice_width + (first + t) * tile, 128), tile)


def project_kernel(cols, *refs, tile, first, count, scaled):
    if scaled:
        x_ref, scale_ref, *refs = refs
    else:
        x_ref, *refs = refs
    w_ref, keep_ref, send_ref = refs
    heads = keep_ref.shape[0]
    slice_width = w_ref.shape[1] // heads
    for h in range(heads):
        for t in range(count):
            lanes = column_lanes(cols, h, tile, first, t, slice_width)
            out = jnp.dot(x_ref[...], w_ref[:, lanes], preferred_element_type=F32)
            if scaled:
                out = out * scale_ref[:, :1]
            put(out, keep_ref, send_ref, h, slice(t * tile, (t + 1) * tile))


def project(x, weights, cols, scale, tile, first, count):
    rows, depth = x.shape
    heads = cols.shape[0]
    out = jax.ShapeDtypeStruct((heads, rows // 2, count * tile), BF16)
    given = [x] if scale is None else [x, scale]
    vmem = pl.BlockSpec(memory_space=pltpu.VMEM)
    smem = pl.BlockSpec(memory_space=pltpu.SMEM)
    return pl.pallas_call(
        functools.partial(
            project_kernel, tile=tile, first=first, count=count, scaled=scale is not None
        ),
        in_specs=[smem] + [vmem] * (len(given) + 1),
        out_specs=[vmem, vmem],
        out_shape=[out, out],
        compiler_params=pltpu.CompilerParams(vmem_limit_bytes=PROJECT_BYTES),
        cost_estimate=pl.CostEstimate(
            flops=2 * rows * depth * count * tile * heads,
            bytes_accessed=2 * (depth + rows) * count * tile * heads,
            transcendentals=0,
        ),
    )(cols, *given, weights)


def pieces_of(value):
    high = lax.reduce_precision(value, 8, 7)
    rest = value - high
    middle = lax.reduce_precision(rest, 8, 7)
    return [high.astype(BF16), middle.astype(BF16), (rest - middle).astype(BF16)]


def row_parts(pieces, jh, net, by_line, rows_dev, lanes):
    parts = []
    for jc in range(2):
        for jx in range(net.near):
            at = jh * net.near + jx
            if by_line:
                for jz in range(net.line):
                    ref = pieces[jc][jz]
                    parts.append(ref[at * rows_dev : (at + 1) * rows_dev, lanes])
            else:
                parts.append(pieces[jc][at][:, lanes])
    return jnp.concatenate(parts, 0)


def expert_kernel(cols, me, *refs, net, groups, rows_dev, tile, counts, width):
    pieces = []
    for per_core in groups:
        pieces.append([refs[:per_core], refs[per_core : 2 * per_core]])
        refs = refs[2 * per_core :]
    gate_ref, up_ref, down_ref, hidden_ref, coef_ref, keep_ref, send_ref, gate_acc, up_acc = refs
    heads = net.heads
    slice_width = width // heads
    plan = [
        (group, jh, t, (0 if group == 0 else counts[0]) + t)
        for group in (1, 0)
        for jh in range(heads)
        for t in range(counts[group])
    ]
    for at, (group, jh, t, in_slice) in enumerate(plan):
        x = row_parts(pieces[group], jh, net, group == 1, rows_dev, slice(t * tile, (t + 1) * tile))
        row = pl.ds(pl.multiple_of(cols[jh] * slice_width + in_slice * tile, 128), tile)
        gate = jnp.dot(x, gate_ref[row, :], preferred_element_type=F32)
        up = jnp.dot(x, up_ref[row, :], preferred_element_type=F32)
        if at == 0:
            gate_acc[...] = gate
            up_acc[...] = up
        else:
            gate_acc[...] += gate
            up_acc[...] += up

    lane = lax.broadcasted_iota(jnp.int32, (1, EXTRA), 1)
    squares = 0.0
    for group in range(2):
        lanes = slice(counts[group] * tile, counts[group] * tile + EXTRA)
        for jh in range(heads):
            extra = row_parts(pieces[group], jh, net, group == 1, rows_dev, lanes).astype(F32)
            squares = squares + extra
    squares = jnp.sum(jnp.where(lane < 3, squares, 0.0), -1, keepdims=True)
    norm = lax.rsqrt(squares / width + EPSILON)
    mine = (lane == 3 + me[0]) | (lane == 3 + net.dp + me[0]) | (lane == 3 + 2 * net.dp + me[0])
    coef = jnp.sum(jnp.where(mine, extra, 0.0), -1, keepdims=True)
    coef_ref[...] = jnp.broadcast_to(coef, coef_ref.shape)
    gate = gate_acc[...] * norm
    up = up_acc[...] * norm
    hidden_ref[...] = (gate / (1.0 + jnp.exp(-gate)) * up).astype(BF16)
    for h in range(heads):
        for t in range(counts[0]):
            lanes = column_lanes(cols, h, tile, 0, t, slice_width)
            out = jnp.dot(hidden_ref[...], down_ref[:, lanes], preferred_element_type=F32) * coef
            put(out, keep_ref, send_ref, h, slice(t * tile, (t + 1) * tile))


def experts_of(net, pieces_a, pieces_b, gate_w, up_w, down_w, cols, me, tile, counts, rows_dev):
    flat = [piece for pieces in (pieces_a, pieces_b) for group in pieces for piece in group]
    width, hidden = gate_w.shape
    rows = net.dp * rows_dev
    heads = net.heads
    vmem = pl.BlockSpec(memory_space=pltpu.VMEM)
    smem = pl.BlockSpec(memory_space=pltpu.SMEM)
    out = jax.ShapeDtypeStruct((heads, rows // 2, counts[0] * tile), BF16)
    return pl.pallas_call(
        functools.partial(
            expert_kernel,
            net=net,
            groups=(len(pieces_a[0]), len(pieces_b[0])),
            rows_dev=rows_dev,
            tile=tile,
            counts=counts,
            width=width,
        ),
        in_specs=[smem, smem] + [vmem] * (len(flat) + 3),
        out_specs=[vmem] * 4,
        out_shape=[
            jax.ShapeDtypeStruct((rows, hidden), BF16),
            jax.ShapeDtypeStruct((rows, EXTRA), F32),
            out,
            out,
        ],
        scratch_shapes=[
            pltpu.VMEM((rows, hidden), F32),
            pltpu.VMEM((rows, hidden), F32),
        ],
        compiler_params=pltpu.CompilerParams(vmem_limit_bytes=EXPERT_BYTES),
        cost_estimate=pl.CostEstimate(
            flops=6 * rows * width * hidden,
            bytes_accessed=6 * width * hidden,
            transcendentals=0,
        ),
    )(cols, me, *flat, gate_w, up_w, down_w)


def payload_kernel(*refs, arrived, width):
    own, rest = refs[:2], refs[2:]
    received, rest = [rest[: arrived[0]], rest[arrived[0] : sum(arrived)]], rest[sum(arrived) :]
    resid_ref, gain_ref, extra_ref = rest[:3]
    mids, rows = rest[3:5], rest[5:7]
    lane = lax.broadcasted_iota(jnp.int32, (1, EXTRA), 1)
    start = 0
    for which in range(2):
        total = own[which][...]
        for ref in received[which]:
            total = total + ref[...].astype(F32)
        size = total.shape[-1]
        mid = resid_ref[:, start : start + size].astype(F32) + total
        mids[which][...] = mid
        rows[which][:, :size] = (mid * gain_ref[:, start : start + size].astype(F32)).astype(BF16)
        squares = jnp.sum(mid * mid, -1, keepdims=True)
        high = squares.astype(BF16)
        left = squares - high.astype(F32)
        middle = left.astype(BF16)
        low = (left - middle.astype(F32)).astype(BF16)
        extra = extra_ref[...]
        for at, part in enumerate((high, middle, low)):
            extra = jnp.where(lane == at, jnp.broadcast_to(part, extra.shape), extra)
        rows[which][:, size:] = extra
        start += size


def payloads(parts_a, parts_b, resid, gain, extra):
    own_a, in_a = parts_a
    own_b, in_b = parts_b
    rows = own_a.shape[0]
    mids = [jax.ShapeDtypeStruct(own.shape, F32) for own in (own_a, own_b)]
    outs = [jax.ShapeDtypeStruct((rows, own.shape[1] + EXTRA), BF16) for own in (own_a, own_b)]
    operands = [own_a, own_b, *in_a, *in_b, resid, gain, extra]
    vmem = pl.BlockSpec(memory_space=pltpu.VMEM)
    return pl.pallas_call(
        functools.partial(
            payload_kernel, arrived=(len(in_a), len(in_b)), width=resid.shape[1]
        ),
        in_specs=[vmem] * len(operands),
        out_specs=[vmem] * 4,
        out_shape=mids + outs,
        compiler_params=pltpu.CompilerParams(vmem_limit_bytes=PAYLOAD_BYTES),
    )(*operands)


def summed_with(own, arrived):
    for value in arrived:
        own = own + value.astype(F32)
    return own


def reduce_both(net, first, second, rows_dev):
    places, line = len(net.plane), net.line
    (keep_a, send_a), (keep_b, send_b) = first, second
    other_a, other_b = net.core(send_a), net.core(send_b)
    shape_a = (places, line * rows_dev, keep_a.shape[-1])
    shape_b = (places, line, rows_dev, keep_b.shape[-1])
    keep_a, other_a = keep_a.reshape(shape_a), other_a.reshape(shape_a)
    keep_b, other_b = keep_b.reshape(shape_b), other_b.reshape(shape_b)
    sum_a = [keep_a[at].astype(F32) + other_a[at].astype(F32) for at in range(places)]
    sum_b = [keep_b[:, jz].astype(F32) + other_b[:, jz].astype(F32) for jz in range(line)]
    go_a = [value.astype(BF16) for value in sum_a[1:]]
    go_b = [value.astype(BF16) for value in sum_b[1:]]
    go_a, go_b = lax.optimization_barrier((go_a, go_b))
    in_b = [net.in_line(value, jz + 1) for jz, value in enumerate(go_b)]
    in_a = [net.in_plane(value, at + 1) for at, value in enumerate(go_a)]
    sum_a = summed_with(sum_a[0], in_a).reshape(line, rows_dev, keep_a.shape[-1])
    sum_b = summed_with(sum_b[0], in_b)
    go_a = [sum_a[jz].astype(BF16) for jz in range(1, line)]
    go_b = [sum_b[at].astype(BF16) for at in range(1, places)]
    go_a, go_b = lax.optimization_barrier((go_a, go_b))
    in_b = [net.in_plane(value, at + 1) for at, value in enumerate(go_b)]
    in_a = [net.in_line(value, jz + 1) for jz, value in enumerate(go_a)]
    return (sum_a[0], in_a), (sum_b[0], in_b)


def gather_both(net, row_a, row_b):
    places, line = len(net.plane), net.line
    row_a, row_b = lax.optimization_barrier((row_a, row_b))
    in_b = [net.in_plane(row_b, at) for at in range(1, places)]
    in_a = [net.in_line(row_a, jz) for jz in range(1, line)]
    held_a = jnp.concatenate([row_a] + in_a, 0)
    held_b = jnp.concatenate([row_b] + in_b, 0)
    held_a, held_b = lax.optimization_barrier((held_a, held_b))
    own_b = [held_b] + [net.in_line(held_b, jz) for jz in range(1, line)]
    own_a = [held_a] + [net.in_plane(held_a, at) for at in range(1, places)]
    return [own_a, [net.core(piece) for piece in own_a]], [own_b, [net.core(piece) for piece in own_b]]


def on_device(
    queries,
    kv_cache,
    lengths,
    resid,
    w_uv,
    o_proj,
    norm_gain,
    expert_ids,
    route_gates,
    expert_owner,
    gate_w,
    up_w,
    down_w,
):
    dp = lax.axis_size("dp")
    heads = lax.axis_size("heads")
    net = Net(dp, heads)
    rows_dev, width = resid.shape
    slice_width = width // heads
    tile = slice_width // 7
    wide_count, narrow_count = 5, 2
    me = lax.axis_index("dp")
    my_head = lax.axis_index("heads")
    slots = jnp.array(
        [
            jc + 2 * jx + 4 * jz
            for jc in range(2)
            for jx in range(net.near)
            for jz in range(net.line)
        ],
        jnp.int32,
    )
    order = jnp.bitwise_xor(slots, me)
    natural = jnp.arange(dp, dtype=jnp.int32)
    cols = jnp.bitwise_xor(jnp.arange(heads, dtype=jnp.int32), my_head)

    latent_out = attend(queries, kv_cache, lengths)
    gathered = lax.all_to_all(
        jnp.swapaxes(latent_out, 0, 1), "dp", split_axis=0, concat_axis=0, tiled=True
    )
    gathered = gathered.reshape(dp, -1, rows_dev, LAT)
    out_proj = o_proj[0].reshape(-1, width)

    holder = jnp.sum(
        (expert_ids[:, :, None] == jnp.arange(expert_owner.shape[0], dtype=jnp.int32)).astype(jnp.int32)
        * expert_owner,
        -1,
    )
    table = jnp.sum(jnp.where(holder[:, :, None] == natural, route_gates[:, :, None], 0.0), 1)
    table_parts = pieces_of(table)

    resid_slice = lax.dynamic_slice_in_dim(resid, my_head * slice_width, slice_width, 1)
    gain_slice = lax.dynamic_slice_in_dim(norm_gain, my_head * slice_width, slice_width, 0)
    extra = jnp.concatenate([jnp.zeros((rows_dev, 3), BF16), *table_parts], 1)
    extra = jnp.pad(extra, ((0, 0), (0, EXTRA - extra.shape[1])))

    gain_slice = gain_slice.reshape(1, -1)
    mine = me.reshape(1).astype(jnp.int32)
    gathered, resid_slice, gain_slice, extra, order, cols, mine = lax.optimization_barrier(
        (gathered, resid_slice, gain_slice, extra, order, cols, mine)
    )
    values = values_of(gathered, w_uv[0], order)
    keep_a, send_a = project(values, out_proj, cols, None, tile, 0, wide_count)
    keep_b, send_b = project(values, out_proj, cols, None, tile, wide_count, narrow_count)
    parts_a, parts_b = reduce_both(net, (keep_a, send_a), (keep_b, send_b), rows_dev)
    mid_a, mid_b, row_a, row_b = payloads(
        parts_a, parts_b, resid_slice, gain_slice, extra
    )
    pieces_a, pieces_b = gather_both(net, row_a, row_b)

    hidden, coef, keep_a, send_a = experts_of(
        net,
        pieces_a,
        pieces_b,
        gate_w[0],
        up_w[0],
        down_w[0],
        cols,
        mine,
        tile,
        (wide_count, narrow_count),
        rows_dev,
    )
    keep_b, send_b = project(hidden, down_w[0], cols, coef, tile, wide_count, narrow_count)
    moe_a, moe_b = reduce_both(net, (keep_a, send_a), (keep_b, send_b), rows_dev)
    return jnp.concatenate(
        [mid_a + summed_with(*moe_a), mid_b + summed_with(*moe_b)], 1
    ).astype(BF16)


def solution(mesh):
    return jax.shard_map(
        on_device,
        mesh=mesh,
        in_specs=(
            P(("groups", "dp"), "heads", None),
            P(("groups", "dp"), None, None),
            P(("groups", "dp")),
            P(("groups", "dp"), None),
            P("heads", "dp", None, None),
            P("heads", "dp", None, None),
            P(),
            P(("groups", "dp"), None),
            P(("groups", "dp"), None),
            P(),
            P("dp", None, "heads"),
            P("dp", None, "heads"),
            P("dp", "heads", None),
        ),
        out_specs=P(("groups", "dp"), "heads"),
        check_vma=False,
    )
```

time: 504 us -> 172 us (0.34)
  waiting for transfers between devices: 293 us -> 77.6 us
  blocking collectives: 119 us -> 0 us
  starting transfers between devices: 5.49 us -> 64 us
  matrix products: 34.6 us -> 0 us
  local copies, waits for them, and re-layouts: 29.6 us -> 9.34 us
  Pallas kernels: 0 us -> 18 us
  between operations: 13.3 us -> 0.4 us
  other arithmetic: 8.93 us -> 2.73 us
    reduce_scatter x2 -> x0, waiting for transfers between devices: 132 us -> none  [the longest x1 90.9 us: on_device(): lax.psum_scatter(jnp.dot(values, out_proj, preferred_element_type=jnp.flo...]
    all_to_all x2 -> x0, blocking collectives: 119 us -> none  [the longest x1 86.7 us: on_device(): lax.all_to_all(buffer.reshape(owners, capacity, normed.shape[1]), 'dp', s...]
    all_to_all x1, waiting for transfers between devices: 132 us -> 21.9 us  [on_device(): lax.all_to_all(jnp.swapaxes(latent_out, 0, 1), 'dp', split_axis=0, concat...]
    ppermute x0 -> x48, starting transfers between devices: none -> 56.5 us  [move(): lax.ppermute(value, ('dp', 'heads'), [(i, i ^ mask) for i in range(count)])]
    ppermute x0 -> x48, waiting for transfers between devices: none -> 55.7 us  [move(): lax.ppermute(value, ('dp', 'heads'), [(i, i ^ mask) for i in range(count)])]
    dot_general x7 -> x0, matrix products: 34.6 us -> none  [the longest x1 8.19 us: on_device(): jnp.dot(hidden_units, local_down, preferred_element_type=jnp.float32)]
    psum x1 -> x0, waiting for transfers between devices: 28.7 us -> none  [on_device(): attention = lax.psum(attn_part, 'heads')]
    pallas_call x0 -> x7, Pallas kernels: none -> 18 us  [the longest x1 6.32 us: attend(): pl.pallas_call(functools.partial(attend_kernel, rows=rows, latent=LAT), g...]
  transfers between devices with their start and end apart: 4 -> 49, of which waited for: 4 -> 25; matrix products, arithmetic and copies ran while one was open for 0% -> 1% of each run, Pallas kernels for 0% -> 1%
where the time goes in v2:
time: 172 us
  waiting for transfers between devices  77.6 us (45%)
  starting transfers between devices  64 us (37%)
  Pallas kernels  18 us (10%)
  local copies, waits for them, and re-layouts  9.34 us (5%)
  other arithmetic  2.73 us (2%)
    ppermute x48, starting transfers between devices, move(): lax.ppermute(value, ('dp', 'heads'), [(i, i ^ mask) for i in range(count)])  56.5 us
    ppermute x48, waiting for transfers between devices, move(): lax.ppermute(value, ('dp', 'heads'), [(i, i ^ mask) for i in range(count)])  55.7 us
    all_to_all x1, waiting for transfers between devices, on_device(): lax.all_to_all(jnp.swapaxes(latent_out, 0, 1), 'dp', split_axis=0, concat...  21.9 us
    all_to_all x1, starting transfers between devices, on_device(): lax.all_to_all(jnp.swapaxes(latent_out, 0, 1), 'dp', split_axis=0, concat...  7.51 us
    unnamed x28, local copies, waits for them, and re-layouts  6.36 us
    pallas_call x1, Pallas kernels, attend(): pl.pallas_call(functools.partial(attend_kernel, rows=rows, latent=LAT), g...  6.32 us
    pallas_call x1, Pallas kernels, experts_of(): pl.pallas_call(functools.partial(expert_kernel, net=net, groups=(len(piec...  5.95 us
    pallas_call x3, Pallas kernels, project(): pl.pallas_call(functools.partial(project_kernel, tile=tile, first=first,...  4.62 us
  transfers between devices with their start and end apart: 49, of which 25 were waited for; matrix products, arithmetic and copies ran while one was open for 1% of the time, Pallas kernels for 1%

profile of v2, /device:TPU:0, one launch (start us, length us, event | category | flops | bytes accessed | tf_op | source)
XLA Modules:
  0.0 172.1 jit_solution(6564868334091846381)
XLA Ops:
  0.0 6.3 %shard_map.136 = bf16[16,64,512]{2,1,0:T(8,128)(2,1)} custom-call(s32[16]{0:T(128)} %lengths.1, bf16[16,64,576]{2,1,0:T(8,128)(2,1)} %q_ref.1, bf16[16,576,256]{2,1,0:T(8,128)(2,1)} %bitcast.183), custom_call_target="tpu_custom_call" | custom-call | tf_op jit(solution)/shard_map/pallas_call | solution.py:48
  6.3 2.8 %copy.64 = bf16[64,16,512]{2,1,0:T(8,128)(2,1)} copy(bf16[64,16,512]{2,0,1:T(8,128)(2,1)} %bitcast.184) | data formatting | bytes 2097152 | tf_op jit(solution)/shard_map/transpose | solution.py:395
  9.1 7.5 %all-to-all-start = ((bf16[64,16,512]{2,1,0:T(8,128)(2,1)}), bf16[64,16,512]{2,1,0:T(8,128)(2,1)S(1)}, u32[]{:S(2)}, u32[]{:S(2)}) async-start(bf16[64,16,512]{2,1,0:T(8,128)(2,1)} %copy.64), calls=%async_computation | async-start | bytes 2097152 | tf_op jit(solution)/shard_map/all_to_all | solution.py:394
  17.7 21.9 %all-to-all-done = bf16[64,16,512]{2,1,0:T(8,128)(2,1)S(1)} async-done(((bf16[64,16,512]{2,1,0:T(8,128)(2,1)}), bf16[64,16,512]{2,1,0:T(8,128)(2,1)S(1)}, u32[]{:S(2)}, u32[]{:S(2)}) %all-to-all-start) | async-done | bytes 1048608 | tf_op jit(solution)/shard_map/all_to_all | solution.py:394
  40.6 3.1 %copy-done.1 = bf16[1,4,128,7168]{3,2,1,0:T(8,128)(2,1)S(1)} copy-done((bf16[1,4,128,7168]{3,2,1,0:T(8,128)(2,1)S(1)}, bf16[1,4,128,7168]{3,2,1,0:T(8,128)(2,1)}, u32[]{:S(2)}) %copy-start.1) | copy-done | bytes 7340056
  43.7 2.1 %shard_map.138 = (bf16[2,128,2560]{2,1,0:T(8,128)(2,1)S(1)}, bf16[2,128,2560]{2,1,0:T(8,128)(2,1)S(1)}) custom-call(s32[2]{0:T(128)S(1)} %iota_xor_fusion.cols, bf16[256,512]{1,0:T(8,128)(2,1)S(1)} %shard_map.137.refs_0_, bf16[512,7168]{1,0:T(8,128)(2,1)S(1)} %bitcast.163), custom_call_target="tpu_custom_call" | custom-call | flops 1342177280 | bytes 7864320 | tf_op jit(solution)/shard_map/pallas_call | solution.py:142
  47.8 2.0 %collective-permute-done.1 = bf16[2,128,1024]{2,1,0:T(8,128)(2,1)S(1)} collective-permute-done((bf16[2,128,1024]{2,1,0:T(8,128)(2,1)S(1)}, bf16[2,128,1024]{2,1,0:T(8,128)(2,1)S(1)}, u32[]{:S(2)}, u32[]{:S(2)}) %collective-permute-start.1) | collective-permute-done | bytes 524320 | tf_op jit(solution)/shard_map/ppermute | solution.py:72
  50.3 3.5 %collective-permute-start.5 = (bf16[4,16,1024]{2,1,0:T(8,128)(2,1)S(1)}, bf16[4,16,1024]{2,1,0:T(8,128)(2,1)S(1)}, u32[]{:S(2)}, u32[]{:S(2)}) collective-permute-start(bf16[4,16,1024]{2,1,0:T(8,128)(2,1)S(1)} %get-tuple-element.64), channel_id=1, source_target_pairs={{0,8},{1,9},{2,10},{3,11},{4,12},{5,13},{6,14},{7,15},{8,0},{9,1},... | collective-permute-start | bytes 393224 | tf_op jit(solution)/shard_map/ppermute | solution.py:72
  59.8 1.6 collective-permute-start.4
  61.5 5.2 %collective-permute-done.6 = bf16[4,16,1024]{2,1,0:T(8,128)(2,1)S(1)} collective-permute-done((bf16[4,16,1024]{2,1,0:T(8,128)(2,1)S(1)}, bf16[4,16,1024]{2,1,0:T(8,128)(2,1)S(1)}, u32[]{:S(2)}, u32[]{:S(2)}) %collective-permute-start.6) | collective-permute-done | bytes 131104 | tf_op jit(solution)/shard_map/ppermute | solution.py:72
  67.3 5.6 %collective-permute-done.3 = bf16[64,2560]{1,0:T(8,128)(2,1)S(1)} collective-permute-done((bf16[64,2560]{1,0:T(8,128)(2,1)S(1)}, bf16[64,2560]{1,0:T(8,128)(2,1)S(1)}, u32[]{:S(2)}, u32[]{:S(2)}) %collective-permute-start.3) | collective-permute-done | bytes 327712 | tf_op jit(solution)/shard_map/ppermute | solution.py:72
  78.4 2.3 %collective-permute-start.9 = (bf16[16,2560]{1,0:T(8,128)(2,1)S(1)}, bf16[16,2560]{1,0:T(8,128)(2,1)S(1)}, u32[]{:S(2)}, u32[]{:S(2)}) collective-permute-start(bf16[16,2560]{1,0:T(8,128)(2,1)S(1)} %get-tuple-element.68), channel_id=1, source_target_pairs={{0,16},{1,17},{2,18},{3,19},{4,20},{5,21},{6,22},{7,23},{8,24},{9,... | collective-permute-start | bytes 245768 | tf_op jit(solution)/shard_map/ppermute | solution.py:72
  82.0 3.1 %collective-permute-done.9.refs_3_ = bf16[16,2560]{1,0:T(8,128)(2,1)S(1)} collective-permute-done((bf16[16,2560]{1,0:T(8,128)(2,1)S(1)}, bf16[16,2560]{1,0:T(8,128)(2,1)S(1)}, u32[]{:S(2)}, u32[]{:S(2)}) %collective-permute-start.9) | collective-permute-done | bytes 81952 | tf_op jit(solution)/shard_map/ppermute | solution.py:72
  85.2 1.8 %collective-permute-done.10.refs_4_ = bf16[16,2560]{1,0:T(8,128)(2,1)S(1)} collective-permute-done((bf16[16,2560]{1,0:T(8,128)(2,1)S(1)}, bf16[16,2560]{1,0:T(8,128)(2,1)S(1)}, u32[]{:S(2)}, u32[]{:S(2)}) %collective-permute-start.10) | collective-permute-done | bytes 81952 | tf_op jit(solution)/shard_map/ppermute | solution.py:72
  87.1 1.7 collective-permute-start.19
  92.0 3.0 %collective-permute-start.14 = (bf16[16,2688]{1,0:T(8,128)(2,1)S(1)}, bf16[16,2688]{1,0:T(8,128)(2,1)S(1)}, u32[]{:S(2)}, u32[]{:S(2)}) collective-permute-start(bf16[16,2688]{1,0:T(8,128)(2,1)S(1)} %get-tuple-element.80), channel_id=1, source_target_pairs={{0,8},{1,9},{2,10},{3,11},{4,12},{5,13},{6,14},{7,15},{8,0},{9,1},... | collective-permute-start | bytes 258056 | tf_op jit(solution)/shard_map/ppermute | solution.py:72
  95.0 2.0 %collective-permute-done.16 = bf16[16,2688]{1,0:T(8,128)(2,1)S(1)} collective-permute-done((bf16[16,2688]{1,0:T(8,128)(2,1)S(1)}, bf16[16,2688]{1,0:T(8,128)(2,1)S(1)}, u32[]{:S(2)}, u32[]{:S(2)}) %collective-permute-start.16) | collective-permute-done | bytes 86048 | tf_op jit(solution)/shard_map/ppermute | solution.py:72
  97.0 1.8 %collective-permute-done.15 = bf16[16,2688]{1,0:T(8,128)(2,1)S(1)} collective-permute-done((bf16[16,2688]{1,0:T(8,128)(2,1)S(1)}, bf16[16,2688]{1,0:T(8,128)(2,1)S(1)}, u32[]{:S(2)}, u32[]{:S(2)}) %collective-permute-start.15) | collective-permute-done | bytes 86048 | tf_op jit(solution)/shard_map/ppermute | solution.py:72
  98.9 1.7 collective-permute-start.22
  104.6 6.4 %collective-permute-done.29.refs_11_ = bf16[64,1152]{1,0:T(8,128)(2,1)S(1)} collective-permute-done((bf16[64,1152]{1,0:T(8,128)(2,1)S(1)}, bf16[64,1152]{1,0:T(8,128)(2,1)S(1)}, u32[]{:S(2)}, u32[]{:S(2)}) %collective-permute-start.29) | collective-permute-done | bytes 147488 | tf_op jit(solution)/shard_map/ppermute | solution.py:72
  111.1 5.2 %collective-permute-start.27 = (bf16[64,1152]{1,0:T(8,128)(2,1)S(1)}, bf16[64,1152]{1,0:T(8,128)(2,1)S(1)}, u32[]{:S(2)}, u32[]{:S(2)}) collective-permute-start(bf16[64,1152]{1,0:T(8,128)(2,1)S(1)} %pad_maximum_fusion.1.refs_8_), channel_id=1, source_target_pairs={{0,8},{1,9},{2,10},{3,11},{4,12},{5,13},{6,14},{7,15},{8,0},{9,1},... | collective-permute-start | bytes 442376 | tf_op jit(solution)/shard_map/ppermute | solution.py:72
  117.6 2.4 %collective-permute-done.27.refs_9_ = bf16[64,1152]{1,0:T(8,128)(2,1)S(1)} collective-permute-done((bf16[64,1152]{1,0:T(8,128)(2,1)S(1)}, bf16[64,1152]{1,0:T(8,128)(2,1)S(1)}, u32[]{:S(2)}, u32[]{:S(2)}) %collective-permute-start.27) | collective-permute-done | bytes 147488 | tf_op jit(solution)/shard_map/ppermute | solution.py:72
  121.1 2.2 %collective-permute-done.32.refs_14_ = bf16[64,1152]{1,0:T(8,128)(2,1)S(1)} collective-permute-done((bf16[64,1152]{1,0:T(8,128)(2,1)S(1)}, bf16[64,1152]{1,0:T(8,128)(2,1)S(1)}, u32[]{:S(2)}, u32[]{:S(2)}) %collective-permute-start.32) | collective-permute-done | bytes 147488 | tf_op jit(solution)/shard_map/ppermute | solution.py:72
  124.8 3.1 %copy-done.2 = bf16[1,7168,512]{2,1,0:T(8,128)(2,1)S(1)} copy-done((bf16[1,7168,512]{2,1,0:T(8,128)(2,1)S(1)}, bf16[1,7168,512]{2,1,0:T(8,128)(2,1)}, u32[]{:S(2)}) %copy-start.2) | copy-done | bytes 7340056
  127.8 6.0 %shard_map.141 = (bf16[256,512]{1,0:T(8,128)(2,1)S(1)}, f32[256,128]{1,0:T(8,128)S(1)}, bf16[2,128,2560]{2,1,0:T(8,128)(2,1)S(1)}, bf16[2,128,2560]{2,1,0:T(8,128)(2,1)S(1)}) custom-call(s32[2]{0:T(128)S(1)} %iota_xor_fusion.cols, s32[1]{0:T(128)} %bitcast.3.me, bf16[64,2688]{1,0:T(8,128)(2,1)S(1)} %pad_maximum_fusion.refs_0_, ...), custom_call_target="tpu_custom_call" | custom-call | flops 5637144576 | bytes 22020096 | tf_op jit(solution)/shard_map/pallas_call | solution.py:235
  135.7 1.9 %collective-permute-done.35 = bf16[2,128,1024]{2,1,0:T(8,128)(2,1)S(1)} collective-permute-done((bf16[2,128,1024]{2,1,0:T(8,128)(2,1)S(1)}, bf16[2,128,1024]{2,1,0:T(8,128)(2,1)S(1)}, u32[]{:S(2)}, u32[]{:S(2)}) %collective-permute-start.35) | collective-permute-done | bytes 524320 | tf_op jit(solution)/shard_map/ppermute | solution.py:72
  140.0 2.5 %collective-permute-start.41 = (bf16[4,16,1024]{2,1,0:T(8,128)(2,1)S(1)}, bf16[4,16,1024]{2,1,0:T(8,128)(2,1)S(1)}, u32[]{:S(2)}, u32[]{:S(2)}) collective-permute-start(bf16[4,16,1024]{2,1,0:T(8,128)(2,1)S(1)} %get-tuple-element.95), channel_id=1, source_target_pairs={{0,24},{1,25},{2,26},{3,27},{4,28},{5,29},{6,30},{7,31},{8,16},{9,... | collective-permute-start | bytes 393224 | tf_op jit(solution)/shard_map/ppermute | solution.py:72
  145.1 1.8 %collective-permute-start.38 = (bf16[64,2560]{1,0:T(8,128)(2,1)S(1)}, bf16[64,2560]{1,0:T(8,128)(2,1)S(1)}, u32[]{:S(2)}, u32[]{:S(2)}) collective-permute-start(bf16[64,2560]{1,0:T(8,128)(2,1)S(1)} %get-tuple-element.92), channel_id=1, source_target_pairs={{0,5},{1,4},{2,7},{3,6},{4,1},{5,0},{6,3},{7,2},{8,13},{9,12},{10,... | collective-permute-start | bytes 983048 | tf_op jit(solution)/shard_map/ppermute | solution.py:72
  146.8 5.4 %collective-permute-done.40 = bf16[4,16,1024]{2,1,0:T(8,128)(2,1)S(1)} collective-permute-done((bf16[4,16,1024]{2,1,0:T(8,128)(2,1)S(1)}, bf16[4,16,1024]{2,1,0:T(8,128)(2,1)S(1)}, u32[]{:S(2)}, u32[]{:S(2)}) %collective-permute-start.40) | collective-permute-done | bytes 131104 | tf_op jit(solution)/shard_map/ppermute | solution.py:72
  153.1 4.8 %collective-permute-done.37 = bf16[64,2560]{1,0:T(8,128)(2,1)S(1)} collective-permute-done((bf16[64,2560]{1,0:T(8,128)(2,1)S(1)}, bf16[64,2560]{1,0:T(8,128)(2,1)S(1)}, u32[]{:S(2)}, u32[]{:S(2)}) %collective-permute-start.37) | collective-permute-done | bytes 327712 | tf_op jit(solution)/shard_map/ppermute | solution.py:72
  165.1 2.5 %collective-permute-start.44 = (bf16[16,2560]{1,0:T(8,128)(2,1)S(1)}, bf16[16,2560]{1,0:T(8,128)(2,1)S(1)}, u32[]{:S(2)}, u32[]{:S(2)}) collective-permute-start(bf16[16,2560]{1,0:T(8,128)(2,1)S(1)} %get-tuple-element.98), channel_id=1, source_target_pairs={{0,24},{1,25},{2,26},{3,27},{4,28},{5,29},{6,30},{7,31},{8,16},{9,... | collective-permute-start | bytes 245768 | tf_op jit(solution)/shard_map/ppermute | solution.py:72
  169.2 2.2 %collective-permute-done.44 = bf16[16,2560]{1,0:T(8,128)(2,1)S(1)} collective-permute-done((bf16[16,2560]{1,0:T(8,128)(2,1)S(1)}, bf16[16,2560]{1,0:T(8,128)(2,1)S(1)}, u32[]{:S(2)}, u32[]{:S(2)}) %collective-permute-start.44) | collective-permute-done | bytes 81952 | tf_op jit(solution)/shard_map/ppermute | solution.py:72
  (135 shorter events, 46.5 us)
Async XLA Ops:
  9.1 30.5 %all-to-all-start = ((bf16[64,16,512]{2,1,0:T(8,128)(2,1)}), bf16[64,16,512]{2,1,0:T(8,128)(2,1)S(1)}, u32[]{:S(2)}, u32[]{:S(2)}) async-start(bf16[64,16,512]{2,1,0:T(8,128)(2,1)} %copy.64), calls=%async_computation | async-start | bytes 2097152 | tf_op jit(solution)/shard_map/all_to_all | solution.py:394
  50.3 9.6 %collective-permute-start.5 = (bf16[4,16,1024]{2,1,0:T(8,128)(2,1)S(1)}, bf16[4,16,1024]{2,1,0:T(8,128)(2,1)S(1)}, u32[]{:S(2)}, u32[]{:S(2)}) collective-permute-start(bf16[4,16,1024]{2,1,0:T(8,128)(2,1)S(1)} %get-tuple-element.64), channel_id=1, source_target_pairs={{0,8},{1,9},{2,10},{3,11},{4,12},{5,13},{6,14},{7,15},{8,0},{9,1},... | collective-permute-start | bytes 393224 | tf_op jit(solution)/shard_map/ppermute | solution.py:72
  53.7 12.9 %collective-permute-start.6 = (bf16[4,16,1024]{2,1,0:T(8,128)(2,1)S(1)}, bf16[4,16,1024]{2,1,0:T(8,128)(2,1)S(1)}, u32[]{:S(2)}, u32[]{:S(2)}) collective-permute-start(bf16[4,16,1024]{2,1,0:T(8,128)(2,1)S(1)} %get-tuple-element.65), channel_id=1, source_target_pairs={{0,16},{1,17},{2,18},{3,19},{4,20},{5,21},{6,22},{7,23},{8,24},{9,... | collective-permute-start | bytes 393224 | tf_op jit(solution)/shard_map/ppermute | solution.py:72
  55.2 11.4 %collective-permute-start.7 = (bf16[4,16,1024]{2,1,0:T(8,128)(2,1)S(1)}, bf16[4,16,1024]{2,1,0:T(8,128)(2,1)S(1)}, u32[]{:S(2)}, u32[]{:S(2)}) collective-permute-start(bf16[4,16,1024]{2,1,0:T(8,128)(2,1)S(1)} %get-tuple-element.66), channel_id=1, source_target_pairs={{0,24},{1,25},{2,26},{3,27},{4,28},{5,29},{6,30},{7,31},{8,16},{9,... | collective-permute-start | bytes 393224 | tf_op jit(solution)/shard_map/ppermute | solution.py:72
  56.6 10.6 %collective-permute-start.2 = (bf16[64,2560]{1,0:T(8,128)(2,1)S(1)}, bf16[64,2560]{1,0:T(8,128)(2,1)S(1)}, u32[]{:S(2)}, u32[]{:S(2)}) collective-permute-start(bf16[64,2560]{1,0:T(8,128)(2,1)S(1)} %get-tuple-element.61), channel_id=1, source_target_pairs={{0,4},{1,5},{2,6},{3,7},{4,0},{5,1},{6,2},{7,3},{8,12},{9,13},{10,... | collective-permute-start | bytes 983048 | tf_op jit(solution)/shard_map/ppermute | solution.py:72
  57.7 15.1 %collective-permute-start.3 = (bf16[64,2560]{1,0:T(8,128)(2,1)S(1)}, bf16[64,2560]{1,0:T(8,128)(2,1)S(1)}, u32[]{:S(2)}, u32[]{:S(2)}) collective-permute-start(bf16[64,2560]{1,0:T(8,128)(2,1)S(1)} %get-tuple-element.62), channel_id=1, source_target_pairs={{0,1},{1,0},{2,3},{3,2},{4,5},{5,4},{6,7},{7,6},{8,9},{9,8},{10,11... | collective-permute-start | bytes 983048 | tf_op jit(solution)/shard_map/ppermute | solution.py:72
  59.8 14.0 %collective-permute-start.4 = (bf16[64,2560]{1,0:T(8,128)(2,1)S(1)}, bf16[64,2560]{1,0:T(8,128)(2,1)S(1)}, u32[]{:S(2)}, u32[]{:S(2)}) collective-permute-start(bf16[64,2560]{1,0:T(8,128)(2,1)S(1)} %get-tuple-element.63), channel_id=1, source_target_pairs={{0,5},{1,4},{2,7},{3,6},{4,1},{5,0},{6,3},{7,2},{8,13},{9,12},{10,... | collective-permute-start | bytes 983048 | tf_op jit(solution)/shard_map/ppermute | solution.py:72
  74.0 6.7 %collective-permute-start.11 = (bf16[16,1024]{1,0:T(8,128)(2,1)S(1)}, bf16[16,1024]{1,0:T(8,128)(2,1)S(1)}, u32[]{:S(2)}, u32[]{:S(2)}) collective-permute-start(bf16[16,1024]{1,0:T(8,128)(2,1)S(1)} %get-tuple-element.70), channel_id=1, source_target_pairs={{0,4},{1,5},{2,6},{3,7},{4,0},{5,1},{6,2},{7,3},{8,12},{9,13},{10,... | collective-permute-start | bytes 98312 | tf_op jit(solution)/shard_map/ppermute | solution.py:72
  75.3 6.7 %collective-permute-start.12 = (bf16[16,1024]{1,0:T(8,128)(2,1)S(1)}, bf16[16,1024]{1,0:T(8,128)(2,1)S(1)}, u32[]{:S(2)}, u32[]{:S(2)}) collective-permute-start(bf16[16,1024]{1,0:T(8,128)(2,1)S(1)} %get-tuple-element.71), channel_id=1, source_target_pairs={{0,1},{1,0},{2,3},{3,2},{4,5},{5,4},{6,7},{7,6},{8,9},{9,8},{10,11... | collective-permute-start | bytes 98312 | tf_op jit(solution)/shard_map/ppermute | solution.py:72
  76.4 5.6 %collective-permute-start.13 = (bf16[16,1024]{1,0:T(8,128)(2,1)S(1)}, bf16[16,1024]{1,0:T(8,128)(2,1)S(1)}, u32[]{:S(2)}, u32[]{:S(2)}) collective-permute-start(bf16[16,1024]{1,0:T(8,128)(2,1)S(1)} %get-tuple-element.72), channel_id=1, source_target_pairs={{0,5},{1,4},{2,7},{3,6},{4,1},{5,0},{6,3},{7,2},{8,13},{9,12},{10,... | collective-permute-start | bytes 98312 | tf_op jit(solution)/shard_map/ppermute | solution.py:72
  78.4 6.8 %collective-permute-start.9 = (bf16[16,2560]{1,0:T(8,128)(2,1)S(1)}, bf16[16,2560]{1,0:T(8,128)(2,1)S(1)}, u32[]{:S(2)}, u32[]{:S(2)}) collective-permute-start(bf16[16,2560]{1,0:T(8,128)(2,1)S(1)} %get-tuple-element.68), channel_id=1, source_target_pairs={{0,16},{1,17},{2,18},{3,19},{4,20},{5,21},{6,22},{7,23},{8,24},{9,... | collective-permute-start | bytes 245768 | tf_op jit(solution)/shard_map/ppermute | solution.py:72
  80.7 6.2 %collective-permute-start.10 = (bf16[16,2560]{1,0:T(8,128)(2,1)S(1)}, bf16[16,2560]{1,0:T(8,128)(2,1)S(1)}, u32[]{:S(2)}, u32[]{:S(2)}) collective-permute-start(bf16[16,2560]{1,0:T(8,128)(2,1)S(1)} %get-tuple-element.69), channel_id=1, source_target_pairs={{0,24},{1,25},{2,26},{3,27},{4,28},{5,29},{6,30},{7,31},{8,16},{9,... | collective-permute-start | bytes 245768 | tf_op jit(solution)/shard_map/ppermute | solution.py:72
  88.8 6.3 %collective-permute-start.18 = (bf16[16,1152]{1,0:T(8,128)(2,1)S(1)}, bf16[16,1152]{1,0:T(8,128)(2,1)S(1)}, u32[]{:S(2)}, u32[]{:S(2)}) collective-permute-start(bf16[16,1152]{1,0:T(8,128)(2,1)S(1)} %get-tuple-element.81), channel_id=1, source_target_pairs={{0,1},{1,0},{2,3},{3,2},{4,5},{5,4},{6,7},{7,6},{8,9},{9,8},{10,11... | collective-permute-start | bytes 110600 | tf_op jit(solution)/shard_map/ppermute | solution.py:72
  90.6 6.4 %collective-permute-start.16 = (bf16[16,2688]{1,0:T(8,128)(2,1)S(1)}, bf16[16,2688]{1,0:T(8,128)(2,1)S(1)}, u32[]{:S(2)}, u32[]{:S(2)}) collective-permute-start(bf16[16,2688]{1,0:T(8,128)(2,1)S(1)} %get-tuple-element.80), channel_id=1, source_target_pairs={{0,24},{1,25},{2,26},{3,27},{4,28},{5,29},{6,30},{7,31},{8,16},{9,... | collective-permute-start | bytes 258056 | tf_op jit(solution)/shard_map/ppermute | solution.py:72
  92.0 6.8 %collective-permute-start.15 = (bf16[16,2688]{1,0:T(8,128)(2,1)S(1)}, bf16[16,2688]{1,0:T(8,128)(2,1)S(1)}, u32[]{:S(2)}, u32[]{:S(2)}) collective-permute-start(bf16[16,2688]{1,0:T(8,128)(2,1)S(1)} %get-tuple-element.80), channel_id=1, source_target_pairs={{0,16},{1,17},{2,18},{3,19},{4,20},{5,21},{6,22},{7,23},{8,24},{9,... | collective-permute-start | bytes 258056 | tf_op jit(solution)/shard_map/ppermute | solution.py:72
  92.0 6.8 %collective-permute-start.14 = (bf16[16,2688]{1,0:T(8,128)(2,1)S(1)}, bf16[16,2688]{1,0:T(8,128)(2,1)S(1)}, u32[]{:S(2)}, u32[]{:S(2)}) collective-permute-start(bf16[16,2688]{1,0:T(8,128)(2,1)S(1)} %get-tuple-element.80), channel_id=1, source_target_pairs={{0,8},{1,9},{2,10},{3,11},{4,12},{5,13},{6,14},{7,15},{8,0},{9,1},... | collective-permute-start | bytes 258056 | tf_op jit(solution)/shard_map/ppermute | solution.py:72
  98.9 21.1 %collective-permute-start.22 = (bf16[64,2688]{1,0:T(8,128)(2,1)S(1)}, bf16[64,2688]{1,0:T(8,128)(2,1)S(1)}, u32[]{:S(2)}, u32[]{:S(2)}) collective-permute-start(bf16[64,2688]{1,0:T(8,128)(2,1)S(1)} %pad_maximum_fusion.refs_0_), channel_id=1, source_target_pairs={{0,5},{1,4},{2,7},{3,6},{4,1},{5,0},{6,3},{7,2},{8,13},{9,12},{10,... | collective-permute-start | bytes 1032200 | tf_op jit(solution)/shard_map/ppermute | solution.py:72
  100.6 19.9 %collective-permute-start.21 = (bf16[64,2688]{1,0:T(8,128)(2,1)S(1)}, bf16[64,2688]{1,0:T(8,128)(2,1)S(1)}, u32[]{:S(2)}, u32[]{:S(2)}) collective-permute-start(bf16[64,2688]{1,0:T(8,128)(2,1)S(1)} %pad_maximum_fusion.refs_0_), channel_id=1, source_target_pairs={{0,1},{1,0},{2,3},{3,2},{4,5},{5,4},{6,7},{7,6},{8,9},{9,8},{10,11... | collective-permute-start | bytes 1032200 | tf_op jit(solution)/shard_map/ppermute | solution.py:72
  101.6 18.9 %collective-permute-start.20 = (bf16[64,2688]{1,0:T(8,128)(2,1)S(1)}, bf16[64,2688]{1,0:T(8,128)(2,1)S(1)}, u32[]{:S(2)}, u32[]{:S(2)}) collective-permute-start(bf16[64,2688]{1,0:T(8,128)(2,1)S(1)} %pad_maximum_fusion.refs_0_), channel_id=1, source_target_pairs={{0,4},{1,5},{2,6},{3,7},{4,0},{5,1},{6,2},{7,3},{8,12},{9,13},{10,... | collective-permute-start | bytes 1032200 | tf_op jit(solution)/shard_map/ppermute | solution.py:72
  102.4 8.6 %collective-permute-start.29 = (bf16[64,1152]{1,0:T(8,128)(2,1)S(1)}, bf16[64,1152]{1,0:T(8,128)(2,1)S(1)}, u32[]{:S(2)}, u32[]{:S(2)}) collective-permute-start(bf16[64,1152]{1,0:T(8,128)(2,1)S(1)} %pad_maximum_fusion.1.refs_8_), channel_id=1, source_target_pairs={{0,24},{1,25},{2,26},{3,27},{4,28},{5,29},{6,30},{7,31},{8,16},{9,... | collective-permute-start | bytes 442376 | tf_op jit(solution)/shard_map/ppermute | solution.py:72
  103.8 13.8 %collective-permute-start.28 = (bf16[64,1152]{1,0:T(8,128)(2,1)S(1)}, bf16[64,1152]{1,0:T(8,128)(2,1)S(1)}, u32[]{:S(2)}, u32[]{:S(2)}) collective-permute-start(bf16[64,1152]{1,0:T(8,128)(2,1)S(1)} %pad_maximum_fusion.1.refs_8_), channel_id=1, source_target_pairs={{0,16},{1,17},{2,18},{3,19},{4,20},{5,21},{6,22},{7,23},{8,24},{9,... | collective-permute-start | bytes 442376 | tf_op jit(solution)/shard_map/ppermute | solution.py:72
  111.1 8.9 %collective-permute-start.27 = (bf16[64,1152]{1,0:T(8,128)(2,1)S(1)}, bf16[64,1152]{1,0:T(8,128)(2,1)S(1)}, u32[]{:S(2)}, u32[]{:S(2)}) collective-permute-start(bf16[64,1152]{1,0:T(8,128)(2,1)S(1)} %pad_maximum_fusion.1.refs_8_), channel_id=1, source_target_pairs={{0,8},{1,9},{2,10},{3,11},{4,12},{5,13},{6,14},{7,15},{8,0},{9,1},... | collective-permute-start | bytes 442376 | tf_op jit(solution)/shard_map/ppermute | solution.py:72
  138.0 7.1 %collective-permute-start.39 = (bf16[4,16,1024]{2,1,0:T(8,128)(2,1)S(1)}, bf16[4,16,1024]{2,1,0:T(8,128)(2,1)S(1)}, u32[]{:S(2)}, u32[]{:S(2)}) collective-permute-start(bf16[4,16,1024]{2,1,0:T(8,128)(2,1)S(1)} %get-tuple-element.93), channel_id=1, source_target_pairs={{0,8},{1,9},{2,10},{3,11},{4,12},{5,13},{6,14},{7,15},{8,0},{9,1},... | collective-permute-start | bytes 393224 | tf_op jit(solution)/shard_map/ppermute | solution.py:72
  139.5 12.7 %collective-permute-start.40 = (bf16[4,16,1024]{2,1,0:T(8,128)(2,1)S(1)}, bf16[4,16,1024]{2,1,0:T(8,128)(2,1)S(1)}, u32[]{:S(2)}, u32[]{:S(2)}) collective-permute-start(bf16[4,16,1024]{2,1,0:T(8,128)(2,1)S(1)} %get-tuple-element.94), channel_id=1, source_target_pairs={{0,16},{1,17},{2,18},{3,19},{4,20},{5,21},{6,22},{7,23},{8,24},{9,... | collective-permute-start | bytes 393224 | tf_op jit(solution)/shard_map/ppermute | solution.py:72
  140.0 12.2 %collective-permute-start.41 = (bf16[4,16,1024]{2,1,0:T(8,128)(2,1)S(1)}, bf16[4,16,1024]{2,1,0:T(8,128)(2,1)S(1)}, u32[]{:S(2)}, u32[]{:S(2)}) collective-permute-start(bf16[4,16,1024]{2,1,0:T(8,128)(2,1)S(1)} %get-tuple-element.95), channel_id=1, source_target_pairs={{0,24},{1,25},{2,26},{3,27},{4,28},{5,29},{6,30},{7,31},{8,16},{9,... | collective-permute-start | bytes 393224 | tf_op jit(solution)/shard_map/ppermute | solution.py:72
  142.5 10.6 %collective-permute-start.36 = (bf16[64,2560]{1,0:T(8,128)(2,1)S(1)}, bf16[64,2560]{1,0:T(8,128)(2,1)S(1)}, u32[]{:S(2)}, u32[]{:S(2)}) collective-permute-start(bf16[64,2560]{1,0:T(8,128)(2,1)S(1)} %get-tuple-element.90), channel_id=1, source_target_pairs={{0,4},{1,5},{2,6},{3,7},{4,0},{5,1},{6,2},{7,3},{8,12},{9,13},{10,... | collective-permute-start | bytes 983048 | tf_op jit(solution)/shard_map/ppermute | solution.py:72
  143.7 14.2 %collective-permute-start.37 = (bf16[64,2560]{1,0:T(8,128)(2,1)S(1)}, bf16[64,2560]{1,0:T(8,128)(2,1)S(1)}, u32[]{:S(2)}, u32[]{:S(2)}) collective-permute-start(bf16[64,2560]{1,0:T(8,128)(2,1)S(1)} %get-tuple-element.91), channel_id=1, source_target_pairs={{0,1},{1,0},{2,3},{3,2},{4,5},{5,4},{6,7},{7,6},{8,9},{9,8},{10,11... | collective-permute-start | bytes 983048 | tf_op jit(solution)/shard_map/ppermute | solution.py:72
  145.1 14.3 %collective-permute-start.38 = (bf16[64,2560]{1,0:T(8,128)(2,1)S(1)}, bf16[64,2560]{1,0:T(8,128)(2,1)S(1)}, u32[]{:S(2)}, u32[]{:S(2)}) collective-permute-start(bf16[64,2560]{1,0:T(8,128)(2,1)S(1)} %get-tuple-element.92), channel_id=1, source_target_pairs={{0,5},{1,4},{2,7},{3,6},{4,1},{5,0},{6,3},{7,2},{8,13},{9,12},{10,... | collective-permute-start | bytes 983048 | tf_op jit(solution)/shard_map/ppermute | solution.py:72
  159.6 5.5 %collective-permute-start.45 = (bf16[16,1024]{1,0:T(8,128)(2,1)S(1)}, bf16[16,1024]{1,0:T(8,128)(2,1)S(1)}, u32[]{:S(2)}, u32[]{:S(2)}) collective-permute-start(bf16[16,1024]{1,0:T(8,128)(2,1)S(1)} %get-tuple-element.100), channel_id=1, source_target_pairs={{0,4},{1,5},{2,6},{3,7},{4,0},{5,1},{6,2},{7,3},{8,12},{9,13},{10,... | collective-permute-start | bytes 98312 | tf_op jit(solution)/shard_map/ppermute | solution.py:72
  160.5 7.1 %collective-permute-start.46 = (bf16[16,1024]{1,0:T(8,128)(2,1)S(1)}, bf16[16,1024]{1,0:T(8,128)(2,1)S(1)}, u32[]{:S(2)}, u32[]{:S(2)}) collective-permute-start(bf16[16,1024]{1,0:T(8,128)(2,1)S(1)} %get-tuple-element.101), channel_id=1, source_target_pairs={{0,1},{1,0},{2,3},{3,2},{4,5},{5,4},{6,7},{7,6},{8,9},{9,8},{10,11... | collective-permute-start | bytes 98312 | tf_op jit(solution)/shard_map/ppermute | solution.py:72
  162.0 5.6 %collective-permute-start.47 = (bf16[16,1024]{1,0:T(8,128)(2,1)S(1)}, bf16[16,1024]{1,0:T(8,128)(2,1)S(1)}, u32[]{:S(2)}, u32[]{:S(2)}) collective-permute-start(bf16[16,1024]{1,0:T(8,128)(2,1)S(1)} %get-tuple-element.102), channel_id=1, source_target_pairs={{0,5},{1,4},{2,7},{3,6},{4,1},{5,0},{6,3},{7,2},{8,13},{9,12},{10,... | collective-permute-start | bytes 98312 | tf_op jit(solution)/shard_map/ppermute | solution.py:72
  165.1 6.3 %collective-permute-start.44 = (bf16[16,2560]{1,0:T(8,128)(2,1)S(1)}, bf16[16,2560]{1,0:T(8,128)(2,1)S(1)}, u32[]{:S(2)}, u32[]{:S(2)}) collective-permute-start(bf16[16,2560]{1,0:T(8,128)(2,1)S(1)} %get-tuple-element.98), channel_id=1, source_target_pairs={{0,24},{1,25},{2,26},{3,27},{4,28},{5,29},{6,30},{7,31},{8,16},{9,... | collective-permute-start | bytes 245768 | tf_op jit(solution)/shard_map/ppermute | solution.py:72
  (30 other events, 474.3 us)

commit v3 on v2

--- a/solution.py
+++ b/solution.py
@@ -18,7 +18,8 @@
 PAYLOAD_BYTES = 4 * 1024 * 1024
 
 
-def attend_kernel(lengths, q_ref, cache_ref, out_ref, *, rows, latent):
+def attend_kernel(lengths, q_ref, cache_ref, out_ref, *scrs, rows, latent):
+    heads = q_ref.shape[1]
     positions = lax.broadcasted_iota(jnp.int32, (1, cache_ref.shape[2]), 1)
     scores = [
         jnp.dot(q_ref[row], cache_ref[row], preferred_element_type=F32) * SCORE_SCALE
@@ -37,7 +38,17 @@
             (((1,), (1,)), ((), ())),
             preferred_element_type=F32,
         )
-        out_ref[row] = mixed.astype(BF16)
+        at = (pl.program_id(0) * rows + row) * heads
+        for part, scr in enumerate(scrs):
+            scr[pl.ds(pl.multiple_of(at, 8), heads), :] = mixed[:, part * 128 : (part + 1) * 128]
+
+    @pl.when(pl.program_id(0) == pl.num_programs(0) - 1)
+    def _():
+        for head in range(heads):
+            for part, scr in enumerate(scrs):
+                out_ref[head, :, part * 128 : (part + 1) * 128] = scr[
+                    pl.ds(head, out_ref.shape[1], stride=heads), :
+                ].astype(BF16)
 
 
 def attend(queries, kv_cache, lengths):
@@ -53,9 +64,10 @@
             pl.BlockSpec((rows, heads, depth), lambda i: (i, 0, 0)),
             pl.BlockSpec((rows, depth, context), lambda i: (i, 0, 0)),
         ],
-        out_specs=pl.BlockSpec((rows, heads, LAT), lambda i: (i, 0, 0)),
-        out_shape=jax.ShapeDtypeStruct((count, heads, LAT), BF16),
-        compiler_params=pltpu.CompilerParams(vmem_limit_bytes=57 * 1024 * 1024),
+        out_specs=pl.BlockSpec(memory_space=pltpu.VMEM),
+        out_shape=jax.ShapeDtypeStruct((heads, count, LAT), BF16),
+        scratch_shapes=[pltpu.VMEM((count * heads, 128), F32)] * (LAT // 128),
+        compiler_params=pltpu.CompilerParams(vmem_limit_bytes=56 * 1024 * 1024),
     )(lengths, queries, cache)
 
 
@@ -65,6 +77,12 @@
         self.near = 2
         self.line = dp // 4
         self.plane = [(jh, jx) for jh in range(heads) for jx in range(self.near)]
+        self.line_bits = self.line.bit_length() - 1
+        self.plane_bits = len(self.plane).bit_length() - 1
+        slots = [0]
+        for bit in reversed(range(1, self.line_bits)):
+            slots = slots + [slot | 1 << bit for slot in slots]
+        self.line_at = {slot | odd: (odd, at) for odd in range(2) for at, slot in enumerate(slots)}
 
     def move(self, value, dp_mask, heads_mask=0):
         mask = dp_mask * self.heads + heads_mask
@@ -169,8 +187,9 @@
             at = jh * net.near + jx
             if by_line:
                 for jz in range(net.line):
-                    ref = pieces[jc][jz]
-                    parts.append(ref[at * rows_dev : (at + 1) * rows_dev, lanes])
+                    piece, index = net.line_at[jz]
+                    start = (index * len(net.plane) + at) * rows_dev
+                    parts.append(pieces[jc][piece][start : start + rows_dev, lanes])
             else:
                 parts.append(pieces[jc][at][:, lanes])
     return jnp.concatenate(parts, 0)
@@ -204,11 +223,10 @@
 
     lane = lax.broadcasted_iota(jnp.int32, (1, EXTRA), 1)
     squares = 0.0
-    for group in range(2):
-        lanes = slice(counts[group] * tile, counts[group] * tile + EXTRA)
-        for jh in range(heads):
-            extra = row_parts(pieces[group], jh, net, group == 1, rows_dev, lanes).astype(F32)
-            squares = squares + extra
+    lanes = slice(counts[1] * tile, counts[1] * tile + EXTRA)
+    for jh in range(heads):
+        extra = row_parts(pieces[1], jh, net, True, rows_dev, lanes).astype(F32)
+        squares = squares + extra
     squares = jnp.sum(jnp.where(lane < 3, squares, 0.0), -1, keepdims=True)
     norm = lax.rsqrt(squares / width + EPSILON)
     mine = (lane == 3 + me[0]) | (lane == 3 + net.dp + me[0]) | (lane == 3 + 2 * net.dp + me[0])
@@ -270,6 +288,7 @@
     mids, rows = rest[3:5], rest[5:7]
     lane = lax.broadcasted_iota(jnp.int32, (1, EXTRA), 1)
     start = 0
+    squares = 0.0
     for which in range(2):
         total = own[which][...]
         for ref in received[which]:
@@ -278,16 +297,16 @@
         mid = resid_ref[:, start : start + size].astype(F32) + total
         mids[which][...] = mid
         rows[which][:, :size] = (mid * gain_ref[:, start : start + size].astype(F32)).astype(BF16)
-        squares = jnp.sum(mid * mid, -1, keepdims=True)
-        high = squares.astype(BF16)
-        left = squares - high.astype(F32)
-        middle = left.astype(BF16)
-        low = (left - middle.astype(F32)).astype(BF16)
-        extra = extra_ref[...]
-        for at, part in enumerate((high, middle, low)):
-            extra = jnp.where(lane == at, jnp.broadcast_to(part, extra.shape), extra)
-        rows[which][:, size:] = extra
+        squares = squares + jnp.sum(mid * mid, -1, keepdims=True)
         start += size
+    high = squares.astype(BF16)
+    left = squares - high.astype(F32)
+    middle = left.astype(BF16)
+    low = (left - middle.astype(F32)).astype(BF16)
+    extra = extra_ref[...]
+    for at, part in enumerate((high, middle, low)):
+        extra = jnp.where(lane == at, jnp.broadcast_to(part, extra.shape), extra)
+    rows[1][:, size:] = extra
 
 
 def payloads(parts_a, parts_b, resid, gain, extra):
@@ -295,7 +314,10 @@
     own_b, in_b = parts_b
     rows = own_a.shape[0]
     mids = [jax.ShapeDtypeStruct(own.shape, F32) for own in (own_a, own_b)]
-    outs = [jax.ShapeDtypeStruct((rows, own.shape[1] + EXTRA), BF16) for own in (own_a, own_b)]
+    outs = [
+        jax.ShapeDtypeStruct((rows, own_a.shape[1]), BF16),
+        jax.ShapeDtypeStruct((rows, own_b.shape[1] + EXTRA), BF16),
+    ]
     operands = [own_a, own_b, *in_a, *in_b, resid, gain, extra]
     vmem = pl.BlockSpec(memory_space=pltpu.VMEM)
     return pl.pallas_call(
@@ -324,32 +346,51 @@
     keep_a, other_a = keep_a.reshape(shape_a), other_a.reshape(shape_a)
     keep_b, other_b = keep_b.reshape(shape_b), other_b.reshape(shape_b)
     sum_a = [keep_a[at].astype(F32) + other_a[at].astype(F32) for at in range(places)]
-    sum_b = [keep_b[:, jz].astype(F32) + other_b[:, jz].astype(F32) for jz in range(line)]
+    sum_b = {jz: keep_b[:, jz].astype(F32) + other_b[:, jz].astype(F32) for jz in range(line)}
     go_a = [value.astype(BF16) for value in sum_a[1:]]
-    go_b = [value.astype(BF16) for value in sum_b[1:]]
+    go_b = [sum_b[jz].astype(BF16) for jz in range(1, line)]
     go_a, go_b = lax.optimization_barrier((go_a, go_b))
     in_b = [net.in_line(value, jz + 1) for jz, value in enumerate(go_b)]
     in_a = [net.in_plane(value, at + 1) for at, value in enumerate(go_a)]
     sum_a = summed_with(sum_a[0], in_a).reshape(line, rows_dev, keep_a.shape[-1])
+    sum_a, in_b = lax.optimization_barrier((sum_a, in_b))
     sum_b = summed_with(sum_b[0], in_b)
     go_a = [sum_a[jz].astype(BF16) for jz in range(1, line)]
-    go_b = [sum_b[at].astype(BF16) for at in range(1, places)]
+    sum_b = {at: sum_b[at] for at in range(places)}
+    go_b, sum_b = split_pairs(sum_b, 0)
     go_a, go_b = lax.optimization_barrier((go_a, go_b))
-    in_b = [net.in_plane(value, at + 1) for at, value in enumerate(go_b)]
+    for bit in range(net.plane_bits):
+        if bit:
+            go_b, sum_b = split_pairs(sum_b, bit)
+        last = net.in_plane(go_b, 1 << bit)
+        if bit < net.plane_bits - 1:
+            sum_b = join_pairs(sum_b, last)
     in_a = [net.in_line(value, jz + 1) for jz, value in enumerate(go_a)]
-    return (sum_a[0], in_a), (sum_b[0], in_b)
+    return (sum_a[0], in_a), (sum_b[0], [last.reshape(rows_dev, -1)])
+
+
+def split_pairs(parts, bit):
+    go = jnp.stack([parts[slot].astype(BF16) for slot in sorted(parts) if slot >> bit & 1])
+    return go, {slot: value for slot, value in parts.items() if not slot >> bit & 1}
+
+
+def join_pairs(parts, arrived):
+    return {slot: parts[slot] + arrived[at].astype(F32) for at, slot in enumerate(sorted(parts))}
 
 
 def gather_both(net, row_a, row_b):
     places, line = len(net.plane), net.line
     row_a, row_b = lax.optimization_barrier((row_a, row_b))
-    in_b = [net.in_plane(row_b, at) for at in range(1, places)]
+    held_b = row_b
+    for bit in range(net.plane_bits):
+        held_b = jnp.concatenate([held_b, net.in_plane(held_b, 1 << bit)], 0)
     in_a = [net.in_line(row_a, jz) for jz in range(1, line)]
     held_a = jnp.concatenate([row_a] + in_a, 0)
-    held_b = jnp.concatenate([row_b] + in_b, 0)
     held_a, held_b = lax.optimization_barrier((held_a, held_b))
-    own_b = [held_b] + [net.in_line(held_b, jz) for jz in range(1, line)]
+    for bit in reversed(range(1, net.line_bits)):
+        held_b = jnp.concatenate([held_b, net.in_line(held_b, 1 << bit)], 0)
     own_a = [held_a] + [net.in_plane(held_a, at) for at in range(1, places)]
+    own_b = [held_b, net.in_line(held_b, 1)]
     return [own_a, [net.core(piece) for piece in own_a]], [own_b, [net.core(piece) for piece in own_b]]
 
 
@@ -373,8 +414,9 @@
     net = Net(dp, heads)
     rows_dev, width = resid.shape
     slice_width = width // heads
-    tile = slice_width // 7
-    wide_count, narrow_count = 5, 2
+    tile, wide_count, narrow_count = slice_width // 14, 10, 4
+    if tile % 128:
+        tile, wide_count, narrow_count = slice_width // 7, 5, 2
     me = lax.axis_index("dp")
     my_head = lax.axis_index("heads")
     slots = jnp.array(
@@ -391,11 +433,9 @@
     cols = jnp.bitwise_xor(jnp.arange(heads, dtype=jnp.int32), my_head)
 
     latent_out = attend(queries, kv_cache, lengths)
-    gathered = lax.all_to_all(
-        jnp.swapaxes(latent_out, 0, 1), "dp", split_axis=0, concat_axis=0, tiled=True
-    )
+    out_proj = o_proj[0].reshape(-1, width)
+    gathered = lax.all_to_all(latent_out, "dp", split_axis=0, concat_axis=0, tiled=True)
     gathered = gathered.reshape(dp, -1, rows_dev, LAT)
-    out_proj = o_proj[0].reshape(-1, width)
 
     holder = jnp.sum(
         (expert_ids[:, :, None] == jnp.arange(expert_owner.shape[0], dtype=jnp.int32)).astype(jnp.int32)

time: 172 us -> 154 us (0.90)
  starting transfers between devices: 64 us -> 56.5 us
  waiting for transfers between devices: 77.6 us -> 70.7 us
  local copies, waits for them, and re-layouts: 9.34 us -> 3.52 us
    ppermute x48 -> x42, starting transfers between devices: 56.5 us -> 49 us  [move(): lax.ppermute(value, ('dp', 'heads'), [(i, i ^ mask) for i in range(count)])]
    ppermute x48 -> x42, waiting for transfers between devices: 55.7 us -> 48.7 us  [move(): lax.ppermute(value, ('dp', 'heads'), [(i, i ^ mask) for i in range(count)])]
    unnamed x28 -> x29, local copies, waits for them, and re-layouts: 6.36 us -> 3.3 us
    transpose x1 -> x0, local copies, waits for them, and re-layouts: 2.77 us -> none  [on_device(): jnp.swapaxes(latent_out, 0, 1)]
  transfers between devices with their start and end apart: 49 -> 43, of which waited for: 25 -> 18; matrix products, arithmetic and copies ran while one was open for 1% -> 1% of each run, Pallas kernels for 1% -> 2%
where the time goes in v3:
time: 154 us
  waiting for transfers between devices  70.7 us (46%)
  starting transfers between devices  56.5 us (37%)
  Pallas kernels  19.6 us (13%)
  local copies, waits for them, and re-layouts  3.52 us (2%)
  other arithmetic  2.8 us (2%)
    ppermute x42, starting transfers between devices, move(): lax.ppermute(value, ('dp', 'heads'), [(i, i ^ mask) for i in range(count)])  49 us
    ppermute x42, waiting for transfers between devices, move(): lax.ppermute(value, ('dp', 'heads'), [(i, i ^ mask) for i in range(count)])  48.7 us
    all_to_all x1, waiting for transfers between devices, on_device(): lax.all_to_all(latent_out, 'dp', split_axis=0, concat_axis=0, tiled=True)  21.9 us
    pallas_call x1, Pallas kernels, attend(): pl.pallas_call(functools.partial(attend_kernel, rows=rows, latent=LAT), g...  7.74 us
    all_to_all x1, starting transfers between devices, on_device(): lax.all_to_all(latent_out, 'dp', split_axis=0, concat_axis=0, tiled=True)  7.51 us
    pallas_call x1, Pallas kernels, experts_of(): pl.pallas_call(functools.partial(expert_kernel, net=net, groups=(len(piec...  6.06 us
    pallas_call x3, Pallas kernels, project(): pl.pallas_call(functools.partial(project_kernel, tile=tile, first=first,...  4.71 us
    unnamed x29, local copies, waits for them, and re-layouts  3.3 us
  transfers between devices with their start and end apart: 43, of which 18 were waited for; matrix products, arithmetic and copies ran while one was open for 1% of the time, Pallas kernels for 2%

profile of v3, /device:TPU:0, one launch (start us, length us, event | category | flops | bytes accessed | tf_op | source)
XLA Modules:
  0.0 153.7 jit_solution(2514878218757497771)
XLA Ops:
  0.0 7.7 %shard_map.136 = bf16[64,16,512]{2,1,0:T(8,128)(2,1)} custom-call(s32[16]{0:T(128)} %lengths.1, bf16[16,64,576]{2,1,0:T(8,128)(2,1)} %q_ref.1, bf16[16,576,256]{2,1,0:T(8,128)(2,1)} %bitcast.190), custom_call_target="tpu_custom_call" | custom-call | tf_op jit(solution)/shard_map/pallas_call | solution.py:59
  7.8 7.5 %all-to-all-start = ((bf16[64,16,512]{2,1,0:T(8,128)(2,1)}), bf16[64,16,512]{2,1,0:T(8,128)(2,1)S(1)}, u32[]{:S(2)}, u32[]{:S(2)}) async-start(bf16[64,16,512]{2,1,0:T(8,128)(2,1)} %shard_map.136), calls=%async_computation | async-start | bytes 2097152 | tf_op jit(solution)/shard_map/all_to_all | solution.py:437
  16.3 21.9 %all-to-all-done = bf16[64,16,512]{2,1,0:T(8,128)(2,1)S(1)} async-done(((bf16[64,16,512]{2,1,0:T(8,128)(2,1)}), bf16[64,16,512]{2,1,0:T(8,128)(2,1)S(1)}, u32[]{:S(2)}, u32[]{:S(2)}) %all-to-all-start) | async-done | bytes 1048608 | tf_op jit(solution)/shard_map/all_to_all | solution.py:437
  39.2 3.1 %copy-done.1 = bf16[1,4,128,7168]{3,2,1,0:T(8,128)(2,1)S(1)} copy-done((bf16[1,4,128,7168]{3,2,1,0:T(8,128)(2,1)S(1)}, bf16[1,4,128,7168]{3,2,1,0:T(8,128)(2,1)}, u32[]{:S(2)}) %copy-start.1) | copy-done | bytes 7340056
  42.3 2.1 %shard_map.138 = (bf16[2,128,2560]{2,1,0:T(8,128)(2,1)S(1)}, bf16[2,128,2560]{2,1,0:T(8,128)(2,1)S(1)}) custom-call(s32[2]{0:T(128)S(1)} %iota_xor_fusion.cols, bf16[256,512]{1,0:T(8,128)(2,1)S(1)} %shard_map.137.refs_0_, bf16[512,7168]{1,0:T(8,128)(2,1)S(1)} %bitcast.169), custom_call_target="tpu_custom_call" | custom-call | flops 1342177280 | bytes 7864320 | tf_op jit(solution)/shard_map/pallas_call | solution.py:160
  46.5 2.0 %collective-permute-done.1 = bf16[2,128,1024]{2,1,0:T(8,128)(2,1)S(1)} collective-permute-done((bf16[2,128,1024]{2,1,0:T(8,128)(2,1)S(1)}, bf16[2,128,1024]{2,1,0:T(8,128)(2,1)S(1)}, u32[]{:S(2)}, u32[]{:S(2)}) %collective-permute-start.1) | collective-permute-done | bytes 524320 | tf_op jit(solution)/shard_map/ppermute | solution.py:90
  48.9 2.0 %collective-permute-start.2 = (bf16[64,2560]{1,0:T(8,128)(2,1)S(1)}, bf16[64,2560]{1,0:T(8,128)(2,1)S(1)}, u32[]{:S(2)}, u32[]{:S(2)}) collective-permute-start(bf16[64,2560]{1,0:T(8,128)(2,1)S(1)} %get-tuple-element.65), channel_id=1, source_target_pairs={{0,4},{1,5},{2,6},{3,7},{4,0},{5,1},{6,2},{7,3},{8,12},{9,13},{10,... | collective-permute-start | bytes 983048 | tf_op jit(solution)/shard_map/ppermute | solution.py:90
  51.0 1.5 collective-permute-start.3
  52.5 3.3 %collective-permute-start.5 = (bf16[4,16,1024]{2,1,0:T(8,128)(2,1)S(1)}, bf16[4,16,1024]{2,1,0:T(8,128)(2,1)S(1)}, u32[]{:S(2)}, u32[]{:S(2)}) collective-permute-start(bf16[4,16,1024]{2,1,0:T(8,128)(2,1)S(1)} %get-tuple-element.68), channel_id=1, source_target_pairs={{0,8},{1,9},{2,10},{3,11},{4,12},{5,13},{6,14},{7,15},{8,0},{9,1},... | collective-permute-start | bytes 393224 | tf_op jit(solution)/shard_map/ppermute | solution.py:90
  57.3 2.2 %collective-permute-done.2 = bf16[64,2560]{1,0:T(8,128)(2,1)S(1)} collective-permute-done((bf16[64,2560]{1,0:T(8,128)(2,1)S(1)}, bf16[64,2560]{1,0:T(8,128)(2,1)S(1)}, u32[]{:S(2)}, u32[]{:S(2)}) %collective-permute-start.2) | collective-permute-done | bytes 327712 | tf_op jit(solution)/shard_map/ppermute | solution.py:90
  59.5 3.8 %collective-permute-start.7 = (bf16[4,16,1024]{2,1,0:T(8,128)(2,1)S(1)}, bf16[4,16,1024]{2,1,0:T(8,128)(2,1)S(1)}, u32[]{:S(2)}, u32[]{:S(2)}) collective-permute-start(bf16[4,16,1024]{2,1,0:T(8,128)(2,1)S(1)} %get-tuple-element.70), channel_id=1, source_target_pairs={{0,24},{1,25},{2,26},{3,27},{4,28},{5,29},{6,30},{7,31},{8,16},{9,... | collective-permute-start | bytes 393224 | tf_op jit(solution)/shard_map/ppermute | solution.py:90
  63.3 4.4 %collective-permute-done.3 = bf16[64,2560]{1,0:T(8,128)(2,1)S(1)} collective-permute-done((bf16[64,2560]{1,0:T(8,128)(2,1)S(1)}, bf16[64,2560]{1,0:T(8,128)(2,1)S(1)}, u32[]{:S(2)}, u32[]{:S(2)}) %collective-permute-start.3) | collective-permute-done | bytes 327712 | tf_op jit(solution)/shard_map/ppermute | solution.py:90
  69.4 2.9 %collective-permute-start.9 = (bf16[16,2560]{1,0:T(8,128)(2,1)S(1)}, bf16[16,2560]{1,0:T(8,128)(2,1)S(1)}, u32[]{:S(2)}, u32[]{:S(2)}) collective-permute-start(bf16[16,2560]{1,0:T(8,128)(2,1)S(1)} %get-tuple-element.76), channel_id=1, source_target_pairs={{0,8},{1,9},{2,10},{3,11},{4,12},{5,13},{6,14},{7,15},{8,0},{9,1},... | collective-permute-start | bytes 245768 | tf_op jit(solution)/shard_map/ppermute | solution.py:90
  76.2 4.6 %collective-permute-done.10.refs_3_ = bf16[16,2560]{1,0:T(8,128)(2,1)S(1)} collective-permute-done((bf16[16,2560]{1,0:T(8,128)(2,1)S(1)}, bf16[16,2560]{1,0:T(8,128)(2,1)S(1)}, u32[]{:S(2)}, u32[]{:S(2)}) %collective-permute-start.10) | collective-permute-done | bytes 81952 | tf_op jit(solution)/shard_map/ppermute | solution.py:90
  82.1 2.0 %collective-permute-start.15 = (bf16[16,2560]{1,0:T(8,128)(2,1)S(1)}, bf16[16,2560]{1,0:T(8,128)(2,1)S(1)}, u32[]{:S(2)}, u32[]{:S(2)}) collective-permute-start(bf16[16,2560]{1,0:T(8,128)(2,1)S(1)} %get-tuple-element.86), channel_id=1, source_target_pairs={{0,24},{1,25},{2,26},{3,27},{4,28},{5,29},{6,30},{7,31},{8,16},{9,... | collective-permute-start | bytes 245768 | tf_op jit(solution)/shard_map/ppermute | solution.py:90
  86.5 1.5 collective-permute-start.17
  88.6 1.8 %collective-permute-done.14 = bf16[16,2560]{1,0:T(8,128)(2,1)S(1)} collective-permute-done((bf16[16,2560]{1,0:T(8,128)(2,1)S(1)}, bf16[16,2560]{1,0:T(8,128)(2,1)S(1)}, u32[]{:S(2)}, u32[]{:S(2)}) %collective-permute-start.14) | collective-permute-done | bytes 81952 | tf_op jit(solution)/shard_map/ppermute | solution.py:90
  91.0 1.7 %collective-permute-start.20 = (bf16[64,2560]{1,0:T(8,128)(2,1)S(1)}, bf16[64,2560]{1,0:T(8,128)(2,1)S(1)}, u32[]{:S(2)}, u32[]{:S(2)}) collective-permute-start(bf16[64,2560]{1,0:T(8,128)(2,1)S(1)} %pad_maximum_fusion.refs_0_), channel_id=1, source_target_pairs={{0,5},{1,4},{2,7},{3,6},{4,1},{5,0},{6,3},{7,2},{8,13},{9,12},{10,... | collective-permute-start | bytes 983048 | tf_op jit(solution)/shard_map/ppermute | solution.py:90
  95.7 8.3 %collective-permute-done.25 = bf16[64,1152]{1,0:T(8,128)(2,1)S(1)} collective-permute-done((bf16[64,1152]{1,0:T(8,128)(2,1)S(1)}, bf16[64,1152]{1,0:T(8,128)(2,1)S(1)}, u32[]{:S(2)}, u32[]{:S(2)}) %collective-permute-start.25) | collective-permute-done | bytes 147488 | tf_op jit(solution)/shard_map/ppermute | solution.py:90
  104.2 4.9 %collective-permute-done.19.refs_2_ = bf16[64,2560]{1,0:T(8,128)(2,1)S(1)} collective-permute-done((bf16[64,2560]{1,0:T(8,128)(2,1)S(1)}, bf16[64,2560]{1,0:T(8,128)(2,1)S(1)}, u32[]{:S(2)}, u32[]{:S(2)}) %collective-permute-start.19) | collective-permute-done | bytes 327712 | tf_op jit(solution)/shard_map/ppermute | solution.py:90
  109.7 3.3 %collective-permute-done.26.refs_9_ = bf16[128,1152]{1,0:T(8,128)(2,1)S(1)} collective-permute-done((bf16[128,1152]{1,0:T(8,128)(2,1)S(1)}, bf16[128,1152]{1,0:T(8,128)(2,1)S(1)}, u32[]{:S(2)}, u32[]{:S(2)}) %collective-permute-start.26) | collective-permute-done | bytes 294944 | tf_op jit(solution)/shard_map/ppermute | solution.py:90
  113.0 1.5 %collective-permute-done.28.refs_11_ = bf16[128,1152]{1,0:T(8,128)(2,1)S(1)} collective-permute-done((bf16[128,1152]{1,0:T(8,128)(2,1)S(1)}, bf16[128,1152]{1,0:T(8,128)(2,1)S(1)}, u32[]{:S(2)}, u32[]{:S(2)}) %collective-permute-start.28) | collective-permute-done | bytes 294944 | tf_op jit(solution)/shard_map/ppermute | solution.py:90
  114.6 6.1 %shard_map.141 = (bf16[256,512]{1,0:T(8,128)(2,1)S(1)}, f32[256,128]{1,0:T(8,128)S(1)}, bf16[2,128,2560]{2,1,0:T(8,128)(2,1)S(1)}, bf16[2,128,2560]{2,1,0:T(8,128)(2,1)S(1)}) custom-call(s32[2]{0:T(128)S(1)} %iota_xor_fusion.cols, s32[1]{0:T(128)} %bitcast.2.me, bf16[64,2560]{1,0:T(8,128)(2,1)S(1)} %pad_maximum_fusion.refs_0_, ...), custom_call_target="tpu_custom_call" | custom-call | flops 5637144576 | bytes 22020096 | tf_op jit(solution)/shard_map/pallas_call | solution.py:253
  122.6 1.9 %collective-permute-done.30 = bf16[2,128,1024]{2,1,0:T(8,128)(2,1)S(1)} collective-permute-done((bf16[2,128,1024]{2,1,0:T(8,128)(2,1)S(1)}, bf16[2,128,1024]{2,1,0:T(8,128)(2,1)S(1)}, u32[]{:S(2)}, u32[]{:S(2)}) %collective-permute-start.30) | collective-permute-done | bytes 524320 | tf_op jit(solution)/shard_map/ppermute | solution.py:90
  128.8 2.3 %collective-permute-start.35 = (bf16[4,16,1024]{2,1,0:T(8,128)(2,1)S(1)}, bf16[4,16,1024]{2,1,0:T(8,128)(2,1)S(1)}, u32[]{:S(2)}, u32[]{:S(2)}) collective-permute-start(bf16[4,16,1024]{2,1,0:T(8,128)(2,1)S(1)} %get-tuple-element.100), channel_id=1, source_target_pairs={{0,16},{1,17},{2,18},{3,19},{4,20},{5,21},{6,22},{7,23},{8,24},{9,... | collective-permute-start | bytes 393224 | tf_op jit(solution)/shard_map/ppermute | solution.py:90
  131.0 4.5 %collective-permute-done.31 = bf16[64,2560]{1,0:T(8,128)(2,1)S(1)} collective-permute-done((bf16[64,2560]{1,0:T(8,128)(2,1)S(1)}, bf16[64,2560]{1,0:T(8,128)(2,1)S(1)}, u32[]{:S(2)}, u32[]{:S(2)}) %collective-permute-start.31) | collective-permute-done | bytes 327712 | tf_op jit(solution)/shard_map/ppermute | solution.py:90
  135.5 2.0 %collective-permute-start.36 = (bf16[4,16,1024]{2,1,0:T(8,128)(2,1)S(1)}, bf16[4,16,1024]{2,1,0:T(8,128)(2,1)S(1)}, u32[]{:S(2)}, u32[]{:S(2)}) collective-permute-start(bf16[4,16,1024]{2,1,0:T(8,128)(2,1)S(1)} %get-tuple-element.101), channel_id=1, source_target_pairs={{0,24},{1,25},{2,26},{3,27},{4,28},{5,29},{6,30},{7,31},{8,16},{9,... | collective-permute-start | bytes 393224 | tf_op jit(solution)/shard_map/ppermute | solution.py:90
  137.5 3.7 %collective-permute-done.32 = bf16[64,2560]{1,0:T(8,128)(2,1)S(1)} collective-permute-done((bf16[64,2560]{1,0:T(8,128)(2,1)S(1)}, bf16[64,2560]{1,0:T(8,128)(2,1)S(1)}, u32[]{:S(2)}, u32[]{:S(2)}) %collective-permute-start.32) | collective-permute-done | bytes 327712 | tf_op jit(solution)/shard_map/ppermute | solution.py:90
  144.4 2.2 %collective-permute-start.38 = (bf16[16,2560]{1,0:T(8,128)(2,1)S(1)}, bf16[16,2560]{1,0:T(8,128)(2,1)S(1)}, u32[]{:S(2)}, u32[]{:S(2)}) collective-permute-start(bf16[16,2560]{1,0:T(8,128)(2,1)S(1)} %get-tuple-element.107), channel_id=1, source_target_pairs={{0,16},{1,17},{2,18},{3,19},{4,20},{5,21},{6,22},{7,23},{8,24},{9,... | collective-permute-start | bytes 245768 | tf_op jit(solution)/shard_map/ppermute | solution.py:90
  146.6 1.8 %collective-permute-start.39 = (bf16[16,2560]{1,0:T(8,128)(2,1)S(1)}, bf16[16,2560]{1,0:T(8,128)(2,1)S(1)}, u32[]{:S(2)}, u32[]{:S(2)}) collective-permute-start(bf16[16,2560]{1,0:T(8,128)(2,1)S(1)} %get-tuple-element.108), channel_id=1, source_target_pairs={{0,24},{1,25},{2,26},{3,27},{4,28},{5,29},{6,30},{7,31},{8,16},{9,... | collective-permute-start | bytes 245768 | tf_op jit(solution)/shard_map/ppermute | solution.py:90
  148.4 1.5 collective-permute-start.41
  149.9 1.8 %collective-permute-done.38 = bf16[16,2560]{1,0:T(8,128)(2,1)S(1)} collective-permute-done((bf16[16,2560]{1,0:T(8,128)(2,1)S(1)}, bf16[16,2560]{1,0:T(8,128)(2,1)S(1)}, u32[]{:S(2)}, u32[]{:S(2)}) %collective-permute-start.38) | collective-permute-done | bytes 81952 | tf_op jit(solution)/shard_map/ppermute | solution.py:90
  (130 shorter events, 31.0 us)
Async XLA Ops:
  7.8 30.5 %all-to-all-start = ((bf16[64,16,512]{2,1,0:T(8,128)(2,1)}), bf16[64,16,512]{2,1,0:T(8,128)(2,1)S(1)}, u32[]{:S(2)}, u32[]{:S(2)}) async-start(bf16[64,16,512]{2,1,0:T(8,128)(2,1)} %shard_map.136), calls=%async_computation | async-start | bytes 2097152 | tf_op jit(solution)/shard_map/all_to_all | solution.py:437
  48.9 10.6 %collective-permute-start.2 = (bf16[64,2560]{1,0:T(8,128)(2,1)S(1)}, bf16[64,2560]{1,0:T(8,128)(2,1)S(1)}, u32[]{:S(2)}, u32[]{:S(2)}) collective-permute-start(bf16[64,2560]{1,0:T(8,128)(2,1)S(1)} %get-tuple-element.65), channel_id=1, source_target_pairs={{0,4},{1,5},{2,6},{3,7},{4,0},{5,1},{6,2},{7,3},{8,12},{9,13},{10,... | collective-permute-start | bytes 983048 | tf_op jit(solution)/shard_map/ppermute | solution.py:90
  51.0 16.7 %collective-permute-start.3 = (bf16[64,2560]{1,0:T(8,128)(2,1)S(1)}, bf16[64,2560]{1,0:T(8,128)(2,1)S(1)}, u32[]{:S(2)}, u32[]{:S(2)}) collective-permute-start(bf16[64,2560]{1,0:T(8,128)(2,1)S(1)} %get-tuple-element.66), channel_id=1, source_target_pairs={{0,1},{1,0},{2,3},{3,2},{4,5},{5,4},{6,7},{7,6},{8,9},{9,8},{10,11... | collective-permute-start | bytes 983048 | tf_op jit(solution)/shard_map/ppermute | solution.py:90
  52.5 15.2 %collective-permute-start.4 = (bf16[64,2560]{1,0:T(8,128)(2,1)S(1)}, bf16[64,2560]{1,0:T(8,128)(2,1)S(1)}, u32[]{:S(2)}, u32[]{:S(2)}) collective-permute-start(bf16[64,2560]{1,0:T(8,128)(2,1)S(1)} %get-tuple-element.67), channel_id=1, source_target_pairs={{0,5},{1,4},{2,7},{3,6},{4,1},{5,0},{6,3},{7,2},{8,13},{9,12},{10,... | collective-permute-start | bytes 983048 | tf_op jit(solution)/shard_map/ppermute | solution.py:90
  52.5 15.4 %collective-permute-start.5 = (bf16[4,16,1024]{2,1,0:T(8,128)(2,1)S(1)}, bf16[4,16,1024]{2,1,0:T(8,128)(2,1)S(1)}, u32[]{:S(2)}, u32[]{:S(2)}) collective-permute-start(bf16[4,16,1024]{2,1,0:T(8,128)(2,1)S(1)} %get-tuple-element.68), channel_id=1, source_target_pairs={{0,8},{1,9},{2,10},{3,11},{4,12},{5,13},{6,14},{7,15},{8,0},{9,1},... | collective-permute-start | bytes 393224 | tf_op jit(solution)/shard_map/ppermute | solution.py:90
  55.9 12.0 %collective-permute-start.6 = (bf16[4,16,1024]{2,1,0:T(8,128)(2,1)S(1)}, bf16[4,16,1024]{2,1,0:T(8,128)(2,1)S(1)}, u32[]{:S(2)}, u32[]{:S(2)}) collective-permute-start(bf16[4,16,1024]{2,1,0:T(8,128)(2,1)S(1)} %get-tuple-element.69), channel_id=1, source_target_pairs={{0,16},{1,17},{2,18},{3,19},{4,20},{5,21},{6,22},{7,23},{8,24},{9,... | collective-permute-start | bytes 393224 | tf_op jit(solution)/shard_map/ppermute | solution.py:90
  59.5 8.4 %collective-permute-start.7 = (bf16[4,16,1024]{2,1,0:T(8,128)(2,1)S(1)}, bf16[4,16,1024]{2,1,0:T(8,128)(2,1)S(1)}, u32[]{:S(2)}, u32[]{:S(2)}) collective-permute-start(bf16[4,16,1024]{2,1,0:T(8,128)(2,1)S(1)} %get-tuple-element.70), channel_id=1, source_target_pairs={{0,24},{1,25},{2,26},{3,27},{4,28},{5,29},{6,30},{7,31},{8,16},{9,... | collective-permute-start | bytes 393224 | tf_op jit(solution)/shard_map/ppermute | solution.py:90
  68.1 6.6 %collective-permute-start.8 = (bf16[2,16,1024]{2,1,0:T(8,128)(2,1)S(1)}, bf16[2,16,1024]{2,1,0:T(8,128)(2,1)S(1)}, u32[]{:S(2)}, u32[]{:S(2)}) collective-permute-start(bf16[2,16,1024]{2,1,0:T(8,128)(2,1)S(1)} %pad_maximum_fusion.4), channel_id=1, source_target_pairs={{0,4},{1,5},{2,6},{3,7},{4,0},{5,1},{6,2},{7,3},{8,12},{9,13},{10,... | collective-permute-start | bytes 196616 | tf_op jit(solution)/shard_map/ppermute | solution.py:90
  69.4 6.7 %collective-permute-start.9 = (bf16[16,2560]{1,0:T(8,128)(2,1)S(1)}, bf16[16,2560]{1,0:T(8,128)(2,1)S(1)}, u32[]{:S(2)}, u32[]{:S(2)}) collective-permute-start(bf16[16,2560]{1,0:T(8,128)(2,1)S(1)} %get-tuple-element.76), channel_id=1, source_target_pairs={{0,8},{1,9},{2,10},{3,11},{4,12},{5,13},{6,14},{7,15},{8,0},{9,1},... | collective-permute-start | bytes 245768 | tf_op jit(solution)/shard_map/ppermute | solution.py:90
  72.3 8.4 %collective-permute-start.10 = (bf16[16,2560]{1,0:T(8,128)(2,1)S(1)}, bf16[16,2560]{1,0:T(8,128)(2,1)S(1)}, u32[]{:S(2)}, u32[]{:S(2)}) collective-permute-start(bf16[16,2560]{1,0:T(8,128)(2,1)S(1)} %get-tuple-element.77), channel_id=1, source_target_pairs={{0,16},{1,17},{2,18},{3,19},{4,20},{5,21},{6,22},{7,23},{8,24},{9,... | collective-permute-start | bytes 245768 | tf_op jit(solution)/shard_map/ppermute | solution.py:90
  73.8 7.0 %collective-permute-start.11 = (bf16[16,2560]{1,0:T(8,128)(2,1)S(1)}, bf16[16,2560]{1,0:T(8,128)(2,1)S(1)}, u32[]{:S(2)}, u32[]{:S(2)}) collective-permute-start(bf16[16,2560]{1,0:T(8,128)(2,1)S(1)} %get-tuple-element.78), channel_id=1, source_target_pairs={{0,24},{1,25},{2,26},{3,27},{4,28},{5,29},{6,30},{7,31},{8,16},{9,... | collective-permute-start | bytes 245768 | tf_op jit(solution)/shard_map/ppermute | solution.py:90
  74.7 6.1 %collective-permute-start.12 = (bf16[1,16,1024]{2,1,0:T(8,128)(2,1)S(1)}, bf16[1,16,1024]{2,1,0:T(8,128)(2,1)S(1)}, u32[]{:S(2)}, u32[]{:S(2)}) collective-permute-start(bf16[1,16,1024]{2,1,0:T(8,128)(2,1)S(1)} %get-tuple-element.130), channel_id=1, source_target_pairs={{0,1},{1,0},{2,3},{3,2},{4,5},{5,4},{6,7},{7,6},{8,9},{9,8},{10,11... | collective-permute-start | bytes 98312 | tf_op jit(solution)/shard_map/ppermute | solution.py:90
  80.9 5.6 %collective-permute-start.16 = (bf16[16,1152]{1,0:T(8,128)(2,1)S(1)}, bf16[16,1152]{1,0:T(8,128)(2,1)S(1)}, u32[]{:S(2)}, u32[]{:S(2)}) collective-permute-start(bf16[16,1152]{1,0:T(8,128)(2,1)S(1)} %get-tuple-element.87), channel_id=1, source_target_pairs={{0,4},{1,5},{2,6},{3,7},{4,0},{5,1},{6,2},{7,3},{8,12},{9,13},{10,... | collective-permute-start | bytes 110600 | tf_op jit(solution)/shard_map/ppermute | solution.py:90
  82.1 6.4 %collective-permute-start.15 = (bf16[16,2560]{1,0:T(8,128)(2,1)S(1)}, bf16[16,2560]{1,0:T(8,128)(2,1)S(1)}, u32[]{:S(2)}, u32[]{:S(2)}) collective-permute-start(bf16[16,2560]{1,0:T(8,128)(2,1)S(1)} %get-tuple-element.86), channel_id=1, source_target_pairs={{0,24},{1,25},{2,26},{3,27},{4,28},{5,29},{6,30},{7,31},{8,16},{9,... | collective-permute-start | bytes 245768 | tf_op jit(solution)/shard_map/ppermute | solution.py:90
  84.1 6.2 %collective-permute-start.14 = (bf16[16,2560]{1,0:T(8,128)(2,1)S(1)}, bf16[16,2560]{1,0:T(8,128)(2,1)S(1)}, u32[]{:S(2)}, u32[]{:S(2)}) collective-permute-start(bf16[16,2560]{1,0:T(8,128)(2,1)S(1)} %get-tuple-element.86), channel_id=1, source_target_pairs={{0,16},{1,17},{2,18},{3,19},{4,20},{5,21},{6,22},{7,23},{8,24},{9,... | collective-permute-start | bytes 245768 | tf_op jit(solution)/shard_map/ppermute | solution.py:90
  91.0 18.6 %collective-permute-start.21 = (bf16[64,2560]{1,0:T(8,128)(2,1)S(1)}, bf16[64,2560]{1,0:T(8,128)(2,1)S(1)}, u32[]{:S(2)}, u32[]{:S(2)}) collective-permute-start(bf16[64,2560]{1,0:T(8,128)(2,1)S(1)} %pad_maximum_fusion.refs_0_), channel_id=1, source_target_pairs={{0,2},{1,3},{2,0},{3,1},{4,6},{5,7},{6,4},{7,5},{8,10},{9,11},{10,... | collective-permute-start | bytes 983048 | tf_op jit(solution)/shard_map/ppermute | solution.py:90
  91.0 13.0 %collective-permute-start.20 = (bf16[64,2560]{1,0:T(8,128)(2,1)S(1)}, bf16[64,2560]{1,0:T(8,128)(2,1)S(1)}, u32[]{:S(2)}, u32[]{:S(2)}) collective-permute-start(bf16[64,2560]{1,0:T(8,128)(2,1)S(1)} %pad_maximum_fusion.refs_0_), channel_id=1, source_target_pairs={{0,5},{1,4},{2,7},{3,6},{4,1},{5,0},{6,3},{7,2},{8,13},{9,12},{10,... | collective-permute-start | bytes 983048 | tf_op jit(solution)/shard_map/ppermute | solution.py:90
  92.8 16.3 %collective-permute-start.19 = (bf16[64,2560]{1,0:T(8,128)(2,1)S(1)}, bf16[64,2560]{1,0:T(8,128)(2,1)S(1)}, u32[]{:S(2)}, u32[]{:S(2)}) collective-permute-start(bf16[64,2560]{1,0:T(8,128)(2,1)S(1)} %pad_maximum_fusion.refs_0_), channel_id=1, source_target_pairs={{0,1},{1,0},{2,3},{3,2},{4,5},{5,4},{6,7},{7,6},{8,9},{9,8},{10,11... | collective-permute-start | bytes 983048 | tf_op jit(solution)/shard_map/ppermute | solution.py:90
  93.4 15.7 %collective-permute-start.18 = (bf16[64,2560]{1,0:T(8,128)(2,1)S(1)}, bf16[64,2560]{1,0:T(8,128)(2,1)S(1)}, u32[]{:S(2)}, u32[]{:S(2)}) collective-permute-start(bf16[64,2560]{1,0:T(8,128)(2,1)S(1)} %pad_maximum_fusion.refs_0_), channel_id=1, source_target_pairs={{0,4},{1,5},{2,6},{3,7},{4,0},{5,1},{6,2},{7,3},{8,12},{9,13},{10,... | collective-permute-start | bytes 983048 | tf_op jit(solution)/shard_map/ppermute | solution.py:90
  94.6 9.4 %collective-permute-start.25 = (bf16[64,1152]{1,0:T(8,128)(2,1)S(1)}, bf16[64,1152]{1,0:T(8,128)(2,1)S(1)}, u32[]{:S(2)}, u32[]{:S(2)}) collective-permute-start(bf16[64,1152]{1,0:T(8,128)(2,1)S(1)} %pad_maximum_fusion.1), channel_id=1, source_target_pairs={{0,16},{1,17},{2,18},{3,19},{4,20},{5,21},{6,22},{7,23},{8,24},{9,... | collective-permute-start | bytes 442376 | tf_op jit(solution)/shard_map/ppermute | solution.py:90
  104.0 9.0 %collective-permute-start.26 = (bf16[128,1152]{1,0:T(8,128)(2,1)S(1)}, bf16[128,1152]{1,0:T(8,128)(2,1)S(1)}, u32[]{:S(2)}, u32[]{:S(2)}) collective-permute-start(bf16[128,1152]{1,0:T(8,128)(2,1)S(1)} %constant_dynamic-update-slice_fusion.refs_8_), channel_id=1, source_target_pairs={{0,8},{1,9},{2,10},{3,11},{4,12},{5,13},{6,14},{7,15},{8,0},{9,1},... | collective-permute-start | bytes 884744 | tf_op jit(solution)/shard_map/ppermute | solution.py:90
  104.1 8.9 %collective-permute-start.24 = (bf16[64,2560]{1,0:T(8,128)(2,1)S(1)}, bf16[64,2560]{1,0:T(8,128)(2,1)S(1)}, u32[]{:S(2)}, u32[]{:S(2)}) collective-permute-start(bf16[64,2560]{1,0:T(8,128)(2,1)S(1)} %collective-permute-done.20.refs_3_), channel_id=1, source_target_pairs={{0,2},{1,3},{2,0},{3,1},{4,6},{5,7},{6,4},{7,5},{8,10},{9,11},{10,... | collective-permute-start | bytes 983048 | tf_op jit(solution)/shard_map/ppermute | solution.py:90
  124.9 10.6 %collective-permute-start.31 = (bf16[64,2560]{1,0:T(8,128)(2,1)S(1)}, bf16[64,2560]{1,0:T(8,128)(2,1)S(1)}, u32[]{:S(2)}, u32[]{:S(2)}) collective-permute-start(bf16[64,2560]{1,0:T(8,128)(2,1)S(1)} %get-tuple-element.96), channel_id=1, source_target_pairs={{0,4},{1,5},{2,6},{3,7},{4,0},{5,1},{6,2},{7,3},{8,12},{9,13},{10,... | collective-permute-start | bytes 983048 | tf_op jit(solution)/shard_map/ppermute | solution.py:90
  125.9 15.4 %collective-permute-start.32 = (bf16[64,2560]{1,0:T(8,128)(2,1)S(1)}, bf16[64,2560]{1,0:T(8,128)(2,1)S(1)}, u32[]{:S(2)}, u32[]{:S(2)}) collective-permute-start(bf16[64,2560]{1,0:T(8,128)(2,1)S(1)} %get-tuple-element.97), channel_id=1, source_target_pairs={{0,1},{1,0},{2,3},{3,2},{4,5},{5,4},{6,7},{7,6},{8,9},{9,8},{10,11... | collective-permute-start | bytes 983048 | tf_op jit(solution)/shard_map/ppermute | solution.py:90
  127.2 15.4 %collective-permute-start.33 = (bf16[64,2560]{1,0:T(8,128)(2,1)S(1)}, bf16[64,2560]{1,0:T(8,128)(2,1)S(1)}, u32[]{:S(2)}, u32[]{:S(2)}) collective-permute-start(bf16[64,2560]{1,0:T(8,128)(2,1)S(1)} %get-tuple-element.98), channel_id=1, source_target_pairs={{0,5},{1,4},{2,7},{3,6},{4,1},{5,0},{6,3},{7,2},{8,13},{9,12},{10,... | collective-permute-start | bytes 983048 | tf_op jit(solution)/shard_map/ppermute | solution.py:90
  128.5 14.4 %collective-permute-start.34 = (bf16[4,16,1024]{2,1,0:T(8,128)(2,1)S(1)}, bf16[4,16,1024]{2,1,0:T(8,128)(2,1)S(1)}, u32[]{:S(2)}, u32[]{:S(2)}) collective-permute-start(bf16[4,16,1024]{2,1,0:T(8,128)(2,1)S(1)} %get-tuple-element.99), channel_id=1, source_target_pairs={{0,8},{1,9},{2,10},{3,11},{4,12},{5,13},{6,14},{7,15},{8,0},{9,1},... | collective-permute-start | bytes 393224 | tf_op jit(solution)/shard_map/ppermute | solution.py:90
  128.8 14.1 %collective-permute-start.35 = (bf16[4,16,1024]{2,1,0:T(8,128)(2,1)S(1)}, bf16[4,16,1024]{2,1,0:T(8,128)(2,1)S(1)}, u32[]{:S(2)}, u32[]{:S(2)}) collective-permute-start(bf16[4,16,1024]{2,1,0:T(8,128)(2,1)S(1)} %get-tuple-element.100), channel_id=1, source_target_pairs={{0,16},{1,17},{2,18},{3,19},{4,20},{5,21},{6,22},{7,23},{8,24},{9,... | collective-permute-start | bytes 393224 | tf_op jit(solution)/shard_map/ppermute | solution.py:90
  135.5 7.3 %collective-permute-start.36 = (bf16[4,16,1024]{2,1,0:T(8,128)(2,1)S(1)}, bf16[4,16,1024]{2,1,0:T(8,128)(2,1)S(1)}, u32[]{:S(2)}, u32[]{:S(2)}) collective-permute-start(bf16[4,16,1024]{2,1,0:T(8,128)(2,1)S(1)} %get-tuple-element.101), channel_id=1, source_target_pairs={{0,24},{1,25},{2,26},{3,27},{4,28},{5,29},{6,30},{7,31},{8,16},{9,... | collective-permute-start | bytes 393224 | tf_op jit(solution)/shard_map/ppermute | solution.py:90
  143.1 5.3 %collective-permute-start.40 = (bf16[2,16,1024]{2,1,0:T(8,128)(2,1)S(1)}, bf16[2,16,1024]{2,1,0:T(8,128)(2,1)S(1)}, u32[]{:S(2)}, u32[]{:S(2)}) collective-permute-start(bf16[2,16,1024]{2,1,0:T(8,128)(2,1)S(1)} %pad_maximum_fusion.5), channel_id=1, source_target_pairs={{0,4},{1,5},{2,6},{3,7},{4,0},{5,1},{6,2},{7,3},{8,12},{9,13},{10,... | collective-permute-start | bytes 196616 | tf_op jit(solution)/shard_map/ppermute | solution.py:90
  144.0 5.9 %collective-permute-start.37 = (bf16[16,2560]{1,0:T(8,128)(2,1)S(1)}, bf16[16,2560]{1,0:T(8,128)(2,1)S(1)}, u32[]{:S(2)}, u32[]{:S(2)}) collective-permute-start(bf16[16,2560]{1,0:T(8,128)(2,1)S(1)} %get-tuple-element.106), channel_id=1, source_target_pairs={{0,8},{1,9},{2,10},{3,11},{4,12},{5,13},{6,14},{7,15},{8,0},{9,1},... | collective-permute-start | bytes 245768 | tf_op jit(solution)/shard_map/ppermute | solution.py:90
  144.4 7.4 %collective-permute-start.38 = (bf16[16,2560]{1,0:T(8,128)(2,1)S(1)}, bf16[16,2560]{1,0:T(8,128)(2,1)S(1)}, u32[]{:S(2)}, u32[]{:S(2)}) collective-permute-start(bf16[16,2560]{1,0:T(8,128)(2,1)S(1)} %get-tuple-element.107), channel_id=1, source_target_pairs={{0,16},{1,17},{2,18},{3,19},{4,20},{5,21},{6,22},{7,23},{8,24},{9,... | collective-permute-start | bytes 245768 | tf_op jit(solution)/shard_map/ppermute | solution.py:90
  146.6 6.3 %collective-permute-start.39 = (bf16[16,2560]{1,0:T(8,128)(2,1)S(1)}, bf16[16,2560]{1,0:T(8,128)(2,1)S(1)}, u32[]{:S(2)}, u32[]{:S(2)}) collective-permute-start(bf16[16,2560]{1,0:T(8,128)(2,1)S(1)} %get-tuple-element.108), channel_id=1, source_target_pairs={{0,24},{1,25},{2,26},{3,27},{4,28},{5,29},{6,30},{7,31},{8,16},{9,... | collective-permute-start | bytes 245768 | tf_op jit(solution)/shard_map/ppermute | solution.py:90
  (24 other events, 453.7 us)

commit v4 on v3

--- a/solution.py
+++ b/solution.py
@@ -55,7 +55,7 @@
     count, heads, depth = queries.shape
     context = kv_cache.shape[1]
     cache = jnp.swapaxes(kv_cache, 1, 2)
-    rows = 4
+    rows = 8
     return pl.pallas_call(
         functools.partial(attend_kernel, rows=rows, latent=LAT),
         grid=(count // rows,),
@@ -195,7 +195,7 @@
     return jnp.concatenate(parts, 0)
 
 
-def expert_kernel(cols, me, *refs, net, groups, rows_dev, tile, counts, width):
+def expert_kernel(cols, me, *refs, net, groups, rows_dev, tile, counts, down_count, width):
     pieces = []
     for per_core in groups:
         pieces.append([refs[:per_core], refs[per_core : 2 * per_core]])
@@ -236,20 +236,20 @@
     up = up_acc[...] * norm
     hidden_ref[...] = (gate / (1.0 + jnp.exp(-gate)) * up).astype(BF16)
     for h in range(heads):
-        for t in range(counts[0]):
+        for t in range(down_count):
             lanes = column_lanes(cols, h, tile, 0, t, slice_width)
             out = jnp.dot(hidden_ref[...], down_ref[:, lanes], preferred_element_type=F32) * coef
             put(out, keep_ref, send_ref, h, slice(t * tile, (t + 1) * tile))
 
 
-def experts_of(net, pieces_a, pieces_b, gate_w, up_w, down_w, cols, me, tile, counts, rows_dev):
+def experts_of(net, pieces_a, pieces_b, gate_w, up_w, down_w, cols, me, tile, counts, down_count, rows_dev):
     flat = [piece for pieces in (pieces_a, pieces_b) for group in pieces for piece in group]
     width, hidden = gate_w.shape
     rows = net.dp * rows_dev
     heads = net.heads
     vmem = pl.BlockSpec(memory_space=pltpu.VMEM)
     smem = pl.BlockSpec(memory_space=pltpu.SMEM)
-    out = jax.ShapeDtypeStruct((heads, rows // 2, counts[0] * tile), BF16)
+    out = jax.ShapeDtypeStruct((heads, rows // 2, down_count * tile), BF16)
     return pl.pallas_call(
         functools.partial(
             expert_kernel,
@@ -258,6 +258,7 @@
             rows_dev=rows_dev,
             tile=tile,
             counts=counts,
+            down_count=down_count,
             width=width,
         ),
         in_specs=[smem, smem] + [vmem] * (len(flat) + 3),
@@ -281,7 +282,7 @@
     )(cols, me, *flat, gate_w, up_w, down_w)
 
 
-def payload_kernel(*refs, arrived, width):
+def payload_kernel(*refs, arrived, split):
     own, rest = refs[:2], refs[2:]
     received, rest = [rest[: arrived[0]], rest[arrived[0] : sum(arrived)]], rest[sum(arrived) :]
     resid_ref, gain_ref, extra_ref = rest[:3]
@@ -296,7 +297,13 @@
         size = total.shape[-1]
         mid = resid_ref[:, start : start + size].astype(F32) + total
         mids[which][...] = mid
-        rows[which][:, :size] = (mid * gain_ref[:, start : start + size].astype(F32)).astype(BF16)
+        row = (mid * gain_ref[:, start : start + size].astype(F32)).astype(BF16)
+        if which == 0:
+            rows[0][:, :size] = row
+        else:
+            more = split - start
+            rows[0][:, start:split] = row[:, :more]
+            rows[1][:, : size - more] = row[:, more:]
         squares = squares + jnp.sum(mid * mid, -1, keepdims=True)
         start += size
     high = squares.astype(BF16)
@@ -306,23 +313,23 @@
     extra = extra_ref[...]
     for at, part in enumerate((high, middle, low)):
         extra = jnp.where(lane == at, jnp.broadcast_to(part, extra.shape), extra)
-    rows[1][:, size:] = extra
-
-
-def payloads(parts_a, parts_b, resid, gain, extra):
+    rows[1][:, start - split :] = extra
+
+
+def payloads(parts_a, parts_b, resid, gain, extra, split):
     own_a, in_a = parts_a
     own_b, in_b = parts_b
     rows = own_a.shape[0]
     mids = [jax.ShapeDtypeStruct(own.shape, F32) for own in (own_a, own_b)]
     outs = [
-        jax.ShapeDtypeStruct((rows, own_a.shape[1]), BF16),
-        jax.ShapeDtypeStruct((rows, own_b.shape[1] + EXTRA), BF16),
+        jax.ShapeDtypeStruct((rows, split), BF16),
+        jax.ShapeDtypeStruct((rows, resid.shape[1] - split + EXTRA), BF16),
     ]
     operands = [own_a, own_b, *in_a, *in_b, resid, gain, extra]
     vmem = pl.BlockSpec(memory_space=pltpu.VMEM)
     return pl.pallas_call(
         functools.partial(
-            payload_kernel, arrived=(len(in_a), len(in_b)), width=resid.shape[1]
+            payload_kernel, arrived=(len(in_a), len(in_b)), split=split
         ),
         in_specs=[vmem] * len(operands),
         out_specs=[vmem] * 4,
@@ -381,11 +388,14 @@
 def gather_both(net, row_a, row_b):
     places, line = len(net.plane), net.line
     row_a, row_b = lax.optimization_barrier((row_a, row_b))
+    in_a = [net.in_line(row_a, jz) for jz in range(1, line)]
+    held_a = jnp.concatenate([row_a] + in_a, 0)
     held_b = row_b
     for bit in range(net.plane_bits):
-        held_b = jnp.concatenate([held_b, net.in_plane(held_b, 1 << bit)], 0)
-    in_a = [net.in_line(row_a, jz) for jz in range(1, line)]
-    held_a = jnp.concatenate([row_a] + in_a, 0)
+        last = net.in_plane(held_b, 1 << bit)
+        if bit == net.plane_bits - 1:
+            held_a, last = lax.optimization_barrier((held_a, last))
+        held_b = jnp.concatenate([held_b, last], 0)
     held_a, held_b = lax.optimization_barrier((held_a, held_b))
     for bit in reversed(range(1, net.line_bits)):
         held_b = jnp.concatenate([held_b, net.in_line(held_b, 1 << bit)], 0)
@@ -417,6 +427,7 @@
     tile, wide_count, narrow_count = slice_width // 14, 10, 4
     if tile % 128:
         tile, wide_count, narrow_count = slice_width // 7, 5, 2
+    gather_counts = (wide_count + 1, narrow_count - 1)
     me = lax.axis_index("dp")
     my_head = lax.axis_index("heads")
     slots = jnp.array(
@@ -460,7 +471,7 @@
     keep_b, send_b = project(values, out_proj, cols, None, tile, wide_count, narrow_count)
     parts_a, parts_b = reduce_both(net, (keep_a, send_a), (keep_b, send_b), rows_dev)
     mid_a, mid_b, row_a, row_b = payloads(
-        parts_a, parts_b, resid_slice, gain_slice, extra
+        parts_a, parts_b, resid_slice, gain_slice, extra, gather_counts[0] * tile
     )
     pieces_a, pieces_b = gather_both(net, row_a, row_b)
 
@@ -474,7 +485,8 @@
         cols,
         mine,
         tile,
-        (wide_count, narrow_count),
+        gather_counts,
+        wide_count,
         rows_dev,
     )
     keep_b, send_b = project(hidden, down_w[0], cols, coef, tile, wide_count, narrow_count)

time: 154 us -> 151 us (0.981)
  starting transfers between devices: 56.5 us -> 50.5 us
  waiting for transfers between devices: 70.7 us -> 75.1 us
    ppermute x42, starting transfers between devices: 49 us -> 42.8 us  [move(): lax.ppermute(value, ('dp', 'heads'), [(i, i ^ mask) for i in range(count)])]
    ppermute x42, waiting for transfers between devices: 48.7 us -> 53.3 us  [move(): lax.ppermute(value, ('dp', 'heads'), [(i, i ^ mask) for i in range(count)])]
  transfers between devices with their start and end apart: 43 -> 43, of which waited for: 18 -> 19; matrix products, arithmetic and copies ran while one was open for 1% -> 1% of each run, Pallas kernels for 2% -> 2%
where the time goes in v4:
time: 151 us
  waiting for transfers between devices  75.1 us (50%)
  starting transfers between devices  50.5 us (33%)
  Pallas kernels  18.8 us (12%)
  local copies, waits for them, and re-layouts  3.51 us (2%)
  other arithmetic  2.8 us (2%)
    ppermute x42, waiting for transfers between devices, move(): lax.ppermute(value, ('dp', 'heads'), [(i, i ^ mask) for i in range(count)])  53.3 us
    ppermute x42, starting transfers between devices, move(): lax.ppermute(value, ('dp', 'heads'), [(i, i ^ mask) for i in range(count)])  42.8 us
    all_to_all x1, waiting for transfers between devices, on_device(): lax.all_to_all(latent_out, 'dp', split_axis=0, concat_axis=0, tiled=True)  21.8 us
    all_to_all x1, starting transfers between devices, on_device(): lax.all_to_all(latent_out, 'dp', split_axis=0, concat_axis=0, tiled=True)  7.68 us
    pallas_call x1, Pallas kernels, attend(): pl.pallas_call(functools.partial(attend_kernel, rows=rows, latent=LAT), g...  6.88 us
    pallas_call x1, Pallas kernels, experts_of(): pl.pallas_call(functools.partial(expert_kernel, net=net, groups=(len(piec...  6.06 us
    pallas_call x3, Pallas kernels, project(): pl.pallas_call(functools.partial(project_kernel, tile=tile, first=first,...  4.72 us
    unnamed x29, local copies, waits for them, and re-layouts  3.29 us
  transfers between devices with their start and end apart: 43, of which 19 were waited for; matrix products, arithmetic and copies ran while one was open for 1% of the time, Pallas kernels for 2%

profile of v4, /device:TPU:0, one launch (start us, length us, event | category | flops | bytes accessed | tf_op | source)
XLA Modules:
  0.0 151.2 jit_solution(14444259574454150332)
XLA Ops:
  0.0 6.9 %shard_map.136 = bf16[64,16,512]{2,1,0:T(8,128)(2,1)} custom-call(s32[16]{0:T(128)} %lengths.1, bf16[16,64,576]{2,1,0:T(8,128)(2,1)} %q_ref.1, bf16[16,576,256]{2,1,0:T(8,128)(2,1)} %bitcast.190), custom_call_target="tpu_custom_call" | custom-call | tf_op jit(solution)/shard_map/pallas_call | solution.py:59
  6.9 7.7 %all-to-all-start = ((bf16[64,16,512]{2,1,0:T(8,128)(2,1)}), bf16[64,16,512]{2,1,0:T(8,128)(2,1)S(1)}, u32[]{:S(2)}, u32[]{:S(2)}) async-start(bf16[64,16,512]{2,1,0:T(8,128)(2,1)} %shard_map.136), calls=%async_computation | async-start | bytes 2097152 | tf_op jit(solution)/shard_map/all_to_all | solution.py:448
  15.6 21.8 %all-to-all-done = bf16[64,16,512]{2,1,0:T(8,128)(2,1)S(1)} async-done(((bf16[64,16,512]{2,1,0:T(8,128)(2,1)}), bf16[64,16,512]{2,1,0:T(8,128)(2,1)S(1)}, u32[]{:S(2)}, u32[]{:S(2)}) %all-to-all-start) | async-done | bytes 1048608 | tf_op jit(solution)/shard_map/all_to_all | solution.py:448
  38.4 3.1 %copy-done.1 = bf16[1,4,128,7168]{3,2,1,0:T(8,128)(2,1)S(1)} copy-done((bf16[1,4,128,7168]{3,2,1,0:T(8,128)(2,1)S(1)}, bf16[1,4,128,7168]{3,2,1,0:T(8,128)(2,1)}, u32[]{:S(2)}) %copy-start.1) | copy-done | bytes 7340056
  41.4 2.1 %shard_map.138 = (bf16[2,128,2560]{2,1,0:T(8,128)(2,1)S(1)}, bf16[2,128,2560]{2,1,0:T(8,128)(2,1)S(1)}) custom-call(s32[2]{0:T(128)S(1)} %iota_xor_fusion.cols, bf16[256,512]{1,0:T(8,128)(2,1)S(1)} %shard_map.137.refs_0_, bf16[512,7168]{1,0:T(8,128)(2,1)S(1)} %bitcast.169), custom_call_target="tpu_custom_call" | custom-call | flops 1342177280 | bytes 7864320 | tf_op jit(solution)/shard_map/pallas_call | solution.py:160
  45.6 2.0 %collective-permute-done.1 = bf16[2,128,1024]{2,1,0:T(8,128)(2,1)S(1)} collective-permute-done((bf16[2,128,1024]{2,1,0:T(8,128)(2,1)S(1)}, bf16[2,128,1024]{2,1,0:T(8,128)(2,1)S(1)}, u32[]{:S(2)}, u32[]{:S(2)}) %collective-permute-start.1) | collective-permute-done | bytes 524320 | tf_op jit(solution)/shard_map/ppermute | solution.py:90
  48.1 2.0 %collective-permute-start.2 = (bf16[64,2560]{1,0:T(8,128)(2,1)S(1)}, bf16[64,2560]{1,0:T(8,128)(2,1)S(1)}, u32[]{:S(2)}, u32[]{:S(2)}) collective-permute-start(bf16[64,2560]{1,0:T(8,128)(2,1)S(1)} %get-tuple-element.67), channel_id=1, source_target_pairs={{0,4},{1,5},{2,6},{3,7},{4,0},{5,1},{6,2},{7,3},{8,12},{9,13},{10,... | collective-permute-start | bytes 983048 | tf_op jit(solution)/shard_map/ppermute | solution.py:90
  50.1 1.5 %collective-permute-start.3 = (bf16[64,2560]{1,0:T(8,128)(2,1)S(1)}, bf16[64,2560]{1,0:T(8,128)(2,1)S(1)}, u32[]{:S(2)}, u32[]{:S(2)}) collective-permute-start(bf16[64,2560]{1,0:T(8,128)(2,1)S(1)} %get-tuple-element.68), channel_id=1, source_target_pairs={{0,1},{1,0},{2,3},{3,2},{4,5},{5,4},{6,7},{7,6},{8,9},{9,8},{10,11... | collective-permute-start | bytes 983048 | tf_op jit(solution)/shard_map/ppermute | solution.py:90
  51.6 3.4 %collective-permute-start.5 = (bf16[4,16,1024]{2,1,0:T(8,128)(2,1)S(1)}, bf16[4,16,1024]{2,1,0:T(8,128)(2,1)S(1)}, u32[]{:S(2)}, u32[]{:S(2)}) collective-permute-start(bf16[4,16,1024]{2,1,0:T(8,128)(2,1)S(1)} %get-tuple-element.70), channel_id=1, source_target_pairs={{0,8},{1,9},{2,10},{3,11},{4,12},{5,13},{6,14},{7,15},{8,0},{9,1},... | collective-permute-start | bytes 393224 | tf_op jit(solution)/shard_map/ppermute | solution.py:90
  55.0 1.4 collective-permute-start.6
  56.4 2.2 %collective-permute-done.2 = bf16[64,2560]{1,0:T(8,128)(2,1)S(1)} collective-permute-done((bf16[64,2560]{1,0:T(8,128)(2,1)S(1)}, bf16[64,2560]{1,0:T(8,128)(2,1)S(1)}, u32[]{:S(2)}, u32[]{:S(2)}) %collective-permute-start.2) | collective-permute-done | bytes 327712 | tf_op jit(solution)/shard_map/ppermute | solution.py:90
  58.6 3.8 %collective-permute-start.7 = (bf16[4,16,1024]{2,1,0:T(8,128)(2,1)S(1)}, bf16[4,16,1024]{2,1,0:T(8,128)(2,1)S(1)}, u32[]{:S(2)}, u32[]{:S(2)}) collective-permute-start(bf16[4,16,1024]{2,1,0:T(8,128)(2,1)S(1)} %get-tuple-element.72), channel_id=1, source_target_pairs={{0,24},{1,25},{2,26},{3,27},{4,28},{5,29},{6,30},{7,31},{8,16},{9,... | collective-permute-start | bytes 393224 | tf_op jit(solution)/shard_map/ppermute | solution.py:90
  62.4 4.4 %collective-permute-done.3 = bf16[64,2560]{1,0:T(8,128)(2,1)S(1)} collective-permute-done((bf16[64,2560]{1,0:T(8,128)(2,1)S(1)}, bf16[64,2560]{1,0:T(8,128)(2,1)S(1)}, u32[]{:S(2)}, u32[]{:S(2)}) %collective-permute-start.3) | collective-permute-done | bytes 327712 | tf_op jit(solution)/shard_map/ppermute | solution.py:90
  68.6 2.9 %collective-permute-start.9 = (bf16[16,2560]{1,0:T(8,128)(2,1)S(1)}, bf16[16,2560]{1,0:T(8,128)(2,1)S(1)}, u32[]{:S(2)}, u32[]{:S(2)}) collective-permute-start(bf16[16,2560]{1,0:T(8,128)(2,1)S(1)} %get-tuple-element.78), channel_id=1, source_target_pairs={{0,8},{1,9},{2,10},{3,11},{4,12},{5,13},{6,14},{7,15},{8,0},{9,1},... | collective-permute-start | bytes 245768 | tf_op jit(solution)/shard_map/ppermute | solution.py:90
  71.5 1.4 collective-permute-start.10
  75.3 4.6 %collective-permute-done.10.refs_3_ = bf16[16,2560]{1,0:T(8,128)(2,1)S(1)} collective-permute-done((bf16[16,2560]{1,0:T(8,128)(2,1)S(1)}, bf16[16,2560]{1,0:T(8,128)(2,1)S(1)}, u32[]{:S(2)}, u32[]{:S(2)}) %collective-permute-start.10) | collective-permute-done | bytes 81952 | tf_op jit(solution)/shard_map/ppermute | solution.py:90
  81.3 2.0 %collective-permute-start.15 = (bf16[16,2816]{1,0:T(8,128)(2,1)S(1)}, bf16[16,2816]{1,0:T(8,128)(2,1)S(1)}, u32[]{:S(2)}, u32[]{:S(2)}) collective-permute-start(bf16[16,2816]{1,0:T(8,128)(2,1)S(1)} %get-tuple-element.88), channel_id=1, source_target_pairs={{0,24},{1,25},{2,26},{3,27},{4,28},{5,29},{6,30},{7,31},{8,16},{9,... | collective-permute-start | bytes 270344 | tf_op jit(solution)/shard_map/ppermute | solution.py:90
  84.2 1.5 collective-permute-start.13
  85.7 1.5 collective-permute-start.17
  88.1 2.0 %collective-permute-done.14 = bf16[16,2816]{1,0:T(8,128)(2,1)S(1)} collective-permute-done((bf16[16,2816]{1,0:T(8,128)(2,1)S(1)}, bf16[16,2816]{1,0:T(8,128)(2,1)S(1)}, u32[]{:S(2)}, u32[]{:S(2)}) %collective-permute-start.14) | collective-permute-done | bytes 90144 | tf_op jit(solution)/shard_map/ppermute | solution.py:90
  90.1 3.6 %collective-permute-done.17 = bf16[32,896]{1,0:T(8,128)(2,1)S(1)} collective-permute-done((bf16[32,896]{1,0:T(8,128)(2,1)S(1)}, bf16[32,896]{1,0:T(8,128)(2,1)S(1)}, u32[]{:S(2)}, u32[]{:S(2)}) %collective-permute-start.17) | collective-permute-done | bytes 57376 | tf_op jit(solution)/shard_map/ppermute | solution.py:90
  93.9 3.4 %collective-permute-start.18 = (bf16[64,2816]{1,0:T(8,128)(2,1)S(1)}, bf16[64,2816]{1,0:T(8,128)(2,1)S(1)}, u32[]{:S(2)}, u32[]{:S(2)}) collective-permute-start(bf16[64,2816]{1,0:T(8,128)(2,1)S(1)} %pad_maximum_fusion.refs_0_), channel_id=1, source_target_pairs={{0,4},{1,5},{2,6},{3,7},{4,0},{5,1},{6,2},{7,3},{8,12},{9,13},{10,... | collective-permute-start | bytes 1081352 | tf_op jit(solution)/shard_map/ppermute | solution.py:90
  97.3 5.7 %collective-permute-done.25 = bf16[64,896]{1,0:T(8,128)(2,1)S(1)} collective-permute-done((bf16[64,896]{1,0:T(8,128)(2,1)S(1)}, bf16[64,896]{1,0:T(8,128)(2,1)S(1)}, u32[]{:S(2)}, u32[]{:S(2)}) %collective-permute-start.25) | collective-permute-done | bytes 114720 | tf_op jit(solution)/shard_map/ppermute | solution.py:90
  107.2 3.9 %collective-permute-done.26.refs_9_ = bf16[128,896]{1,0:T(8,128)(2,1)S(1)} collective-permute-done((bf16[128,896]{1,0:T(8,128)(2,1)S(1)}, bf16[128,896]{1,0:T(8,128)(2,1)S(1)}, u32[]{:S(2)}, u32[]{:S(2)}) %collective-permute-start.26) | collective-permute-done | bytes 229408 | tf_op jit(solution)/shard_map/ppermute | solution.py:90
  111.1 1.5 collective-permute-done.28.refs_11_
  112.7 6.1 %shard_map.141 = (bf16[256,512]{1,0:T(8,128)(2,1)S(1)}, f32[256,128]{1,0:T(8,128)S(1)}, bf16[2,128,2560]{2,1,0:T(8,128)(2,1)S(1)}, bf16[2,128,2560]{2,1,0:T(8,128)(2,1)S(1)}) custom-call(s32[2]{0:T(128)S(1)} %iota_xor_fusion.cols, s32[1]{0:T(128)} %bitcast.2.me, bf16[64,2816]{1,0:T(8,128)(2,1)S(1)} %pad_maximum_fusion.refs_0_, ...), custom_call_target="tpu_custom_call" | custom-call | flops 5637144576 | bytes 22020096 | tf_op jit(solution)/shard_map/pallas_call | solution.py:253
  120.7 1.9 %collective-permute-done.30 = bf16[2,128,1024]{2,1,0:T(8,128)(2,1)S(1)} collective-permute-done((bf16[2,128,1024]{2,1,0:T(8,128)(2,1)S(1)}, bf16[2,128,1024]{2,1,0:T(8,128)(2,1)S(1)}, u32[]{:S(2)}, u32[]{:S(2)}) %collective-permute-start.30) | collective-permute-done | bytes 524320 | tf_op jit(solution)/shard_map/ppermute | solution.py:90
  123.7 2.8 %collective-permute-start.33 = (bf16[64,2560]{1,0:T(8,128)(2,1)S(1)}, bf16[64,2560]{1,0:T(8,128)(2,1)S(1)}, u32[]{:S(2)}, u32[]{:S(2)}) collective-permute-start(bf16[64,2560]{1,0:T(8,128)(2,1)S(1)} %get-tuple-element.102), channel_id=1, source_target_pairs={{0,5},{1,4},{2,7},{3,6},{4,1},{5,0},{6,3},{7,2},{8,13},{9,12},{10,... | collective-permute-start | bytes 983048 | tf_op jit(solution)/shard_map/ppermute | solution.py:90
  126.8 6.8 %collective-permute-done.31 = bf16[64,2560]{1,0:T(8,128)(2,1)S(1)} collective-permute-done((bf16[64,2560]{1,0:T(8,128)(2,1)S(1)}, bf16[64,2560]{1,0:T(8,128)(2,1)S(1)}, u32[]{:S(2)}, u32[]{:S(2)}) %collective-permute-start.31) | collective-permute-done | bytes 327712 | tf_op jit(solution)/shard_map/ppermute | solution.py:90
  133.6 6.3 %collective-permute-done.32 = bf16[64,2560]{1,0:T(8,128)(2,1)S(1)} collective-permute-done((bf16[64,2560]{1,0:T(8,128)(2,1)S(1)}, bf16[64,2560]{1,0:T(8,128)(2,1)S(1)}, u32[]{:S(2)}, u32[]{:S(2)}) %collective-permute-start.32) | collective-permute-done | bytes 327712 | tf_op jit(solution)/shard_map/ppermute | solution.py:90
  142.4 4.0 %collective-permute-start.39 = (bf16[16,2560]{1,0:T(8,128)(2,1)S(1)}, bf16[16,2560]{1,0:T(8,128)(2,1)S(1)}, u32[]{:S(2)}, u32[]{:S(2)}) collective-permute-start(bf16[16,2560]{1,0:T(8,128)(2,1)S(1)} %get-tuple-element.112), channel_id=1, source_target_pairs={{0,24},{1,25},{2,26},{3,27},{4,28},{5,29},{6,30},{7,31},{8,16},{9,... | collective-permute-start | bytes 245768 | tf_op jit(solution)/shard_map/ppermute | solution.py:90
  146.8 3.6 %collective-permute-done.38 = bf16[16,2560]{1,0:T(8,128)(2,1)S(1)} collective-permute-done((bf16[16,2560]{1,0:T(8,128)(2,1)S(1)}, bf16[16,2560]{1,0:T(8,128)(2,1)S(1)}, u32[]{:S(2)}, u32[]{:S(2)}) %collective-permute-start.38) | collective-permute-done | bytes 81952 | tf_op jit(solution)/shard_map/ppermute | solution.py:90
  (130 shorter events, 22.8 us)
Async XLA Ops:
  6.9 30.5 %all-to-all-start = ((bf16[64,16,512]{2,1,0:T(8,128)(2,1)}), bf16[64,16,512]{2,1,0:T(8,128)(2,1)S(1)}, u32[]{:S(2)}, u32[]{:S(2)}) async-start(bf16[64,16,512]{2,1,0:T(8,128)(2,1)} %shard_map.136), calls=%async_computation | async-start | bytes 2097152 | tf_op jit(solution)/shard_map/all_to_all | solution.py:448
  48.1 10.6 %collective-permute-start.2 = (bf16[64,2560]{1,0:T(8,128)(2,1)S(1)}, bf16[64,2560]{1,0:T(8,128)(2,1)S(1)}, u32[]{:S(2)}, u32[]{:S(2)}) collective-permute-start(bf16[64,2560]{1,0:T(8,128)(2,1)S(1)} %get-tuple-element.67), channel_id=1, source_target_pairs={{0,4},{1,5},{2,6},{3,7},{4,0},{5,1},{6,2},{7,3},{8,12},{9,13},{10,... | collective-permute-start | bytes 983048 | tf_op jit(solution)/shard_map/ppermute | solution.py:90
  50.1 16.7 %collective-permute-start.3 = (bf16[64,2560]{1,0:T(8,128)(2,1)S(1)}, bf16[64,2560]{1,0:T(8,128)(2,1)S(1)}, u32[]{:S(2)}, u32[]{:S(2)}) collective-permute-start(bf16[64,2560]{1,0:T(8,128)(2,1)S(1)} %get-tuple-element.68), channel_id=1, source_target_pairs={{0,1},{1,0},{2,3},{3,2},{4,5},{5,4},{6,7},{7,6},{8,9},{9,8},{10,11... | collective-permute-start | bytes 983048 | tf_op jit(solution)/shard_map/ppermute | solution.py:90
  51.6 15.2 %collective-permute-start.4 = (bf16[64,2560]{1,0:T(8,128)(2,1)S(1)}, bf16[64,2560]{1,0:T(8,128)(2,1)S(1)}, u32[]{:S(2)}, u32[]{:S(2)}) collective-permute-start(bf16[64,2560]{1,0:T(8,128)(2,1)S(1)} %get-tuple-element.69), channel_id=1, source_target_pairs={{0,5},{1,4},{2,7},{3,6},{4,1},{5,0},{6,3},{7,2},{8,13},{9,12},{10,... | collective-permute-start | bytes 983048 | tf_op jit(solution)/shard_map/ppermute | solution.py:90
  51.6 15.4 %collective-permute-start.5 = (bf16[4,16,1024]{2,1,0:T(8,128)(2,1)S(1)}, bf16[4,16,1024]{2,1,0:T(8,128)(2,1)S(1)}, u32[]{:S(2)}, u32[]{:S(2)}) collective-permute-start(bf16[4,16,1024]{2,1,0:T(8,128)(2,1)S(1)} %get-tuple-element.70), channel_id=1, source_target_pairs={{0,8},{1,9},{2,10},{3,11},{4,12},{5,13},{6,14},{7,15},{8,0},{9,1},... | collective-permute-start | bytes 393224 | tf_op jit(solution)/shard_map/ppermute | solution.py:90
  55.0 12.0 %collective-permute-start.6 = (bf16[4,16,1024]{2,1,0:T(8,128)(2,1)S(1)}, bf16[4,16,1024]{2,1,0:T(8,128)(2,1)S(1)}, u32[]{:S(2)}, u32[]{:S(2)}) collective-permute-start(bf16[4,16,1024]{2,1,0:T(8,128)(2,1)S(1)} %get-tuple-element.71), channel_id=1, source_target_pairs={{0,16},{1,17},{2,18},{3,19},{4,20},{5,21},{6,22},{7,23},{8,24},{9,... | collective-permute-start | bytes 393224 | tf_op jit(solution)/shard_map/ppermute | solution.py:90
  58.6 8.4 %collective-permute-start.7 = (bf16[4,16,1024]{2,1,0:T(8,128)(2,1)S(1)}, bf16[4,16,1024]{2,1,0:T(8,128)(2,1)S(1)}, u32[]{:S(2)}, u32[]{:S(2)}) collective-permute-start(bf16[4,16,1024]{2,1,0:T(8,128)(2,1)S(1)} %get-tuple-element.72), channel_id=1, source_target_pairs={{0,24},{1,25},{2,26},{3,27},{4,28},{5,29},{6,30},{7,31},{8,16},{9,... | collective-permute-start | bytes 393224 | tf_op jit(solution)/shard_map/ppermute | solution.py:90
  67.3 6.6 %collective-permute-start.8 = (bf16[2,16,1024]{2,1,0:T(8,128)(2,1)S(1)}, bf16[2,16,1024]{2,1,0:T(8,128)(2,1)S(1)}, u32[]{:S(2)}, u32[]{:S(2)}) collective-permute-start(bf16[2,16,1024]{2,1,0:T(8,128)(2,1)S(1)} %pad_maximum_fusion.3), channel_id=1, source_target_pairs={{0,4},{1,5},{2,6},{3,7},{4,0},{5,1},{6,2},{7,3},{8,12},{9,13},{10,... | collective-permute-start | bytes 196616 | tf_op jit(solution)/shard_map/ppermute | solution.py:90
  68.6 6.7 %collective-permute-start.9 = (bf16[16,2560]{1,0:T(8,128)(2,1)S(1)}, bf16[16,2560]{1,0:T(8,128)(2,1)S(1)}, u32[]{:S(2)}, u32[]{:S(2)}) collective-permute-start(bf16[16,2560]{1,0:T(8,128)(2,1)S(1)} %get-tuple-element.78), channel_id=1, source_target_pairs={{0,8},{1,9},{2,10},{3,11},{4,12},{5,13},{6,14},{7,15},{8,0},{9,1},... | collective-permute-start | bytes 245768 | tf_op jit(solution)/shard_map/ppermute | solution.py:90
  71.5 8.5 %collective-permute-start.10 = (bf16[16,2560]{1,0:T(8,128)(2,1)S(1)}, bf16[16,2560]{1,0:T(8,128)(2,1)S(1)}, u32[]{:S(2)}, u32[]{:S(2)}) collective-permute-start(bf16[16,2560]{1,0:T(8,128)(2,1)S(1)} %get-tuple-element.79), channel_id=1, source_target_pairs={{0,16},{1,17},{2,18},{3,19},{4,20},{5,21},{6,22},{7,23},{8,24},{9,... | collective-permute-start | bytes 245768 | tf_op jit(solution)/shard_map/ppermute | solution.py:90
  72.9 7.0 %collective-permute-start.11 = (bf16[16,2560]{1,0:T(8,128)(2,1)S(1)}, bf16[16,2560]{1,0:T(8,128)(2,1)S(1)}, u32[]{:S(2)}, u32[]{:S(2)}) collective-permute-start(bf16[16,2560]{1,0:T(8,128)(2,1)S(1)} %get-tuple-element.80), channel_id=1, source_target_pairs={{0,24},{1,25},{2,26},{3,27},{4,28},{5,29},{6,30},{7,31},{8,16},{9,... | collective-permute-start | bytes 245768 | tf_op jit(solution)/shard_map/ppermute | solution.py:90
  73.8 6.1 %collective-permute-start.12 = (bf16[1,16,1024]{2,1,0:T(8,128)(2,1)S(1)}, bf16[1,16,1024]{2,1,0:T(8,128)(2,1)S(1)}, u32[]{:S(2)}, u32[]{:S(2)}) collective-permute-start(bf16[1,16,1024]{2,1,0:T(8,128)(2,1)S(1)} %get-tuple-element.134), channel_id=1, source_target_pairs={{0,1},{1,0},{2,3},{3,2},{4,5},{5,4},{6,7},{7,6},{8,9},{9,8},{10,11... | collective-permute-start | bytes 98312 | tf_op jit(solution)/shard_map/ppermute | solution.py:90
  81.3 6.8 %collective-permute-start.15 = (bf16[16,2816]{1,0:T(8,128)(2,1)S(1)}, bf16[16,2816]{1,0:T(8,128)(2,1)S(1)}, u32[]{:S(2)}, u32[]{:S(2)}) collective-permute-start(bf16[16,2816]{1,0:T(8,128)(2,1)S(1)} %get-tuple-element.88), channel_id=1, source_target_pairs={{0,24},{1,25},{2,26},{3,27},{4,28},{5,29},{6,30},{7,31},{8,16},{9,... | collective-permute-start | bytes 270344 | tf_op jit(solution)/shard_map/ppermute | solution.py:90
  83.2 6.8 %collective-permute-start.14 = (bf16[16,2816]{1,0:T(8,128)(2,1)S(1)}, bf16[16,2816]{1,0:T(8,128)(2,1)S(1)}, u32[]{:S(2)}, u32[]{:S(2)}) collective-permute-start(bf16[16,2816]{1,0:T(8,128)(2,1)S(1)} %get-tuple-element.88), channel_id=1, source_target_pairs={{0,16},{1,17},{2,18},{3,19},{4,20},{5,21},{6,22},{7,23},{8,24},{9,... | collective-permute-start | bytes 270344 | tf_op jit(solution)/shard_map/ppermute | solution.py:90
  84.2 6.0 %collective-permute-start.13 = (bf16[16,2816]{1,0:T(8,128)(2,1)S(1)}, bf16[16,2816]{1,0:T(8,128)(2,1)S(1)}, u32[]{:S(2)}, u32[]{:S(2)}) collective-permute-start(bf16[16,2816]{1,0:T(8,128)(2,1)S(1)} %get-tuple-element.88), channel_id=1, source_target_pairs={{0,8},{1,9},{2,10},{3,11},{4,12},{5,13},{6,14},{7,15},{8,0},{9,1},... | collective-permute-start | bytes 270344 | tf_op jit(solution)/shard_map/ppermute | solution.py:90
  85.7 8.1 %collective-permute-start.17 = (bf16[32,896]{1,0:T(8,128)(2,1)S(1)}, bf16[32,896]{1,0:T(8,128)(2,1)S(1)}, u32[]{:S(2)}, u32[]{:S(2)}) collective-permute-start(bf16[32,896]{1,0:T(8,128)(2,1)S(1)} %pad_maximum_fusion.5), channel_id=1, source_target_pairs={{0,1},{1,0},{2,3},{3,2},{4,5},{5,4},{6,7},{7,6},{8,9},{9,8},{10,11... | collective-permute-start | bytes 172040 | tf_op jit(solution)/shard_map/ppermute | solution.py:90
  93.8 11.0 %collective-permute-start.20 = (bf16[64,2816]{1,0:T(8,128)(2,1)S(1)}, bf16[64,2816]{1,0:T(8,128)(2,1)S(1)}, u32[]{:S(2)}, u32[]{:S(2)}) collective-permute-start(bf16[64,2816]{1,0:T(8,128)(2,1)S(1)} %pad_maximum_fusion.refs_0_), channel_id=1, source_target_pairs={{0,5},{1,4},{2,7},{3,6},{4,1},{5,0},{6,3},{7,2},{8,13},{9,12},{10,... | collective-permute-start | bytes 1081352 | tf_op jit(solution)/shard_map/ppermute | solution.py:90
  93.8 12.3 %collective-permute-start.19 = (bf16[64,2816]{1,0:T(8,128)(2,1)S(1)}, bf16[64,2816]{1,0:T(8,128)(2,1)S(1)}, u32[]{:S(2)}, u32[]{:S(2)}) collective-permute-start(bf16[64,2816]{1,0:T(8,128)(2,1)S(1)} %pad_maximum_fusion.refs_0_), channel_id=1, source_target_pairs={{0,1},{1,0},{2,3},{3,2},{4,5},{5,4},{6,7},{7,6},{8,9},{9,8},{10,11... | collective-permute-start | bytes 1081352 | tf_op jit(solution)/shard_map/ppermute | solution.py:90
  93.9 13.3 %collective-permute-start.18 = (bf16[64,2816]{1,0:T(8,128)(2,1)S(1)}, bf16[64,2816]{1,0:T(8,128)(2,1)S(1)}, u32[]{:S(2)}, u32[]{:S(2)}) collective-permute-start(bf16[64,2816]{1,0:T(8,128)(2,1)S(1)} %pad_maximum_fusion.refs_0_), channel_id=1, source_target_pairs={{0,4},{1,5},{2,6},{3,7},{4,0},{5,1},{6,2},{7,3},{8,12},{9,13},{10,... | collective-permute-start | bytes 1081352 | tf_op jit(solution)/shard_map/ppermute | solution.py:90
  103.1 8.0 %collective-permute-start.26 = (bf16[128,896]{1,0:T(8,128)(2,1)S(1)}, bf16[128,896]{1,0:T(8,128)(2,1)S(1)}, u32[]{:S(2)}, u32[]{:S(2)}) collective-permute-start(bf16[128,896]{1,0:T(8,128)(2,1)S(1)} %constant_dynamic-update-slice_fusion.refs_8_), channel_id=1, source_target_pairs={{0,8},{1,9},{2,10},{3,11},{4,12},{5,13},{6,14},{7,15},{8,0},{9,1},... | collective-permute-start | bytes 688136 | tf_op jit(solution)/shard_map/ppermute | solution.py:90
  104.6 6.6 %collective-permute-start.21 = (bf16[64,2816]{1,0:T(8,128)(2,1)S(1)}, bf16[64,2816]{1,0:T(8,128)(2,1)S(1)}, u32[]{:S(2)}, u32[]{:S(2)}) collective-permute-start(bf16[64,2816]{1,0:T(8,128)(2,1)S(1)} %pad_maximum_fusion.refs_0_), channel_id=1, source_target_pairs={{0,2},{1,3},{2,0},{3,1},{4,6},{5,7},{6,4},{7,5},{8,10},{9,11},{10,... | collective-permute-start | bytes 1081352 | tf_op jit(solution)/shard_map/ppermute | solution.py:90
  104.7 7.9 %collective-permute-start.24 = (bf16[64,2816]{1,0:T(8,128)(2,1)S(1)}, bf16[64,2816]{1,0:T(8,128)(2,1)S(1)}, u32[]{:S(2)}, u32[]{:S(2)}) collective-permute-start(bf16[64,2816]{1,0:T(8,128)(2,1)S(1)} %collective-permute-done.20.refs_3_), channel_id=1, source_target_pairs={{0,2},{1,3},{2,0},{3,1},{4,6},{5,7},{6,4},{7,5},{8,10},{9,11},{10,... | collective-permute-start | bytes 1081352 | tf_op jit(solution)/shard_map/ppermute | solution.py:90
  106.2 6.5 %collective-permute-start.23 = (bf16[64,2816]{1,0:T(8,128)(2,1)S(1)}, bf16[64,2816]{1,0:T(8,128)(2,1)S(1)}, u32[]{:S(2)}, u32[]{:S(2)}) collective-permute-start(bf16[64,2816]{1,0:T(8,128)(2,1)S(1)} %collective-permute-done.19.refs_2_), channel_id=1, source_target_pairs={{0,2},{1,3},{2,0},{3,1},{4,6},{5,7},{6,4},{7,5},{8,10},{9,11},{10,... | collective-permute-start | bytes 1081352 | tf_op jit(solution)/shard_map/ppermute | solution.py:90
  123.0 10.6 %collective-permute-start.31 = (bf16[64,2560]{1,0:T(8,128)(2,1)S(1)}, bf16[64,2560]{1,0:T(8,128)(2,1)S(1)}, u32[]{:S(2)}, u32[]{:S(2)}) collective-permute-start(bf16[64,2560]{1,0:T(8,128)(2,1)S(1)} %get-tuple-element.100), channel_id=1, source_target_pairs={{0,4},{1,5},{2,6},{3,7},{4,0},{5,1},{6,2},{7,3},{8,12},{9,13},{10,... | collective-permute-start | bytes 983048 | tf_op jit(solution)/shard_map/ppermute | solution.py:90
  123.1 16.8 %collective-permute-start.32 = (bf16[64,2560]{1,0:T(8,128)(2,1)S(1)}, bf16[64,2560]{1,0:T(8,128)(2,1)S(1)}, u32[]{:S(2)}, u32[]{:S(2)}) collective-permute-start(bf16[64,2560]{1,0:T(8,128)(2,1)S(1)} %get-tuple-element.101), channel_id=1, source_target_pairs={{0,1},{1,0},{2,3},{3,2},{4,5},{5,4},{6,7},{7,6},{8,9},{9,8},{10,11... | collective-permute-start | bytes 983048 | tf_op jit(solution)/shard_map/ppermute | solution.py:90
  123.7 16.2 %collective-permute-start.33 = (bf16[64,2560]{1,0:T(8,128)(2,1)S(1)}, bf16[64,2560]{1,0:T(8,128)(2,1)S(1)}, u32[]{:S(2)}, u32[]{:S(2)}) collective-permute-start(bf16[64,2560]{1,0:T(8,128)(2,1)S(1)} %get-tuple-element.102), channel_id=1, source_target_pairs={{0,5},{1,4},{2,7},{3,6},{4,1},{5,0},{6,3},{7,2},{8,13},{9,12},{10,... | collective-permute-start | bytes 983048 | tf_op jit(solution)/shard_map/ppermute | solution.py:90
  126.6 13.6 %collective-permute-start.34 = (bf16[4,16,1024]{2,1,0:T(8,128)(2,1)S(1)}, bf16[4,16,1024]{2,1,0:T(8,128)(2,1)S(1)}, u32[]{:S(2)}, u32[]{:S(2)}) collective-permute-start(bf16[4,16,1024]{2,1,0:T(8,128)(2,1)S(1)} %get-tuple-element.103), channel_id=1, source_target_pairs={{0,8},{1,9},{2,10},{3,11},{4,12},{5,13},{6,14},{7,15},{8,0},{9,1},... | collective-permute-start | bytes 393224 | tf_op jit(solution)/shard_map/ppermute | solution.py:90
  126.8 13.3 %collective-permute-start.35 = (bf16[4,16,1024]{2,1,0:T(8,128)(2,1)S(1)}, bf16[4,16,1024]{2,1,0:T(8,128)(2,1)S(1)}, u32[]{:S(2)}, u32[]{:S(2)}) collective-permute-start(bf16[4,16,1024]{2,1,0:T(8,128)(2,1)S(1)} %get-tuple-element.104), channel_id=1, source_target_pairs={{0,16},{1,17},{2,18},{3,19},{4,20},{5,21},{6,22},{7,23},{8,24},{9,... | collective-permute-start | bytes 393224 | tf_op jit(solution)/shard_map/ppermute | solution.py:90
  133.6 6.9 %collective-permute-start.36 = (bf16[4,16,1024]{2,1,0:T(8,128)(2,1)S(1)}, bf16[4,16,1024]{2,1,0:T(8,128)(2,1)S(1)}, u32[]{:S(2)}, u32[]{:S(2)}) collective-permute-start(bf16[4,16,1024]{2,1,0:T(8,128)(2,1)S(1)} %get-tuple-element.105), channel_id=1, source_target_pairs={{0,24},{1,25},{2,26},{3,27},{4,28},{5,29},{6,30},{7,31},{8,16},{9,... | collective-permute-start | bytes 393224 | tf_op jit(solution)/shard_map/ppermute | solution.py:90
  140.7 5.8 %collective-permute-start.40 = (bf16[2,16,1024]{2,1,0:T(8,128)(2,1)S(1)}, bf16[2,16,1024]{2,1,0:T(8,128)(2,1)S(1)}, u32[]{:S(2)}, u32[]{:S(2)}) collective-permute-start(bf16[2,16,1024]{2,1,0:T(8,128)(2,1)S(1)} %pad_maximum_fusion.4), channel_id=1, source_target_pairs={{0,4},{1,5},{2,6},{3,7},{4,0},{5,1},{6,2},{7,3},{8,12},{9,13},{10,... | collective-permute-start | bytes 196616 | tf_op jit(solution)/shard_map/ppermute | solution.py:90
  142.4 8.1 %collective-permute-start.38 = (bf16[16,2560]{1,0:T(8,128)(2,1)S(1)}, bf16[16,2560]{1,0:T(8,128)(2,1)S(1)}, u32[]{:S(2)}, u32[]{:S(2)}) collective-permute-start(bf16[16,2560]{1,0:T(8,128)(2,1)S(1)} %get-tuple-element.111), channel_id=1, source_target_pairs={{0,16},{1,17},{2,18},{3,19},{4,20},{5,21},{6,22},{7,23},{8,24},{9,... | collective-permute-start | bytes 245768 | tf_op jit(solution)/shard_map/ppermute | solution.py:90
  142.4 8.0 %collective-permute-start.39 = (bf16[16,2560]{1,0:T(8,128)(2,1)S(1)}, bf16[16,2560]{1,0:T(8,128)(2,1)S(1)}, u32[]{:S(2)}, u32[]{:S(2)}) collective-permute-start(bf16[16,2560]{1,0:T(8,128)(2,1)S(1)} %get-tuple-element.112), channel_id=1, source_target_pairs={{0,24},{1,25},{2,26},{3,27},{4,28},{5,29},{6,30},{7,31},{8,16},{9,... | collective-permute-start | bytes 245768 | tf_op jit(solution)/shard_map/ppermute | solution.py:90
  (24 other events, 449.9 us)

commit v5 on v4

--- a/solution.py
+++ b/solution.py
@@ -396,7 +396,6 @@
         if bit == net.plane_bits - 1:
             held_a, last = lax.optimization_barrier((held_a, last))
         held_b = jnp.concatenate([held_b, last], 0)
-    held_a, held_b = lax.optimization_barrier((held_a, held_b))
     for bit in reversed(range(1, net.line_bits)):
         held_b = jnp.concatenate([held_b, net.in_line(held_b, 1 << bit)], 0)
     own_a = [held_a] + [net.in_plane(held_a, at) for at in range(1, places)]

time: 151 us -> 151 us (level)
  waiting for transfers between devices: 75.1 us -> 69.2 us
  starting transfers between devices: 50.5 us -> 55.6 us
    ppermute x42, waiting for transfers between devices: 53.3 us -> 47.4 us  [move(): lax.ppermute(value, ('dp', 'heads'), [(i, i ^ mask) for i in range(count)])]
    ppermute x42, starting transfers between devices: 42.8 us -> 47.9 us  [move(): lax.ppermute(value, ('dp', 'heads'), [(i, i ^ mask) for i in range(count)])]
    unnamed x29 -> x31, local copies, waits for them, and re-layouts: 3.29 us -> 3.31 us
  transfers between devices with their start and end apart: 43 -> 43, of which waited for: 19 -> 17; matrix products, arithmetic and copies ran while one was open for 1% -> 1% of each run, Pallas kernels for 2% -> 2%
where the time goes in v5:
time: 151 us; the launch traced here: 150 us
  waiting for transfers between devices  69.2 us (46%)
  starting transfers between devices  55.6 us (37%)
  Pallas kernels  18.8 us (12%)
  local copies, waits for them, and re-layouts  3.53 us (2%)
  other arithmetic  2.81 us (2%)
    ppermute x42, starting transfers between devices, move(): lax.ppermute(value, ('dp', 'heads'), [(i, i ^ mask) for i in range(count)])  47.9 us
    ppermute x42, waiting for transfers between devices, move(): lax.ppermute(value, ('dp', 'heads'), [(i, i ^ mask) for i in range(count)])  47.4 us
    all_to_all x1, waiting for transfers between devices, on_device(): lax.all_to_all(latent_out, 'dp', split_axis=0, concat_axis=0, tiled=True)  21.8 us
    all_to_all x1, starting transfers between devices, on_device(): lax.all_to_all(latent_out, 'dp', split_axis=0, concat_axis=0, tiled=True)  7.68 us
    pallas_call x1, Pallas kernels, attend(): pl.pallas_call(functools.partial(attend_kernel, rows=rows, latent=LAT), g...  6.88 us
    pallas_call x1, Pallas kernels, experts_of(): pl.pallas_call(functools.partial(expert_kernel, net=net, groups=(len(piec...  6.06 us
    pallas_call x3, Pallas kernels, project(): pl.pallas_call(functools.partial(project_kernel, tile=tile, first=first,...  4.72 us
    unnamed x31, local copies, waits for them, and re-layouts  3.31 us
  transfers between devices with their start and end apart: 43, of which 17 were waited for; matrix products, arithmetic and copies ran while one was open for 1% of the time, Pallas kernels for 2%

profile of v5, /device:TPU:0, one launch (start us, length us, event | category | flops | bytes accessed | tf_op | source)
XLA Modules:
  0.0 150.4 jit_solution(9532405463954815337)
XLA Ops:
  0.0 6.9 %shard_map.136 = bf16[64,16,512]{2,1,0:T(8,128)(2,1)} custom-call(s32[16]{0:T(128)} %lengths.1, bf16[16,64,576]{2,1,0:T(8,128)(2,1)} %q_ref.1, bf16[16,576,256]{2,1,0:T(8,128)(2,1)} %bitcast.190), custom_call_target="tpu_custom_call" | custom-call | tf_op jit(solution)/shard_map/pallas_call | solution.py:59
  6.9 7.7 %all-to-all-start = ((bf16[64,16,512]{2,1,0:T(8,128)(2,1)}), bf16[64,16,512]{2,1,0:T(8,128)(2,1)S(1)}, u32[]{:S(2)}, u32[]{:S(2)}) async-start(bf16[64,16,512]{2,1,0:T(8,128)(2,1)} %shard_map.136), calls=%async_computation | async-start | bytes 2097152 | tf_op jit(solution)/shard_map/all_to_all | solution.py:447
  15.6 21.8 %all-to-all-done = bf16[64,16,512]{2,1,0:T(8,128)(2,1)S(1)} async-done(((bf16[64,16,512]{2,1,0:T(8,128)(2,1)}), bf16[64,16,512]{2,1,0:T(8,128)(2,1)S(1)}, u32[]{:S(2)}, u32[]{:S(2)}) %all-to-all-start) | async-done | bytes 1048608 | tf_op jit(solution)/shard_map/all_to_all | solution.py:447
  38.4 3.1 %copy-done.1 = bf16[1,4,128,7168]{3,2,1,0:T(8,128)(2,1)S(1)} copy-done((bf16[1,4,128,7168]{3,2,1,0:T(8,128)(2,1)S(1)}, bf16[1,4,128,7168]{3,2,1,0:T(8,128)(2,1)}, u32[]{:S(2)}) %copy-start.1) | copy-done | bytes 7340056
  41.4 2.1 %shard_map.138 = (bf16[2,128,2560]{2,1,0:T(8,128)(2,1)S(1)}, bf16[2,128,2560]{2,1,0:T(8,128)(2,1)S(1)}) custom-call(s32[2]{0:T(128)S(1)} %iota_xor_fusion.cols, bf16[256,512]{1,0:T(8,128)(2,1)S(1)} %shard_map.137.refs_0_, bf16[512,7168]{1,0:T(8,128)(2,1)S(1)} %bitcast.169), custom_call_target="tpu_custom_call" | custom-call | flops 1342177280 | bytes 7864320 | tf_op jit(solution)/shard_map/pallas_call | solution.py:160
  45.6 2.0 %collective-permute-done.1 = bf16[2,128,1024]{2,1,0:T(8,128)(2,1)S(1)} collective-permute-done((bf16[2,128,1024]{2,1,0:T(8,128)(2,1)S(1)}, bf16[2,128,1024]{2,1,0:T(8,128)(2,1)S(1)}, u32[]{:S(2)}, u32[]{:S(2)}) %collective-permute-start.1) | collective-permute-done | bytes 524320 | tf_op jit(solution)/shard_map/ppermute | solution.py:90
  48.1 2.0 %collective-permute-start.2 = (bf16[64,2560]{1,0:T(8,128)(2,1)S(1)}, bf16[64,2560]{1,0:T(8,128)(2,1)S(1)}, u32[]{:S(2)}, u32[]{:S(2)}) collective-permute-start(bf16[64,2560]{1,0:T(8,128)(2,1)S(1)} %get-tuple-element.65), channel_id=1, source_target_pairs={{0,4},{1,5},{2,6},{3,7},{4,0},{5,1},{6,2},{7,3},{8,12},{9,13},{10,... | collective-permute-start | bytes 983048 | tf_op jit(solution)/shard_map/ppermute | solution.py:90
  50.1 1.5 %collective-permute-start.3 = (bf16[64,2560]{1,0:T(8,128)(2,1)S(1)}, bf16[64,2560]{1,0:T(8,128)(2,1)S(1)}, u32[]{:S(2)}, u32[]{:S(2)}) collective-permute-start(bf16[64,2560]{1,0:T(8,128)(2,1)S(1)} %get-tuple-element.66), channel_id=1, source_target_pairs={{0,1},{1,0},{2,3},{3,2},{4,5},{5,4},{6,7},{7,6},{8,9},{9,8},{10,11... | collective-permute-start | bytes 983048 | tf_op jit(solution)/shard_map/ppermute | solution.py:90
  51.6 3.4 %collective-permute-start.5 = (bf16[4,16,1024]{2,1,0:T(8,128)(2,1)S(1)}, bf16[4,16,1024]{2,1,0:T(8,128)(2,1)S(1)}, u32[]{:S(2)}, u32[]{:S(2)}) collective-permute-start(bf16[4,16,1024]{2,1,0:T(8,128)(2,1)S(1)} %get-tuple-element.68), channel_id=1, source_target_pairs={{0,8},{1,9},{2,10},{3,11},{4,12},{5,13},{6,14},{7,15},{8,0},{9,1},... | collective-permute-start | bytes 393224 | tf_op jit(solution)/shard_map/ppermute | solution.py:90
  56.4 2.2 %collective-permute-done.2 = bf16[64,2560]{1,0:T(8,128)(2,1)S(1)} collective-permute-done((bf16[64,2560]{1,0:T(8,128)(2,1)S(1)}, bf16[64,2560]{1,0:T(8,128)(2,1)S(1)}, u32[]{:S(2)}, u32[]{:S(2)}) %collective-permute-start.2) | collective-permute-done | bytes 327712 | tf_op jit(solution)/shard_map/ppermute | solution.py:90
  58.6 3.8 %collective-permute-start.7 = (bf16[4,16,1024]{2,1,0:T(8,128)(2,1)S(1)}, bf16[4,16,1024]{2,1,0:T(8,128)(2,1)S(1)}, u32[]{:S(2)}, u32[]{:S(2)}) collective-permute-start(bf16[4,16,1024]{2,1,0:T(8,128)(2,1)S(1)} %get-tuple-element.70), channel_id=1, source_target_pairs={{0,24},{1,25},{2,26},{3,27},{4,28},{5,29},{6,30},{7,31},{8,16},{9,... | collective-permute-start | bytes 393224 | tf_op jit(solution)/shard_map/ppermute | solution.py:90
  62.4 4.4 %collective-permute-done.3 = bf16[64,2560]{1,0:T(8,128)(2,1)S(1)} collective-permute-done((bf16[64,2560]{1,0:T(8,128)(2,1)S(1)}, bf16[64,2560]{1,0:T(8,128)(2,1)S(1)}, u32[]{:S(2)}, u32[]{:S(2)}) %collective-permute-start.3) | collective-permute-done | bytes 327712 | tf_op jit(solution)/shard_map/ppermute | solution.py:90
  68.6 2.9 %collective-permute-start.9 = (bf16[16,2560]{1,0:T(8,128)(2,1)S(1)}, bf16[16,2560]{1,0:T(8,128)(2,1)S(1)}, u32[]{:S(2)}, u32[]{:S(2)}) collective-permute-start(bf16[16,2560]{1,0:T(8,128)(2,1)S(1)} %get-tuple-element.76), channel_id=1, source_target_pairs={{0,8},{1,9},{2,10},{3,11},{4,12},{5,13},{6,14},{7,15},{8,0},{9,1},... | collective-permute-start | bytes 245768 | tf_op jit(solution)/shard_map/ppermute | solution.py:90
  75.3 4.6 %collective-permute-done.10.refs_3_ = bf16[16,2560]{1,0:T(8,128)(2,1)S(1)} collective-permute-done((bf16[16,2560]{1,0:T(8,128)(2,1)S(1)}, bf16[16,2560]{1,0:T(8,128)(2,1)S(1)}, u32[]{:S(2)}, u32[]{:S(2)}) %collective-permute-start.10) | collective-permute-done | bytes 81952 | tf_op jit(solution)/shard_map/ppermute | solution.py:90
  80.1 1.8 %collective-permute-start.15 = (bf16[16,2816]{1,0:T(8,128)(2,1)S(1)}, bf16[16,2816]{1,0:T(8,128)(2,1)S(1)}, u32[]{:S(2)}, u32[]{:S(2)}) collective-permute-start(bf16[16,2816]{1,0:T(8,128)(2,1)S(1)} %get-tuple-element.86), channel_id=1, source_target_pairs={{0,24},{1,25},{2,26},{3,27},{4,28},{5,29},{6,30},{7,31},{8,16},{9,... | collective-permute-start | bytes 270344 | tf_op jit(solution)/shard_map/ppermute | solution.py:90
  83.0 1.5 collective-permute-start.13
  85.6 2.7 %collective-permute-done.16 = bf16[16,896]{1,0:T(8,128)(2,1)S(1)} collective-permute-done((bf16[16,896]{1,0:T(8,128)(2,1)S(1)}, bf16[16,896]{1,0:T(8,128)(2,1)S(1)}, u32[]{:S(2)}, u32[]{:S(2)}) %collective-permute-start.16) | collective-permute-done | bytes 28704 | tf_op jit(solution)/shard_map/ppermute | solution.py:90
  89.8 2.7 %collective-permute-done.17 = bf16[32,896]{1,0:T(8,128)(2,1)S(1)} collective-permute-done((bf16[32,896]{1,0:T(8,128)(2,1)S(1)}, bf16[32,896]{1,0:T(8,128)(2,1)S(1)}, u32[]{:S(2)}, u32[]{:S(2)}) %collective-permute-start.17) | collective-permute-done | bytes 57376 | tf_op jit(solution)/shard_map/ppermute | solution.py:90
  93.5 2.3 %collective-permute-start.20 = (bf16[64,2816]{1,0:T(8,128)(2,1)S(1)}, bf16[64,2816]{1,0:T(8,128)(2,1)S(1)}, u32[]{:S(2)}, u32[]{:S(2)}) collective-permute-start(bf16[64,2816]{1,0:T(8,128)(2,1)S(1)} %pad_maximum_fusion.refs_0_), channel_id=1, source_target_pairs={{0,5},{1,4},{2,7},{3,6},{4,1},{5,0},{6,3},{7,2},{8,13},{9,12},{10,... | collective-permute-start | bytes 1081352 | tf_op jit(solution)/shard_map/ppermute | solution.py:90
  97.0 2.5 %collective-permute-done.25 = bf16[64,896]{1,0:T(8,128)(2,1)S(1)} collective-permute-done((bf16[64,896]{1,0:T(8,128)(2,1)S(1)}, bf16[64,896]{1,0:T(8,128)(2,1)S(1)}, u32[]{:S(2)}, u32[]{:S(2)}) %collective-permute-start.25) | collective-permute-done | bytes 114720 | tf_op jit(solution)/shard_map/ppermute | solution.py:90
  101.2 3.5 %collective-permute-done.20.refs_3_ = bf16[64,2816]{1,0:T(8,128)(2,1)S(1)} collective-permute-done((bf16[64,2816]{1,0:T(8,128)(2,1)S(1)}, bf16[64,2816]{1,0:T(8,128)(2,1)S(1)}, u32[]{:S(2)}, u32[]{:S(2)}) %collective-permute-start.20) | collective-permute-done | bytes 360480 | tf_op jit(solution)/shard_map/ppermute | solution.py:90
  104.7 3.7 %collective-permute-done.19.refs_2_ = bf16[64,2816]{1,0:T(8,128)(2,1)S(1)} collective-permute-done((bf16[64,2816]{1,0:T(8,128)(2,1)S(1)}, bf16[64,2816]{1,0:T(8,128)(2,1)S(1)}, u32[]{:S(2)}, u32[]{:S(2)}) %collective-permute-start.19) | collective-permute-done | bytes 360480 | tf_op jit(solution)/shard_map/ppermute | solution.py:90
  109.0 1.9 %collective-permute-done.28.refs_11_ = bf16[128,896]{1,0:T(8,128)(2,1)S(1)} collective-permute-done((bf16[128,896]{1,0:T(8,128)(2,1)S(1)}, bf16[128,896]{1,0:T(8,128)(2,1)S(1)}, u32[]{:S(2)}, u32[]{:S(2)}) %collective-permute-start.28) | collective-permute-done | bytes 229408 | tf_op jit(solution)/shard_map/ppermute | solution.py:90
  111.0 6.1 %shard_map.141 = (bf16[256,512]{1,0:T(8,128)(2,1)S(1)}, f32[256,128]{1,0:T(8,128)S(1)}, bf16[2,128,2560]{2,1,0:T(8,128)(2,1)S(1)}, bf16[2,128,2560]{2,1,0:T(8,128)(2,1)S(1)}) custom-call(s32[2]{0:T(128)S(1)} %iota_xor_fusion.cols, s32[1]{0:T(128)} %bitcast.2.me, bf16[64,2816]{1,0:T(8,128)(2,1)S(1)} %pad_maximum_fusion.refs_0_, ...), custom_call_target="tpu_custom_call" | custom-call | flops 5637144576 | bytes 22020096 | tf_op jit(solution)/shard_map/pallas_call | solution.py:253
  119.0 1.9 %collective-permute-done.30 = bf16[2,128,1024]{2,1,0:T(8,128)(2,1)S(1)} collective-permute-done((bf16[2,128,1024]{2,1,0:T(8,128)(2,1)S(1)}, bf16[2,128,1024]{2,1,0:T(8,128)(2,1)S(1)}, u32[]{:S(2)}, u32[]{:S(2)}) %collective-permute-start.30) | collective-permute-done | bytes 524320 | tf_op jit(solution)/shard_map/ppermute | solution.py:90
  125.7 1.5 collective-permute-start.35
  127.2 4.7 %collective-permute-done.31 = bf16[64,2560]{1,0:T(8,128)(2,1)S(1)} collective-permute-done((bf16[64,2560]{1,0:T(8,128)(2,1)S(1)}, bf16[64,2560]{1,0:T(8,128)(2,1)S(1)}, u32[]{:S(2)}, u32[]{:S(2)}) %collective-permute-start.31) | collective-permute-done | bytes 327712 | tf_op jit(solution)/shard_map/ppermute | solution.py:90
  131.9 1.8 %collective-permute-start.36 = (bf16[4,16,1024]{2,1,0:T(8,128)(2,1)S(1)}, bf16[4,16,1024]{2,1,0:T(8,128)(2,1)S(1)}, u32[]{:S(2)}, u32[]{:S(2)}) collective-permute-start(bf16[4,16,1024]{2,1,0:T(8,128)(2,1)S(1)} %get-tuple-element.101), channel_id=1, source_target_pairs={{0,24},{1,25},{2,26},{3,27},{4,28},{5,29},{6,30},{7,31},{8,16},{9,... | collective-permute-start | bytes 393224 | tf_op jit(solution)/shard_map/ppermute | solution.py:90
  133.7 5.5 %collective-permute-done.32 = bf16[64,2560]{1,0:T(8,128)(2,1)S(1)} collective-permute-done((bf16[64,2560]{1,0:T(8,128)(2,1)S(1)}, bf16[64,2560]{1,0:T(8,128)(2,1)S(1)}, u32[]{:S(2)}, u32[]{:S(2)}) %collective-permute-start.32) | collective-permute-done | bytes 327712 | tf_op jit(solution)/shard_map/ppermute | solution.py:90
  141.2 1.6 %collective-permute-start.38 = (bf16[16,2560]{1,0:T(8,128)(2,1)S(1)}, bf16[16,2560]{1,0:T(8,128)(2,1)S(1)}, u32[]{:S(2)}, u32[]{:S(2)}) collective-permute-start(bf16[16,2560]{1,0:T(8,128)(2,1)S(1)} %get-tuple-element.107), channel_id=1, source_target_pairs={{0,16},{1,17},{2,18},{3,19},{4,20},{5,21},{6,22},{7,23},{8,24},{9,... | collective-permute-start | bytes 245768 | tf_op jit(solution)/shard_map/ppermute | solution.py:90
  142.8 2.0 %collective-permute-start.39 = (bf16[16,2560]{1,0:T(8,128)(2,1)S(1)}, bf16[16,2560]{1,0:T(8,128)(2,1)S(1)}, u32[]{:S(2)}, u32[]{:S(2)}) collective-permute-start(bf16[16,2560]{1,0:T(8,128)(2,1)S(1)} %get-tuple-element.108), channel_id=1, source_target_pairs={{0,24},{1,25},{2,26},{3,27},{4,28},{5,29},{6,30},{7,31},{8,16},{9,... | collective-permute-start | bytes 245768 | tf_op jit(solution)/shard_map/ppermute | solution.py:90
  146.2 3.4 %collective-permute-done.38 = bf16[16,2560]{1,0:T(8,128)(2,1)S(1)} collective-permute-done((bf16[16,2560]{1,0:T(8,128)(2,1)S(1)}, bf16[16,2560]{1,0:T(8,128)(2,1)S(1)}, u32[]{:S(2)}, u32[]{:S(2)}) %collective-permute-start.38) | collective-permute-done | bytes 81952 | tf_op jit(solution)/shard_map/ppermute | solution.py:90
  (132 shorter events, 30.4 us)
Async XLA Ops:
  6.9 30.5 %all-to-all-start = ((bf16[64,16,512]{2,1,0:T(8,128)(2,1)}), bf16[64,16,512]{2,1,0:T(8,128)(2,1)S(1)}, u32[]{:S(2)}, u32[]{:S(2)}) async-start(bf16[64,16,512]{2,1,0:T(8,128)(2,1)} %shard_map.136), calls=%async_computation | async-start | bytes 2097152 | tf_op jit(solution)/shard_map/all_to_all | solution.py:447
  48.1 10.6 %collective-permute-start.2 = (bf16[64,2560]{1,0:T(8,128)(2,1)S(1)}, bf16[64,2560]{1,0:T(8,128)(2,1)S(1)}, u32[]{:S(2)}, u32[]{:S(2)}) collective-permute-start(bf16[64,2560]{1,0:T(8,128)(2,1)S(1)} %get-tuple-element.65), channel_id=1, source_target_pairs={{0,4},{1,5},{2,6},{3,7},{4,0},{5,1},{6,2},{7,3},{8,12},{9,13},{10,... | collective-permute-start | bytes 983048 | tf_op jit(solution)/shard_map/ppermute | solution.py:90
  50.1 16.7 %collective-permute-start.3 = (bf16[64,2560]{1,0:T(8,128)(2,1)S(1)}, bf16[64,2560]{1,0:T(8,128)(2,1)S(1)}, u32[]{:S(2)}, u32[]{:S(2)}) collective-permute-start(bf16[64,2560]{1,0:T(8,128)(2,1)S(1)} %get-tuple-element.66), channel_id=1, source_target_pairs={{0,1},{1,0},{2,3},{3,2},{4,5},{5,4},{6,7},{7,6},{8,9},{9,8},{10,11... | collective-permute-start | bytes 983048 | tf_op jit(solution)/shard_map/ppermute | solution.py:90
  51.6 15.2 %collective-permute-start.4 = (bf16[64,2560]{1,0:T(8,128)(2,1)S(1)}, bf16[64,2560]{1,0:T(8,128)(2,1)S(1)}, u32[]{:S(2)}, u32[]{:S(2)}) collective-permute-start(bf16[64,2560]{1,0:T(8,128)(2,1)S(1)} %get-tuple-element.67), channel_id=1, source_target_pairs={{0,5},{1,4},{2,7},{3,6},{4,1},{5,0},{6,3},{7,2},{8,13},{9,12},{10,... | collective-permute-start | bytes 983048 | tf_op jit(solution)/shard_map/ppermute | solution.py:90
  51.6 15.4 %collective-permute-start.5 = (bf16[4,16,1024]{2,1,0:T(8,128)(2,1)S(1)}, bf16[4,16,1024]{2,1,0:T(8,128)(2,1)S(1)}, u32[]{:S(2)}, u32[]{:S(2)}) collective-permute-start(bf16[4,16,1024]{2,1,0:T(8,128)(2,1)S(1)} %get-tuple-element.68), channel_id=1, source_target_pairs={{0,8},{1,9},{2,10},{3,11},{4,12},{5,13},{6,14},{7,15},{8,0},{9,1},... | collective-permute-start | bytes 393224 | tf_op jit(solution)/shard_map/ppermute | solution.py:90
  55.0 12.0 %collective-permute-start.6 = (bf16[4,16,1024]{2,1,0:T(8,128)(2,1)S(1)}, bf16[4,16,1024]{2,1,0:T(8,128)(2,1)S(1)}, u32[]{:S(2)}, u32[]{:S(2)}) collective-permute-start(bf16[4,16,1024]{2,1,0:T(8,128)(2,1)S(1)} %get-tuple-element.69), channel_id=1, source_target_pairs={{0,16},{1,17},{2,18},{3,19},{4,20},{5,21},{6,22},{7,23},{8,24},{9,... | collective-permute-start | bytes 393224 | tf_op jit(solution)/shard_map/ppermute | solution.py:90
  58.6 8.4 %collective-permute-start.7 = (bf16[4,16,1024]{2,1,0:T(8,128)(2,1)S(1)}, bf16[4,16,1024]{2,1,0:T(8,128)(2,1)S(1)}, u32[]{:S(2)}, u32[]{:S(2)}) collective-permute-start(bf16[4,16,1024]{2,1,0:T(8,128)(2,1)S(1)} %get-tuple-element.70), channel_id=1, source_target_pairs={{0,24},{1,25},{2,26},{3,27},{4,28},{5,29},{6,30},{7,31},{8,16},{9,... | collective-permute-start | bytes 393224 | tf_op jit(solution)/shard_map/ppermute | solution.py:90
  67.3 6.6 %collective-permute-start.8 = (bf16[2,16,1024]{2,1,0:T(8,128)(2,1)S(1)}, bf16[2,16,1024]{2,1,0:T(8,128)(2,1)S(1)}, u32[]{:S(2)}, u32[]{:S(2)}) collective-permute-start(bf16[2,16,1024]{2,1,0:T(8,128)(2,1)S(1)} %pad_maximum_fusion.3), channel_id=1, source_target_pairs={{0,4},{1,5},{2,6},{3,7},{4,0},{5,1},{6,2},{7,3},{8,12},{9,13},{10,... | collective-permute-start | bytes 196616 | tf_op jit(solution)/shard_map/ppermute | solution.py:90
  68.6 6.7 %collective-permute-start.9 = (bf16[16,2560]{1,0:T(8,128)(2,1)S(1)}, bf16[16,2560]{1,0:T(8,128)(2,1)S(1)}, u32[]{:S(2)}, u32[]{:S(2)}) collective-permute-start(bf16[16,2560]{1,0:T(8,128)(2,1)S(1)} %get-tuple-element.76), channel_id=1, source_target_pairs={{0,8},{1,9},{2,10},{3,11},{4,12},{5,13},{6,14},{7,15},{8,0},{9,1},... | collective-permute-start | bytes 245768 | tf_op jit(solution)/shard_map/ppermute | solution.py:90
  71.5 8.5 %collective-permute-start.10 = (bf16[16,2560]{1,0:T(8,128)(2,1)S(1)}, bf16[16,2560]{1,0:T(8,128)(2,1)S(1)}, u32[]{:S(2)}, u32[]{:S(2)}) collective-permute-start(bf16[16,2560]{1,0:T(8,128)(2,1)S(1)} %get-tuple-element.77), channel_id=1, source_target_pairs={{0,16},{1,17},{2,18},{3,19},{4,20},{5,21},{6,22},{7,23},{8,24},{9,... | collective-permute-start | bytes 245768 | tf_op jit(solution)/shard_map/ppermute | solution.py:90
  72.9 7.0 %collective-permute-start.11 = (bf16[16,2560]{1,0:T(8,128)(2,1)S(1)}, bf16[16,2560]{1,0:T(8,128)(2,1)S(1)}, u32[]{:S(2)}, u32[]{:S(2)}) collective-permute-start(bf16[16,2560]{1,0:T(8,128)(2,1)S(1)} %get-tuple-element.78), channel_id=1, source_target_pairs={{0,24},{1,25},{2,26},{3,27},{4,28},{5,29},{6,30},{7,31},{8,16},{9,... | collective-permute-start | bytes 245768 | tf_op jit(solution)/shard_map/ppermute | solution.py:90
  73.9 6.1 %collective-permute-start.12 = (bf16[1,16,1024]{2,1,0:T(8,128)(2,1)S(1)}, bf16[1,16,1024]{2,1,0:T(8,128)(2,1)S(1)}, u32[]{:S(2)}, u32[]{:S(2)}) collective-permute-start(bf16[1,16,1024]{2,1,0:T(8,128)(2,1)S(1)} %get-tuple-element.130), channel_id=1, source_target_pairs={{0,1},{1,0},{2,3},{3,2},{4,5},{5,4},{6,7},{7,6},{8,9},{9,8},{10,11... | collective-permute-start | bytes 98312 | tf_op jit(solution)/shard_map/ppermute | solution.py:90
  80.1 9.6 %collective-permute-start.15 = (bf16[16,2816]{1,0:T(8,128)(2,1)S(1)}, bf16[16,2816]{1,0:T(8,128)(2,1)S(1)}, u32[]{:S(2)}, u32[]{:S(2)}) collective-permute-start(bf16[16,2816]{1,0:T(8,128)(2,1)S(1)} %get-tuple-element.86), channel_id=1, source_target_pairs={{0,24},{1,25},{2,26},{3,27},{4,28},{5,29},{6,30},{7,31},{8,16},{9,... | collective-permute-start | bytes 270344 | tf_op jit(solution)/shard_map/ppermute | solution.py:90
  81.9 7.9 %collective-permute-start.14 = (bf16[16,2816]{1,0:T(8,128)(2,1)S(1)}, bf16[16,2816]{1,0:T(8,128)(2,1)S(1)}, u32[]{:S(2)}, u32[]{:S(2)}) collective-permute-start(bf16[16,2816]{1,0:T(8,128)(2,1)S(1)} %get-tuple-element.86), channel_id=1, source_target_pairs={{0,16},{1,17},{2,18},{3,19},{4,20},{5,21},{6,22},{7,23},{8,24},{9,... | collective-permute-start | bytes 270344 | tf_op jit(solution)/shard_map/ppermute | solution.py:90
  83.0 6.8 %collective-permute-start.13 = (bf16[16,2816]{1,0:T(8,128)(2,1)S(1)}, bf16[16,2816]{1,0:T(8,128)(2,1)S(1)}, u32[]{:S(2)}, u32[]{:S(2)}) collective-permute-start(bf16[16,2816]{1,0:T(8,128)(2,1)S(1)} %get-tuple-element.86), channel_id=1, source_target_pairs={{0,8},{1,9},{2,10},{3,11},{4,12},{5,13},{6,14},{7,15},{8,0},{9,1},... | collective-permute-start | bytes 270344 | tf_op jit(solution)/shard_map/ppermute | solution.py:90
  92.6 7.0 %collective-permute-start.25 = (bf16[64,896]{1,0:T(8,128)(2,1)S(1)}, bf16[64,896]{1,0:T(8,128)(2,1)S(1)}, u32[]{:S(2)}, u32[]{:S(2)}) collective-permute-start(bf16[64,896]{1,0:T(8,128)(2,1)S(1)} %pad_maximum_fusion.1), channel_id=1, source_target_pairs={{0,16},{1,17},{2,18},{3,19},{4,20},{5,21},{6,22},{7,23},{8,24},{9,... | collective-permute-start | bytes 344072 | tf_op jit(solution)/shard_map/ppermute | solution.py:90
  93.5 11.2 %collective-permute-start.20 = (bf16[64,2816]{1,0:T(8,128)(2,1)S(1)}, bf16[64,2816]{1,0:T(8,128)(2,1)S(1)}, u32[]{:S(2)}, u32[]{:S(2)}) collective-permute-start(bf16[64,2816]{1,0:T(8,128)(2,1)S(1)} %pad_maximum_fusion.refs_0_), channel_id=1, source_target_pairs={{0,5},{1,4},{2,7},{3,6},{4,1},{5,0},{6,3},{7,2},{8,13},{9,12},{10,... | collective-permute-start | bytes 1081352 | tf_op jit(solution)/shard_map/ppermute | solution.py:90
  95.8 12.6 %collective-permute-start.19 = (bf16[64,2816]{1,0:T(8,128)(2,1)S(1)}, bf16[64,2816]{1,0:T(8,128)(2,1)S(1)}, u32[]{:S(2)}, u32[]{:S(2)}) collective-permute-start(bf16[64,2816]{1,0:T(8,128)(2,1)S(1)} %pad_maximum_fusion.refs_0_), channel_id=1, source_target_pairs={{0,1},{1,0},{2,3},{3,2},{4,5},{5,4},{6,7},{7,6},{8,9},{9,8},{10,11... | collective-permute-start | bytes 1081352 | tf_op jit(solution)/shard_map/ppermute | solution.py:90
  96.3 12.1 %collective-permute-start.18 = (bf16[64,2816]{1,0:T(8,128)(2,1)S(1)}, bf16[64,2816]{1,0:T(8,128)(2,1)S(1)}, u32[]{:S(2)}, u32[]{:S(2)}) collective-permute-start(bf16[64,2816]{1,0:T(8,128)(2,1)S(1)} %pad_maximum_fusion.refs_0_), channel_id=1, source_target_pairs={{0,4},{1,5},{2,6},{3,7},{4,0},{5,1},{6,2},{7,3},{8,12},{9,13},{10,... | collective-permute-start | bytes 1081352 | tf_op jit(solution)/shard_map/ppermute | solution.py:90
  99.6 9.3 %collective-permute-start.26 = (bf16[128,896]{1,0:T(8,128)(2,1)S(1)}, bf16[128,896]{1,0:T(8,128)(2,1)S(1)}, u32[]{:S(2)}, u32[]{:S(2)}) collective-permute-start(bf16[128,896]{1,0:T(8,128)(2,1)S(1)} %constant_dynamic-update-slice_fusion.refs_8_), channel_id=1, source_target_pairs={{0,8},{1,9},{2,10},{3,11},{4,12},{5,13},{6,14},{7,15},{8,0},{9,1},... | collective-permute-start | bytes 688136 | tf_op jit(solution)/shard_map/ppermute | solution.py:90
  101.1 7.9 %collective-permute-start.21 = (bf16[64,2816]{1,0:T(8,128)(2,1)S(1)}, bf16[64,2816]{1,0:T(8,128)(2,1)S(1)}, u32[]{:S(2)}, u32[]{:S(2)}) collective-permute-start(bf16[64,2816]{1,0:T(8,128)(2,1)S(1)} %pad_maximum_fusion.refs_0_), channel_id=1, source_target_pairs={{0,2},{1,3},{2,0},{3,1},{4,6},{5,7},{6,4},{7,5},{8,10},{9,11},{10,... | collective-permute-start | bytes 1081352 | tf_op jit(solution)/shard_map/ppermute | solution.py:90
  104.7 6.2 %collective-permute-start.24 = (bf16[64,2816]{1,0:T(8,128)(2,1)S(1)}, bf16[64,2816]{1,0:T(8,128)(2,1)S(1)}, u32[]{:S(2)}, u32[]{:S(2)}) collective-permute-start(bf16[64,2816]{1,0:T(8,128)(2,1)S(1)} %collective-permute-done.20.refs_3_), channel_id=1, source_target_pairs={{0,2},{1,3},{2,0},{3,1},{4,6},{5,7},{6,4},{7,5},{8,10},{9,11},{10,... | collective-permute-start | bytes 1081352 | tf_op jit(solution)/shard_map/ppermute | solution.py:90
  121.3 10.6 %collective-permute-start.31 = (bf16[64,2560]{1,0:T(8,128)(2,1)S(1)}, bf16[64,2560]{1,0:T(8,128)(2,1)S(1)}, u32[]{:S(2)}, u32[]{:S(2)}) collective-permute-start(bf16[64,2560]{1,0:T(8,128)(2,1)S(1)} %get-tuple-element.96), channel_id=1, source_target_pairs={{0,4},{1,5},{2,6},{3,7},{4,0},{5,1},{6,2},{7,3},{8,12},{9,13},{10,... | collective-permute-start | bytes 983048 | tf_op jit(solution)/shard_map/ppermute | solution.py:90
  122.7 16.5 %collective-permute-start.32 = (bf16[64,2560]{1,0:T(8,128)(2,1)S(1)}, bf16[64,2560]{1,0:T(8,128)(2,1)S(1)}, u32[]{:S(2)}, u32[]{:S(2)}) collective-permute-start(bf16[64,2560]{1,0:T(8,128)(2,1)S(1)} %get-tuple-element.97), channel_id=1, source_target_pairs={{0,1},{1,0},{2,3},{3,2},{4,5},{5,4},{6,7},{7,6},{8,9},{9,8},{10,11... | collective-permute-start | bytes 983048 | tf_op jit(solution)/shard_map/ppermute | solution.py:90
  123.7 15.5 %collective-permute-start.33 = (bf16[64,2560]{1,0:T(8,128)(2,1)S(1)}, bf16[64,2560]{1,0:T(8,128)(2,1)S(1)}, u32[]{:S(2)}, u32[]{:S(2)}) collective-permute-start(bf16[64,2560]{1,0:T(8,128)(2,1)S(1)} %get-tuple-element.98), channel_id=1, source_target_pairs={{0,5},{1,4},{2,7},{3,6},{4,1},{5,0},{6,3},{7,2},{8,13},{9,12},{10,... | collective-permute-start | bytes 983048 | tf_op jit(solution)/shard_map/ppermute | solution.py:90
  124.9 14.5 %collective-permute-start.34 = (bf16[4,16,1024]{2,1,0:T(8,128)(2,1)S(1)}, bf16[4,16,1024]{2,1,0:T(8,128)(2,1)S(1)}, u32[]{:S(2)}, u32[]{:S(2)}) collective-permute-start(bf16[4,16,1024]{2,1,0:T(8,128)(2,1)S(1)} %get-tuple-element.99), channel_id=1, source_target_pairs={{0,8},{1,9},{2,10},{3,11},{4,12},{5,13},{6,14},{7,15},{8,0},{9,1},... | collective-permute-start | bytes 393224 | tf_op jit(solution)/shard_map/ppermute | solution.py:90
  125.7 13.7 %collective-permute-start.35 = (bf16[4,16,1024]{2,1,0:T(8,128)(2,1)S(1)}, bf16[4,16,1024]{2,1,0:T(8,128)(2,1)S(1)}, u32[]{:S(2)}, u32[]{:S(2)}) collective-permute-start(bf16[4,16,1024]{2,1,0:T(8,128)(2,1)S(1)} %get-tuple-element.100), channel_id=1, source_target_pairs={{0,16},{1,17},{2,18},{3,19},{4,20},{5,21},{6,22},{7,23},{8,24},{9,... | collective-permute-start | bytes 393224 | tf_op jit(solution)/shard_map/ppermute | solution.py:90
  131.9 7.5 %collective-permute-start.36 = (bf16[4,16,1024]{2,1,0:T(8,128)(2,1)S(1)}, bf16[4,16,1024]{2,1,0:T(8,128)(2,1)S(1)}, u32[]{:S(2)}, u32[]{:S(2)}) collective-permute-start(bf16[4,16,1024]{2,1,0:T(8,128)(2,1)S(1)} %get-tuple-element.101), channel_id=1, source_target_pairs={{0,24},{1,25},{2,26},{3,27},{4,28},{5,29},{6,30},{7,31},{8,16},{9,... | collective-permute-start | bytes 393224 | tf_op jit(solution)/shard_map/ppermute | solution.py:90
  139.6 5.2 %collective-permute-start.40 = (bf16[2,16,1024]{2,1,0:T(8,128)(2,1)S(1)}, bf16[2,16,1024]{2,1,0:T(8,128)(2,1)S(1)}, u32[]{:S(2)}, u32[]{:S(2)}) collective-permute-start(bf16[2,16,1024]{2,1,0:T(8,128)(2,1)S(1)} %pad_maximum_fusion.4), channel_id=1, source_target_pairs={{0,4},{1,5},{2,6},{3,7},{4,0},{5,1},{6,2},{7,3},{8,12},{9,13},{10,... | collective-permute-start | bytes 196616 | tf_op jit(solution)/shard_map/ppermute | solution.py:90
  140.4 5.8 %collective-permute-start.37 = (bf16[16,2560]{1,0:T(8,128)(2,1)S(1)}, bf16[16,2560]{1,0:T(8,128)(2,1)S(1)}, u32[]{:S(2)}, u32[]{:S(2)}) collective-permute-start(bf16[16,2560]{1,0:T(8,128)(2,1)S(1)} %get-tuple-element.106), channel_id=1, source_target_pairs={{0,8},{1,9},{2,10},{3,11},{4,12},{5,13},{6,14},{7,15},{8,0},{9,1},... | collective-permute-start | bytes 245768 | tf_op jit(solution)/shard_map/ppermute | solution.py:90
  141.2 8.4 %collective-permute-start.38 = (bf16[16,2560]{1,0:T(8,128)(2,1)S(1)}, bf16[16,2560]{1,0:T(8,128)(2,1)S(1)}, u32[]{:S(2)}, u32[]{:S(2)}) collective-permute-start(bf16[16,2560]{1,0:T(8,128)(2,1)S(1)} %get-tuple-element.107), channel_id=1, source_target_pairs={{0,16},{1,17},{2,18},{3,19},{4,20},{5,21},{6,22},{7,23},{8,24},{9,... | collective-permute-start | bytes 245768 | tf_op jit(solution)/shard_map/ppermute | solution.py:90
  142.8 6.8 %collective-permute-start.39 = (bf16[16,2560]{1,0:T(8,128)(2,1)S(1)}, bf16[16,2560]{1,0:T(8,128)(2,1)S(1)}, u32[]{:S(2)}, u32[]{:S(2)}) collective-permute-start(bf16[16,2560]{1,0:T(8,128)(2,1)S(1)} %get-tuple-element.108), channel_id=1, source_target_pairs={{0,24},{1,25},{2,26},{3,27},{4,28},{5,29},{6,30},{7,31},{8,16},{9,... | collective-permute-start | bytes 245768 | tf_op jit(solution)/shard_map/ppermute | solution.py:90
  (24 other events, 434.5 us)
